TPU v7x, 32 devices: a whole 2x2x4 slice. The times are simulated.
32 devices in a mesh: dp: 8 (over z, x), mp: 4 (over y, core).
Axes of the slice: x: 2, y: 2, z: 4, core: 2. Of those that a mesh axis runs over, the one named last changes fastest.
Arguments:
- tokens: bfloat16 [12288, 768], P('dp'), may hold values from -6 to 6
- lengths: int32 [8], P('dp'), may hold values from 1 to 1536, 9216 in all
- horizontal: int32 [12288], P('dp'), may hold values from 0 to 63
- vertical: int32 [12288], P('dp'), may hold values from 0 to 63
- gain_attn: bfloat16 [768], replicated, may hold values from 0.5 to 1.5
- w_qkv: bfloat16 [3, 768, 768], P(None, None, 'mp'), may hold values from -0.21875 to 0.21875
- bias_tables: bfloat16 [96, 12], P(None, 'mp'), may hold values from -4 to 4
- w_output: bfloat16 [768, 768], P('mp'), may hold values from -1.75 to 1.75
- gain_ffn: bfloat16 [768], replicated, may hold values from 0.5 to 1.5
- w_inner: bfloat16 [768, 3072], P(None, 'mp'), may hold values from -0.21875 to 0.21875
- w_outer: bfloat16 [3072, 768], P('mp'), may hold values from -0.109375 to 0.109375
- cotangent: bfloat16 [12288, 768], P('dp'), may hold values from -6 to 6
Outputs:
- mixed: bfloat16 [12288, 768], P(('dp', 'mp'))
- input_grad: float32 [12288, 768], P(('dp', 'mp'))
- grad_qkv: float32 [3, 768, 768], P(None, 'dp', 'mp')
- grad_output: float32 [768, 768], P('mp', 'dp')
- grad_inner: float32 [768, 3072], P('dp', 'mp')
- grad_outer: float32 [3072, 768], P('mp', 'dp')
- grad_gain_attn: float32 [768], replicated
- grad_gain_ffn: float32 [768], replicated
- grad_tables: float32 [96, 12], P(None, 'mp')
Inputs may be any that keep to these rules, and one draw needn't show every extreme that they name: `lengths`: live tokens of each document; the longest document has exactly 1536.
All inputs are finite; a program needn't handle non-finite values. No bound on the sum of `lengths` on one device may be relied on, other than what follows from the above.
Results may differ from a plain program's by a relative error of at most 0.015.
Values may be sent and summed in bfloat16 or wider, within the bound.
A program may use at most 192 MiB of HBM per device.

v0:
```python
import jax
import jax.numpy as jnp
from jax import lax
from jax.sharding import PartitionSpec as P

HEADS = 12
BUCKETS = 32
CODES = 64


epsilon = 1e-06
highest = lax.Precision.HIGHEST


def rms_norm(inputs, gain_vector):
    factor = lax.rsqrt(jnp.mean(inputs * inputs, axis=-1, keepdims=True) + epsilon)
    return inputs * factor * gain_vector


def norm_back(inputs, grad_normed, gain_vector):
    factor = lax.rsqrt(jnp.mean(inputs * inputs, axis=-1, keepdims=True) + epsilon)
    normed_rows = inputs * factor
    scaled = grad_normed * gain_vector
    return factor * (scaled - normed_rows * jnp.mean(scaled * normed_rows, axis=-1, keepdims=True))


def gain_term(inputs, grad_normed):
    factor = lax.rsqrt(jnp.mean(inputs * inputs, axis=-1, keepdims=True) + epsilon)
    return jnp.sum(grad_normed * inputs * factor, axis=0)


def line_ids(row_start, block_rows, row_count, half_count):
    offsets = (
        jnp.arange(row_count, dtype=jnp.int32)[None, :]
        - (row_start + jnp.arange(block_rows, dtype=jnp.int32))[:, None]
    )
    return jnp.clip(offsets, -half_count, half_count - 1) + half_count


def line_bias(table_line, bucket_ids):
    result = jnp.zeros((table_line.shape[1],) + bucket_ids.shape, jnp.float32)
    for bucket in range(table_line.shape[0]):
        result = jnp.where((bucket_ids == bucket)[None], table_line[bucket][:, None, None], result)
    return result


def line_grad_of(grad_logits, bucket_ids, bucket_count):
    grad_f = grad_logits.astype(jnp.float32)
    sums = [
        jnp.sum(jnp.where((bucket_ids == bucket)[None], grad_f, 0.0), axis=(1, 2))
        for bucket in range(bucket_count)
    ]
    return jnp.stack(sums, axis=0)


def plane_blocks(table_plane, code_count):
    bucket_count = table_plane.shape[0] // 2
    half_count = bucket_count // 2
    code_ids = jnp.arange(code_count, dtype=jnp.int32)
    differ = (
        jnp.clip(code_ids[None, :] - code_ids[:, None], -half_count, half_count - 1) + half_count
    )
    bucket_hot = (
        differ[:, :, None] == jnp.arange(bucket_count, dtype=jnp.int32)[None, None, :]
    ).astype(jnp.float32)
    across = jnp.einsum("acb,bh->hac", bucket_hot, table_plane[:bucket_count], precision=highest)
    upward = jnp.einsum("acb,bh->hac", bucket_hot, table_plane[bucket_count:], precision=highest)
    zero_block = jnp.zeros_like(across)
    upper_rows = jnp.concatenate([across, zero_block], axis=2)
    lower_rows = jnp.concatenate([zero_block, upward], axis=2)
    return jnp.concatenate([upper_rows, lower_rows], axis=1)


def local(
    tokens,
    lengths,
    horizontal,
    vertical,
    gain_attn,
    w_qkv,
    bias_tables,
    w_output,
    gain_ffn,
    w_inner,
    w_outer,
    cotangent,
):
    row_count, model_width = tokens.shape
    local_width = w_qkv.shape[2]
    head_here = bias_tables.shape[1]
    head_size = local_width // head_here
    bucket_count = BUCKETS
    half_count = bucket_count // 2
    block_rows = min(512, row_count)
    block_count = row_count // block_rows
    share_rows = row_count // lax.axis_size("mp")
    mp_index = lax.axis_index("mp")
    share_start = mp_index * share_rows
    score_scale = head_size ** (-0.5)
    tokens_f = tokens.astype(jnp.float32)
    gain_a = gain_attn.astype(jnp.float32)
    gain_f = gain_ffn.astype(jnp.float32)
    tables_f = bias_tables.astype(jnp.float32)
    table_line = tables_f[:bucket_count]
    table_plane = tables_f[bucket_count:]
    w_heads = w_qkv.reshape(3, model_width, head_here, head_size)
    w_out_heads = w_output.reshape(head_here, head_size, model_width)
    key_live = jnp.arange(row_count, dtype=jnp.int32) < lengths[0]
    code_ids = jnp.arange(CODES, dtype=jnp.int32)[None, :]
    code_hot = jnp.concatenate(
        [horizontal[:, None] == code_ids, vertical[:, None] == code_ids], axis=1
    ).astype(jnp.bfloat16)
    plane_matrix, plane_back = jax.vjp(
        lambda table_part: plane_blocks(table_part, CODES), table_plane
    )
    spread = jnp.einsum(
        "ic,hcd->hid",
        code_hot,
        plane_matrix.astype(jnp.bfloat16),
        preferred_element_type=jnp.float32,
    ).astype(jnp.bfloat16)
    token_share = lax.dynamic_slice_in_dim(tokens_f, share_start, share_rows, 0)
    normed_a = rms_norm(tokens_f, gain_a).astype(jnp.bfloat16)
    projected = jnp.einsum(
        "id,kdhe->khie", normed_a, w_heads, preferred_element_type=jnp.float32
    ).astype(jnp.bfloat16)
    queries = projected[0]
    key_rows = projected[1]
    values = projected[2]

    def scores_at(row_start):
        query_rows = lax.dynamic_slice_in_dim(queries, row_start, block_rows, 1)
        spread_rows = lax.dynamic_slice_in_dim(spread, row_start, block_rows, 1)
        bucket_ids = line_ids(row_start, block_rows, row_count, half_count)
        logits = (
            jnp.einsum("hie,hje->hij", query_rows, key_rows, preferred_element_type=jnp.float32)
            * score_scale
        )
        planar = jnp.einsum(
            "hic,jc->hij", spread_rows, code_hot, preferred_element_type=jnp.float32
        )
        logits = logits + (line_bias(table_line, bucket_ids) + planar)
        return (jnp.where(key_live[None, None, :], logits, -1e30), query_rows, bucket_ids)

    def attend(row_start):
        logits, query_rows, bucket_ids = scores_at(row_start)
        maximum = jnp.max(logits, axis=-1, keepdims=True)
        weights = jnp.exp(logits - maximum)
        totals = jnp.sum(weights, axis=-1, keepdims=True)
        probs_low = (weights / totals).astype(jnp.bfloat16)
        mixed_rows = jnp.einsum(
            "hij,hje->hie", probs_low, values, preferred_element_type=jnp.float32
        )
        return (mixed_rows.astype(jnp.bfloat16), (maximum + jnp.log(totals))[:, :, 0])

    starts = jnp.arange(block_count, dtype=jnp.int32) * block_rows
    attended, log_totals = lax.map(attend, starts)
    partial_attn = jnp.einsum(
        "nhie,hed->nid", attended, w_out_heads, preferred_element_type=jnp.float32
    ).reshape(row_count, model_width)
    hidden_in = tokens_f + lax.psum(partial_attn, "mp")
    normed_f = rms_norm(hidden_in, gain_f).astype(jnp.bfloat16)
    inner = jnp.dot(normed_f, w_inner, preferred_element_type=jnp.float32)
    activated = jax.nn.gelu(inner).astype(jnp.bfloat16)
    partial_ffn = jnp.dot(activated, w_outer, preferred_element_type=jnp.float32)
    ffn_full = lax.psum(partial_ffn.astype(jnp.bfloat16), "mp").astype(jnp.float32)
    hidden_share = lax.dynamic_slice_in_dim(hidden_in, share_start, share_rows, 0)
    mixed = (hidden_share + lax.dynamic_slice_in_dim(ffn_full, share_start, share_rows, 0)).astype(
        jnp.bfloat16
    )
    grad_act = jnp.einsum("id,fd->if", cotangent, w_outer, preferred_element_type=jnp.float32)
    grad_outer_w = jnp.einsum("if,id->fd", activated, cotangent, preferred_element_type=jnp.float32)
    gelu_value, gelu_back = jax.vjp(jax.nn.gelu, inner)
    grad_inner_low = gelu_back(grad_act)[0].astype(jnp.bfloat16)
    grad_inner_w = jnp.einsum(
        "id,if->df", normed_f, grad_inner_low, preferred_element_type=jnp.float32
    )
    partial_norm = jnp.einsum(
        "if,df->id", grad_inner_low, w_inner, preferred_element_type=jnp.float32
    )
    cotangent_f = cotangent.astype(jnp.float32)
    grad_normed = lax.psum(partial_norm, "mp")
    grad_hidden = cotangent_f + norm_back(hidden_in, grad_normed, gain_f)
    gain_ffn_grad = gain_term(
        lax.dynamic_slice_in_dim(hidden_in, share_start, share_rows, 0),
        lax.dynamic_slice_in_dim(grad_normed, share_start, share_rows, 0),
    )
    grad_hidden_low = grad_hidden.astype(jnp.bfloat16)
    grad_hidden_share = lax.dynamic_slice_in_dim(grad_hidden, share_start, share_rows, 0)
    grad_blocks = grad_hidden_low.reshape(block_count, block_rows, model_width)
    grad_output_w = jnp.einsum(
        "nhie,nid->hed", attended, grad_blocks, preferred_element_type=jnp.float32
    ).reshape(local_width, model_width)
    grad_attended = jnp.einsum(
        "nid,hed->nhie", grad_blocks, w_out_heads, preferred_element_type=jnp.float32
    ).astype(jnp.bfloat16)

    def backward_step(carry, index):
        query_grad, key_grad, value_grad, plane_grad, line_grad = carry
        row_start = index * block_rows
        logits, query_rows, bucket_ids = scores_at(row_start)
        probs_f = jnp.exp(logits - log_totals[index][:, :, None])
        probs_low = probs_f.astype(jnp.bfloat16)
        grad_rows = grad_attended[index]
        grad_probs = jnp.einsum(
            "hie,hje->hij", grad_rows, values, preferred_element_type=jnp.float32
        )
        grad_logits = (
            probs_f * (grad_probs - jnp.sum(probs_f * grad_probs, axis=-1, keepdims=True))
        ).astype(jnp.bfloat16)
        query_part = (
            jnp.einsum("hij,hje->hie", grad_logits, key_rows, preferred_element_type=jnp.float32)
            * score_scale
        )
        query_grad = lax.dynamic_update_slice(
            query_grad, query_part, (jnp.int32(0), row_start, jnp.int32(0))
        )
        key_grad = (
            key_grad
            + jnp.einsum(
                "hij,hie->hje", grad_logits, query_rows, preferred_element_type=jnp.float32
            )
            * score_scale
        )
        value_grad = value_grad + jnp.einsum(
            "hij,hie->hje", probs_low, grad_rows, preferred_element_type=jnp.float32
        )
        line_grad = line_grad + line_grad_of(grad_logits, bucket_ids, bucket_count)
        spread_grad = jnp.einsum(
            "hij,jc->hic", grad_logits, code_hot, preferred_element_type=jnp.float32
        )
        hot_rows = lax.dynamic_slice_in_dim(code_hot, row_start, block_rows, 0).astype(jnp.float32)
        plane_grad = plane_grad + jnp.einsum(
            "ic,hid->hcd", hot_rows, spread_grad, precision=highest
        )
        return ((query_grad, key_grad, value_grad, plane_grad, line_grad), None)

    empty_rows = jnp.zeros((head_here, row_count, head_size), jnp.float32)
    initial = (
        empty_rows,
        empty_rows,
        empty_rows,
        jnp.zeros_like(plane_matrix),
        jnp.zeros_like(table_line),
    )
    carried, unused = lax.scan(backward_step, initial, jnp.arange(block_count, dtype=jnp.int32))
    query_grad, key_grad, value_grad, plane_grad, line_grad = carried
    stacked = jnp.stack([query_grad, key_grad, value_grad]).astype(jnp.bfloat16)
    grad_qkv_w = jnp.einsum(
        "id,khie->kdhe", normed_a, stacked, preferred_element_type=jnp.float32
    ).reshape(3, model_width, local_width)
    partial_norm_a = jnp.einsum(
        "khie,kdhe->id", stacked, w_heads, preferred_element_type=jnp.float32
    )
    plane_table_grad = plane_back(plane_grad)[0]
    local_tables = jnp.concatenate([line_grad, plane_table_grad], axis=0)
    tables_embedded = lax.dynamic_update_slice(
        jnp.zeros((3 * bucket_count, HEADS), jnp.float32),
        local_tables,
        (jnp.int32(0), mp_index * head_here),
    )
    grad_normed_a = lax.psum(partial_norm_a.astype(jnp.bfloat16), "mp").astype(jnp.float32)
    grad_share_a = lax.dynamic_slice_in_dim(grad_normed_a, share_start, share_rows, 0)
    input_grad = grad_hidden_share + norm_back(token_share, grad_share_a, gain_a)
    gain_attn_grad = gain_term(token_share, grad_share_a)
    gain_attn_sum, gain_ffn_sum, tables_sum = lax.psum(
        (gain_attn_grad, gain_ffn_grad, tables_embedded), ("dp", "mp")
    )
    grad_tables = lax.dynamic_slice_in_dim(tables_sum, mp_index * head_here, head_here, 1)
    qkv_part, output_part, inner_part, outer_part = (
        lax.psum_scatter(grad_qkv_w, "dp", scatter_dimension=1, tiled=True),
        lax.psum_scatter(grad_output_w, "dp", scatter_dimension=1, tiled=True),
        lax.psum_scatter(grad_inner_w, "dp", scatter_dimension=0, tiled=True),
        lax.psum_scatter(grad_outer_w, "dp", scatter_dimension=1, tiled=True),
    )
    return (
        mixed,
        input_grad,
        qkv_part,
        output_part,
        inner_part,
        outer_part,
        gain_attn_sum,
        gain_ffn_sum,
        grad_tables,
    )


def solution(mesh):
    return jax.shard_map(
        local,
        mesh=mesh,
        in_specs=(
            P("dp", None),
            P("dp"),
            P("dp"),
            P("dp"),
            P(),
            P(None, None, "mp"),
            P(None, "mp"),
            P("mp", None),
            P(),
            P(None, "mp"),
            P("mp", None),
            P("dp", None),
        ),
        out_specs=(
            P(("dp", "mp"), None),
            P(("dp", "mp"), None),
            P(None, "dp", "mp"),
            P("mp", "dp"),
            P("dp", "mp"),
            P("mp", "dp"),
            P(),
            P(),
            P(None, "mp"),
        ),
        check_vma=False,
    )
```

profile of v0, /device:TPU:0, one launch (start us, length us, event | category | flops | bytes accessed | tf_op | source)
XLA Modules:
  0.0 1303.5 jit_solution(14158338288577273646)
XLA Ops:
  20.9 240.2 %while.32 = (s32[]{:T(128)}, bf16[3,3,512,64]{2,3,1,0:T(8,128)(2,1)}, f32[3,3,512]{2,1,0:T(4,128)S(1)}, s32[3]{0:T(128)S(1)}, bf16[3,1536,64]{1,2,0:T(8,128)(2,1...) while((s32[]{:T(128)}, ...), condition=%wide.region_4.5_spmd.clone, body=%wide.region_1.4_spmd.clone.sunk | while | flops 1334673920 | bytes 137689456 | solution.py:157
  25.3 5.2 fusion.245
  30.4 23.3 %fusion.244 = (pred[512,1536]{1,0:T(8,128)(4,1)S(1)}, pred[512,1536]{1,0:T(8,128)(4,1)S(1)}, pred[512,1536]{1,0:T(8,128)(4,1)S(1)}, pred[512,1536]{1,0:T(8,128)(...) fusion(s32[512]{0:T(512)S(1)} %iota_add_fusion.4), kind=kLoop, calls=%fused_computation.39.clone.1 | loop fusion | flops 27525120 | bytes 25167872 | tf_op jit(solution)/shard_map/while/body/eval_jaxpr/eq | solution.py:43
  53.7 38.1 %fusion.246 = (f32[3,512]{1,0:T(4,128)S(1)}, f32[3,512,1536]{2,1,0:T(8,128)}) fusion(bf16[1536,128]{1,0:T(8,128)(2,1)S(1)} %get-tuple-element.1089, bf16[3,1536,128]{2,1,0:T(8,128)(2,1)} %get-tuple-element.1088, s32[]{:T(128)S(6)} %select_n.594, f32[3]{0:T(128)S(1)} %get-tuple-element.872, pred[512,1536]{1,0:T(8,128)(4,1)S(1)} %get-tuple-element.873, ...), kind=kOutput, calls=%fused_computation.343.clone.1 | convolution fusion | flops 691272192 | bytes 44834692 | tf_op jit(solution)/shard_map/while/body/eval_jaxpr/hic,jc->hij/dot_general | solution.py:139
  91.9 5.2 fusion.247
  105.1 5.2 fusion.245
  110.3 23.3 %fusion.244 = (pred[512,1536]{1,0:T(8,128)(4,1)S(1)}, pred[512,1536]{1,0:T(8,128)(4,1)S(1)}, pred[512,1536]{1,0:T(8,128)(4,1)S(1)}, pred[512,1536]{1,0:T(8,128)(...) fusion(s32[512]{0:T(512)S(1)} %iota_add_fusion.4), kind=kLoop, calls=%fused_computation.39.clone.1 | loop fusion | flops 27525120 | bytes 25167872 | tf_op jit(solution)/shard_map/while/body/eval_jaxpr/eq | solution.py:43
  133.6 38.1 %fusion.246 = (f32[3,512]{1,0:T(4,128)S(1)}, f32[3,512,1536]{2,1,0:T(8,128)}) fusion(bf16[1536,128]{1,0:T(8,128)(2,1)S(1)} %get-tuple-element.1089, bf16[3,1536,128]{2,1,0:T(8,128)(2,1)} %get-tuple-element.1088, s32[]{:T(128)S(6)} %select_n.594, f32[3]{0:T(128)S(1)} %get-tuple-element.872, pred[512,1536]{1,0:T(8,128)(4,1)S(1)} %get-tuple-element.873, ...), kind=kOutput, calls=%fused_computation.343.clone.1 | convolution fusion | flops 691272192 | bytes 44834692 | tf_op jit(solution)/shard_map/while/body/eval_jaxpr/hic,jc->hij/dot_general | solution.py:139
  171.8 5.2 fusion.247
  185.0 5.2 fusion.245
  190.1 23.3 %fusion.244 = (pred[512,1536]{1,0:T(8,128)(4,1)S(1)}, pred[512,1536]{1,0:T(8,128)(4,1)S(1)}, pred[512,1536]{1,0:T(8,128)(4,1)S(1)}, pred[512,1536]{1,0:T(8,128)(...) fusion(s32[512]{0:T(512)S(1)} %iota_add_fusion.4), kind=kLoop, calls=%fused_computation.39.clone.1 | loop fusion | flops 27525120 | bytes 25167872 | tf_op jit(solution)/shard_map/while/body/eval_jaxpr/eq | solution.py:43
  213.5 38.1 %fusion.246 = (f32[3,512]{1,0:T(4,128)S(1)}, f32[3,512,1536]{2,1,0:T(8,128)}) fusion(bf16[1536,128]{1,0:T(8,128)(2,1)S(1)} %get-tuple-element.1089, bf16[3,1536,128]{2,1,0:T(8,128)(2,1)} %get-tuple-element.1088, s32[]{:T(128)S(6)} %select_n.594, f32[3]{0:T(128)S(1)} %get-tuple-element.872, pred[512,1536]{1,0:T(8,128)(4,1)S(1)} %get-tuple-element.873, ...), kind=kOutput, calls=%fused_computation.343.clone.1 | convolution fusion | flops 691272192 | bytes 44834692 | tf_op jit(solution)/shard_map/while/body/eval_jaxpr/hic,jc->hij/dot_general | solution.py:139
  251.6 5.2 fusion.247
  266.4 6.1 fusion.183
  272.5 90.6 %all-reduce.10.cloned.1.call-done = f32[1536,768]{1,0:T(8,128)} async-done(((f32[1536,768]{1,0:T(8,128)}), f32[1536,768]{1,0:T(8,128)}) %all-reduce.10.cloned.1.call-update) | async-done | bytes 4718608 | tf_op jit(solution)/shard_map/psum | solution.py:161
  367.6 6.1 fusion.145
  379.5 7.0 convolution_convert_fusion
  386.5 87.2 %all-reduce.12.cloned.1.call-done = f32[1536,768]{1,0:T(8,128)} async-done(((f32[1536,768]{1,0:T(8,128)}), f32[1536,768]{1,0:T(8,128)}) %all-reduce.12.cloned.1.call-update) | async-done | bytes 4718608 | tf_op jit(solution)/shard_map/psum | solution.py:182
  473.7 4.7 multiply_reduce_fusion.1
  479.6 4.7 fusion.181
  492.0 482.7 %while.33 = (s32[]{:T(128)}, bf16[3,1536,64]{1,2,0:T(8,128)(2,1)}, f32[3,1536,64]{1,2,0:T(8,128)}, f32[3,1536,64]{1,2,0:T(8,128)}, f32[3,128,128]{1,2,0:T(8,128)...) while((s32[]{:T(128)}, bf16[3,1536,64]{1,2,0:T(8,128)(2,1)}, ...), condition=%wide.region_45.46_spmd.clone, body=%wide.region_11.45_spmd.clone.sunk | while | flops 3306259200 | bytes 327133600 | solution.py:246
  512.5 6.0 fusion.264
  518.5 5.1 fusion.265
  523.6 24.6 %fusion.263 = (pred[512,1536]{1,0:T(8,128)(4,1)S(1)}, pred[512,1536]{1,0:T(8,128)(4,1)S(1)}, pred[512,1536]{1,0:T(8,128)(4,1)}, pred[512,1536]{1,0:T(8,128)(4,1)...) fusion(s32[512]{0:T(512)S(1)} %iota_add_fusion.5), kind=kLoop, calls=%fused_computation.184.clone.1 | loop fusion | flops 27525120 | bytes 25167872 | tf_op jit(solution)/shard_map/while/body/eval_jaxpr/eq | solution.py:43
  548.2 39.2 %multiply_reduce_fusion.8 = (f32[3,512]{1,0:T(4,128)S(1)}, f32[3,512,1536]{2,1,0:T(8,128)}) fusion(f32[3,512,1536]{2,1,0:T(8,128)} %fusion.264, f32[3,512]{1,0:T(4,128)S(1)} %dynamic-slice_bitcast_fusion.2, bf16[1536,128]{1,0:T(8,128)(2,1)} %copy-done.25, bf16[3,1536,128]{2,1,0:T(8,128)(2,1)} %get-tuple-element.1147, s32[]{:T(128)S(6)} %select_n.597, ...), kind=kOutput, calls=%fused_computation.149.clone.1 | convolution fusion | flops 695990784 | bytes 54278020 | tf_op jit(solution)/shard_map/while/body/eval_jaxpr/hic,jc->hij/dot_general | solution.py:139
  587.4 36.0 %fusion.266 = (f32[3]{0:T(128)S(1)}, f32[3]{0:T(128)S(1)}, f32[3]{0:T(128)S(1)}, f32[3]{0:T(128)S(1)}, f32[3]{0:T(128)S(1)}, /*index=5*/f32[3]{0:T(128)S(1)}, f3...) fusion(pred[512,1536]{1,0:T(8,128)(4,1)} %get-tuple-element.954, ...), kind=kLoop, calls=%fused_computation.147.clone.1 | loop fusion | flops 94371792 | bytes 37755096 | tf_op jit(solution)/shard_map/while/body/eval_jaxpr/reduce_sum | solution.py:50
  629.1 20.3 %fusion.272 = (f32[3]{0:T(128)S(1)}, f32[3]{0:T(128)S(1)}, f32[3]{0:T(128)S(1)}, f32[3]{0:T(128)S(1)}, f32[3]{0:T(128)S(1)}, /*index=5*/f32[3]{0:T(128)S(1)}, f3...) fusion(bf16[3,512,1536]{2,1,0:T(8,128)(2,1)S(1)} %get-tuple-ele, ...), kind=kLoop, calls=%fused_computation.146.clone.1 | loop fusion | flops 68419536 | bytes 15728808 | tf_op jit(solution)/shard_map/while/body/eval_jaxpr/reduce_sum | solution.py:50
  652.6 4.7 fusion.267
  665.0 6.0 fusion.264
  671.0 5.1 fusion.265
  676.1 24.6 %fusion.263 = (pred[512,1536]{1,0:T(8,128)(4,1)S(1)}, pred[512,1536]{1,0:T(8,128)(4,1)S(1)}, pred[512,1536]{1,0:T(8,128)(4,1)}, pred[512,1536]{1,0:T(8,128)(4,1)...) fusion(s32[512]{0:T(512)S(1)} %iota_add_fusion.5), kind=kLoop, calls=%fused_computation.184.clone.1 | loop fusion | flops 27525120 | bytes 25167872 | tf_op jit(solution)/shard_map/while/body/eval_jaxpr/eq | solution.py:43
  700.7 39.1 %multiply_reduce_fusion.8 = (f32[3,512]{1,0:T(4,128)S(1)}, f32[3,512,1536]{2,1,0:T(8,128)}) fusion(f32[3,512,1536]{2,1,0:T(8,128)} %fusion.264, f32[3,512]{1,0:T(4,128)S(1)} %dynamic-slice_bitcast_fusion.2, bf16[1536,128]{1,0:T(8,128)(2,1)} %copy-done.25, bf16[3,1536,128]{2,1,0:T(8,128)(2,1)} %get-tuple-element.1147, s32[]{:T(128)S(6)} %select_n.597, ...), kind=kOutput, calls=%fused_computation.149.clone.1 | convolution fusion | flops 695990784 | bytes 54278020 | tf_op jit(solution)/shard_map/while/body/eval_jaxpr/hic,jc->hij/dot_general | solution.py:139
  739.8 36.0 %fusion.266 = (f32[3]{0:T(128)S(1)}, f32[3]{0:T(128)S(1)}, f32[3]{0:T(128)S(1)}, f32[3]{0:T(128)S(1)}, f32[3]{0:T(128)S(1)}, /*index=5*/f32[3]{0:T(128)S(1)}, f3...) fusion(pred[512,1536]{1,0:T(8,128)(4,1)} %get-tuple-element.954, ...), kind=kLoop, calls=%fused_computation.147.clone.1 | loop fusion | flops 94371792 | bytes 37755096 | tf_op jit(solution)/shard_map/while/body/eval_jaxpr/reduce_sum | solution.py:50
  781.6 20.3 %fusion.272 = (f32[3]{0:T(128)S(1)}, f32[3]{0:T(128)S(1)}, f32[3]{0:T(128)S(1)}, f32[3]{0:T(128)S(1)}, f32[3]{0:T(128)S(1)}, /*index=5*/f32[3]{0:T(128)S(1)}, f3...) fusion(bf16[3,512,1536]{2,1,0:T(8,128)(2,1)S(1)} %get-tuple-ele, ...), kind=kLoop, calls=%fused_computation.146.clone.1 | loop fusion | flops 68419536 | bytes 15728808 | tf_op jit(solution)/shard_map/while/body/eval_jaxpr/reduce_sum | solution.py:50
  817.5 6.0 fusion.264
  823.5 5.1 fusion.265
  828.6 24.6 %fusion.263 = (pred[512,1536]{1,0:T(8,128)(4,1)S(1)}, pred[512,1536]{1,0:T(8,128)(4,1)S(1)}, pred[512,1536]{1,0:T(8,128)(4,1)}, pred[512,1536]{1,0:T(8,128)(4,1)...) fusion(s32[512]{0:T(512)S(1)} %iota_add_fusion.5), kind=kLoop, calls=%fused_computation.184.clone.1 | loop fusion | flops 27525120 | bytes 25167872 | tf_op jit(solution)/shard_map/while/body/eval_jaxpr/eq | solution.py:43
  853.1 39.1 %multiply_reduce_fusion.8 = (f32[3,512]{1,0:T(4,128)S(1)}, f32[3,512,1536]{2,1,0:T(8,128)}) fusion(f32[3,512,1536]{2,1,0:T(8,128)} %fusion.264, f32[3,512]{1,0:T(4,128)S(1)} %dynamic-slice_bitcast_fusion.2, bf16[1536,128]{1,0:T(8,128)(2,1)} %copy-done.25, bf16[3,1536,128]{2,1,0:T(8,128)(2,1)} %get-tuple-element.1147, s32[]{:T(128)S(6)} %select_n.597, ...), kind=kOutput, calls=%fused_computation.149.clone.1 | convolution fusion | flops 695990784 | bytes 54278020 | tf_op jit(solution)/shard_map/while/body/eval_jaxpr/hic,jc->hij/dot_general | solution.py:139
  892.3 36.0 %fusion.266 = (f32[3]{0:T(128)S(1)}, f32[3]{0:T(128)S(1)}, f32[3]{0:T(128)S(1)}, f32[3]{0:T(128)S(1)}, f32[3]{0:T(128)S(1)}, /*index=5*/f32[3]{0:T(128)S(1)}, f3...) fusion(pred[512,1536]{1,0:T(8,128)(4,1)} %get-tuple-element.954, ...), kind=kLoop, calls=%fused_computation.147.clone.1 | loop fusion | flops 94371792 | bytes 37755096 | tf_op jit(solution)/shard_map/while/body/eval_jaxpr/reduce_sum | solution.py:50
  934.1 20.3 %fusion.272 = (f32[3]{0:T(128)S(1)}, f32[3]{0:T(128)S(1)}, f32[3]{0:T(128)S(1)}, f32[3]{0:T(128)S(1)}, f32[3]{0:T(128)S(1)}, /*index=5*/f32[3]{0:T(128)S(1)}, f3...) fusion(bf16[3,512,1536]{2,1,0:T(8,128)(2,1)S(1)} %get-tuple-ele, ...), kind=kLoop, calls=%fused_computation.146.clone.1 | loop fusion | flops 68419536 | bytes 15728808 | tf_op jit(solution)/shard_map/while/body/eval_jaxpr/reduce_sum | solution.py:50
  978.2 4.8 bitcast_convert_fusion
  984.8 6.0 fusion.178
  990.9 7.0 fusion.180
  1014.0 63.6 %all-reduce.14.cloned.1.call-done = (bf16[1536,768]{1,0:T(8,128)(2,1)}, bf16[1536,768]{1,0:T(8,128)(2,1)}) async-done(((bf16[1536,768]{1,0:T(8,128)(2,1)}, bf16[1536,768]{1,0:T(8,128)(2,1)}), (bf16[1536,768]{1,0:T(8,128)(2,1)}, bf16[1536,768]{1,0:T(8,128)(2,1)})) %all-reduce.14.cloned.1.call-update) | async-done | bytes 4718608 | tf_op jit(solution)/shard_map/psum | solution.py:166
  1082.4 40.3 %all-reduce.4 = (f32[768]{0:T(1024)}, f32[768]{0:T(1024)}, f32[96,12]{0,1:T(8,128)S(1)}) all-reduce(f32[768]{0:T(1024)S(1)} %get-tuple-element.352, f32[768]{0:T(1024)S(1)} %get-tuple-element.550, f32[96,12]{0,1:T(8,128)S(1)} %dynamic_update_slice.14), channel_id=1, replica_groups=mesh['dp'=8,'mp'=4] {'dp','mp'}, use_global_device_ids=true, to_apply=%region_53.54 | all-reduce | flops 2688 | bytes 21504 | tf_op jit(solution)/shard_map/psum | solution.py:266
  1126.4 25.2 %reduce-scatter.9.cloned.1.call-done = f32[96,768]{1,0:T(8,128)} async-done(((f32[768,768]{1,0:T(8,128)}), f32[96,768]{1,0:T(8,128)}) %reduce-scatter.9.cloned.1.call-update) | async-done | bytes 294928 | tf_op jit(solution)/shard_map/reduce_scatter | solution.py:273
  1151.6 72.4 %reduce-scatter.11.cloned.1.call-done = f32[768,96]{0,1:T(8,128)} async-done(((f32[768,768]{0,1:T(8,128)}), f32[768,96]{0,1:T(8,128)}) %reduce-scatter.11.cloned.1.call-update) | async-done | bytes 294928 | tf_op jit(solution)/shard_map/reduce_scatter | solution.py:274
  1224.0 72.5 %reduce-scatter.7.cloned.1.call-done = f32[3,96,192]{2,1,0:T(8,128)} async-done(((f32[3,768,192]{2,1,0:T(8,128)}), f32[3,96,192]{2,1,0:T(8,128)}) %reduce-scatter.7.cloned.1.call-update) | async-done | bytes 221200 | tf_op jit(solution)/shard_map/reduce_scatter | solution.py:271
  (422 shorter events, 136.2 us)
Async XLA Ops:
  7.2 360.0 %copy-start = (bf16[768,768]{1,0:T(8,128)(2,1)S(1)}, bf16[768,768]{1,0:T(8,128)(2,1)}, u32[]{:S(2)}) copy-start(bf16[768,768]{1,0:T(8,128)(2,1)} %param.25) | copy-start | bytes 3538948
  7.2 356.0 %all-reduce.10.cloned.1.call-start = ((), (), s32[]{:S(2)}) async-start(), calls=%async_computation.4 | async-start | bytes 9437184 | tf_op jit(solution)/shard_map/psum | solution.py:161
  10.0 10.5 copy-start.38
  13.0 7.5 copy-start.42
  91.9 6.4 copy-start.5
  171.7 6.4 copy-start.5
  251.6 6.4 copy-start.5
  266.3 207.4 %all-reduce.12.cloned.1.call-start = ((), (), s32[]{:S(2)}) async-start(), calls=%async_computation.5 | async-start | bytes 9437184 | tf_op jit(solution)/shard_map/psum | solution.py:182
  266.4 212.1 %copy-start.36 = (f32[768]{0:T(1024)}, f32[768]{0:T(1024)S(1)}, u32[]{:S(2)}) copy-start(f32[768]{0:T(1024)S(1)} %convert_element_type.91) | copy-start | bytes 9220
  367.1 6.6 copy-start.17
  367.1 111.3 %copy-start.34 = (f32[1536]{0:T(1024)}, f32[1536]{0:T(1024)S(1)}, u32[]{:S(2)}) copy-start(f32[1536]{0:T(1024)S(1)} %add_rsqrt_fusion) | copy-start | bytes 18436
  379.4 633.0 %reduce-scatter.13.cloned.1.call-start = ((), (), s32[]{:S(2)}) async-start(), calls=%async_computation.9 | async-start | bytes 884736
  479.6 6.1 copy-start.33
  487.7 589.9 %all-reduce.14.cloned.1.call-start = ((), (), s32[]{:S(2)}) async-start(), calls=%async_computation.10 | async-start | bytes 9437184 | tf_op jit(solution)/shard_map/psum | solution.py:166
  508.5 10.0 copy-start.22
  508.5 10.0 copy-start.25
  508.5 10.0 copy-start.28
  587.3 36.1 %copy-start.4 = (f32[3,512,1536]{2,1,0:T(8,128)S(1)}, f32[3,512,1536]{2,1,0:T(8,128)}, u32[]{:S(2)}) copy-start(f32[3,512,1536]{2,1,0:T(8,128)} %get-tuple-element.1018) | copy-start | bytes 28311556 | tf_op jit(solution)/shard_map/while
  587.4 36.1 %copy-start.18 = (f32[3,1536,64]{1,2,0:T(8,128)S(1)}, f32[3,1536,64]{1,2,0:T(8,128)}, u32[]{:S(2)}) copy-start(f32[3,1536,64]{1,2,0:T(8,128)} %get-tuple-element.1119) | copy-start | bytes 3538948 | tf_op jit(solution)/shard_map/while
  626.3 23.1 %copy-start.19 = (f32[3,1536,64]{1,2,0:T(8,128)}, f32[3,1536,64]{1,2,0:T(8,128)S(1)}, u32[]{:S(2)}) copy-start(f32[3,1536,64]{1,2,0:T(8,128)S(1)} %fusion.269) | copy-start | bytes 3538948 | tf_op jit(solution)/shard_map/while
  649.4 7.8 copy-start.26
  652.5 6.4 copy-start.20
  652.5 6.4 copy-start.29
  661.0 10.0 copy-start.22
  661.0 10.0 copy-start.25
  661.0 10.0 copy-start.28
  739.8 36.1 %copy-start.4 = (f32[3,512,1536]{2,1,0:T(8,128)S(1)}, f32[3,512,1536]{2,1,0:T(8,128)}, u32[]{:S(2)}) copy-start(f32[3,512,1536]{2,1,0:T(8,128)} %get-tuple-element.1018) | copy-start | bytes 28311556 | tf_op jit(solution)/shard_map/while
  739.8 36.1 %copy-start.18 = (f32[3,1536,64]{1,2,0:T(8,128)S(1)}, f32[3,1536,64]{1,2,0:T(8,128)}, u32[]{:S(2)}) copy-start(f32[3,1536,64]{1,2,0:T(8,128)} %get-tuple-element.1119) | copy-start | bytes 3538948 | tf_op jit(solution)/shard_map/while
  778.7 23.1 %copy-start.19 = (f32[3,1536,64]{1,2,0:T(8,128)}, f32[3,1536,64]{1,2,0:T(8,128)S(1)}, u32[]{:S(2)}) copy-start(f32[3,1536,64]{1,2,0:T(8,128)S(1)} %fusion.269) | copy-start | bytes 3538948 | tf_op jit(solution)/shard_map/while
  801.9 7.8 copy-start.26
  805.0 6.4 copy-start.20
  805.0 6.4 copy-start.29
  813.5 10.0 copy-start.22
  813.5 10.0 copy-start.25
  813.5 10.0 copy-start.28
  892.3 36.1 %copy-start.4 = (f32[3,512,1536]{2,1,0:T(8,128)S(1)}, f32[3,512,1536]{2,1,0:T(8,128)}, u32[]{:S(2)}) copy-start(f32[3,512,1536]{2,1,0:T(8,128)} %get-tuple-element.1018) | copy-start | bytes 28311556 | tf_op jit(solution)/shard_map/while
  892.3 36.1 %copy-start.18 = (f32[3,1536,64]{1,2,0:T(8,128)S(1)}, f32[3,1536,64]{1,2,0:T(8,128)}, u32[]{:S(2)}) copy-start(f32[3,1536,64]{1,2,0:T(8,128)} %get-tuple-element.1119) | copy-start | bytes 3538948 | tf_op jit(solution)/shard_map/while
  931.2 23.1 %copy-start.19 = (f32[3,1536,64]{1,2,0:T(8,128)}, f32[3,1536,64]{1,2,0:T(8,128)S(1)}, u32[]{:S(2)}) copy-start(f32[3,1536,64]{1,2,0:T(8,128)S(1)} %fusion.269) | copy-start | bytes 3538948 | tf_op jit(solution)/shard_map/while
  954.3 7.8 copy-start.26
  957.5 6.4 copy-start.20
  957.5 6.4 copy-start.29
  983.1 168.5 %reduce-scatter.9.cloned.1.call-start = ((), (), s32[]{:S(2)}) async-start(), calls=%async_computation.7 | async-start | bytes 2654208 | tf_op jit(solution)/shard_map/reduce_scatter | solution.py:273
  990.8 7.2 copy-start.27
  990.8 7.2 copy-start.39
  990.8 7.2 copy-start.43
  990.9 233.1 %reduce-scatter.11.cloned.1.call-start = ((), (), s32[]{:S(2)}) async-start(), calls=%async_computation.8 | async-start | bytes 2654208 | tf_op jit(solution)/shard_map/reduce_scatter | solution.py:274
  998.0 298.5 %reduce-scatter.7.cloned.1.call-start = ((), (), s32[]{:S(2)}) async-start(), calls=%async_computation.6 | async-start | bytes 2654208 | tf_op jit(solution)/shard_map/reduce_scatter | solution.py:271
  1077.6 218.9 %copy-start.1 = (bf16[768,768]{1,0:T(8,128)(2,1)S(1)}, bf16[768,768]{1,0:T(8,128)(2,1)}, u32[]{:S(2)}) copy-start(bf16[768,768]{1,0:T(8,128)(2,1)} %param.25) | copy-start | bytes 3538948
  (57 other events, 207.9 us)
Sparse Core Ops, SparseCore 0:
  266.4 96.7 all-reduce.9
  379.5 94.1 all-reduce.11
  487.8 62.6 reduce-scatter.12
  983.2 94.3 all-reduce.13
  1081.9 69.6 reduce-scatter.8
  1155.9 68.0 reduce-scatter.10
  1228.4 67.9 reduce-scatter.6
where the time goes:
time: 1310 us; the launch traced here: 1300 us
  waiting for transfers between devices  412 us (31%)
  matrix products  384 us (29%)
  other arithmetic  369 us (28%)
  local copies, waits for them, and re-layouts  43.3 us (3%)
  loops' own time  40.7 us (3%)
  blocking collectives  40.3 us (3%)
  between operations  14.7 us (1%)
    dot_general x6, matrix products, scores_at(): jnp.einsum('hic,jc->hij', spread_rows, code_hot, preferred_element_type=j...  232 us
    reduce_sum x6, other arithmetic, line_grad_of(): jnp.sum(jnp.where((bucket_ids == bucket)[None], grad_f, 0.0), axis=(1, 2))  169 us
    eq x6, other arithmetic, line_bias(): bucket_ids == bucket  144 us
    psum x1, waiting for transfers between devices, local(): hidden_in = tokens_f + lax.psum(partial_attn, 'mp')  90.6 us
    psum x1, waiting for transfers between devices, local(): grad_normed = lax.psum(partial_norm, 'mp')  87.2 us
    reduce_scatter x1, waiting for transfers between devices, local(): lax.psum_scatter(grad_qkv_w, 'dp', scatter_dimension=1, tiled=True)  72.5 us
    reduce_scatter x1, waiting for transfers between devices, local(): lax.psum_scatter(grad_outer_w, 'dp', scatter_dimension=1, tiled=True)  72.4 us
    psum x1, waiting for transfers between devices, local(): lax.psum(partial_ffn.astype(jnp.bfloat16), 'mp').astype(jnp.float32)  63.6 us
  transfers between devices with their start and end apart: 7, of which 6 were waited for; matrix products, arithmetic and copies ran while one was open for 38% of the time, Pallas kernels for 0%

commit v1 on v0

v1 whole, which is shorter than its diff:
```python
import functools
import jax
import jax.numpy as jnp
import numpy as np
from jax import lax
from jax.experimental import pallas as pl
from jax.experimental.pallas import tpu as pltpu
from jax.sharding import PartitionSpec as P

BUCKETS = 32
CODES = 64
HALF = BUCKETS // 2
EPSILON = 1e-06
DEAD = -1e9
CHUNK = 512
BLOCK = 128
BAND = 3 * BLOCK
WIDE = 6 * BLOCK
FAR = 64
MASK = 76
LSE = 80
MIB = 2**20

f32 = jnp.float32
bf16 = jnp.bfloat16


def expansion():
    offsets = np.arange(WIDE) - 2 * BLOCK
    line = np.clip(offsets, -HALF, HALF - 1) + HALF
    line[5 * BLOCK :] = 0
    wrapped = np.arange(BLOCK)
    wrapped = np.where(wrapped < CODES, wrapped, wrapped - BLOCK)
    plane = np.clip(wrapped, -HALF, HALF - 1) + HALF
    buckets = np.concatenate([line, BUCKETS + plane, 2 * BUCKETS + plane])
    return (np.arange(3 * BUCKETS)[:, None] == buckets[None, :]).astype(np.float32)


def collapse():
    buckets = np.argmax(expansion(), axis=0)
    buckets[5 * BLOCK + 1 : WIDE] = 0
    buckets = np.concatenate([buckets, np.zeros(BLOCK, int), np.full(BLOCK, BUCKETS - 1)])
    return (buckets[:, None] == np.arange(3 * BUCKETS)[None, :]).astype(np.float32)


def roll_rows(value, right):
    rows, width = value.shape
    index = lax.broadcasted_iota(jnp.int32, value.shape, 0)
    step = 1
    while step < rows:
        shift = step if right else width - step
        value = jnp.where((index // step) % 2 == 1, pltpu.roll(value, shift, 1), value)
        step *= 2
    return value


def dot(a, b):
    return jnp.dot(a, b, preferred_element_type=f32)


def dot_nt(a, b):
    return lax.dot_general(a, b, (((1,), (1,)), ((), ())), preferred_element_type=f32)


def split3(value):
    high = value.astype(bf16).astype(f32)
    rest = value - high
    middle = rest.astype(bf16).astype(f32)
    return high, middle, rest - middle


def prep_kernel(
    length_ref, tokens_ref, gain_ref, w_ref, codes_ref, tables_ref, expand_ref,
    normed_ref, q_ref, k_ref, kt_ref, v_ref, band_ref, band_t_ref,
    plane_ref, proj_ref,
):
    heads = q_ref.shape[0]
    step = pl.program_id(0)
    width = w_ref.shape[2]
    expanded = dot(tables_ref[...], expand_ref[...])

    @pl.when(step == 0)
    def _():
        rows = lax.broadcasted_iota(jnp.int32, (BLOCK, BLOCK), 0)
        lanes = lax.broadcasted_iota(jnp.int32, (BLOCK, BLOCK), 1)
        for h in range(heads):
            line = jnp.broadcast_to(expanded[h : h + 1, :WIDE], (BLOCK, WIDE))
            band = roll_rows(line, True)
            band_ref[h] = band
            band_t_ref[h] = band.T
            across = roll_rows(jnp.broadcast_to(expanded[h : h + 1, WIDE : WIDE + BLOCK], (BLOCK, BLOCK)), True)
            upward = roll_rows(jnp.broadcast_to(expanded[h : h + 1, WIDE + BLOCK :], (BLOCK, BLOCK)), True)
            plane = jnp.where(
                (rows < CODES) & (lanes < CODES), across, jnp.where((rows >= CODES) & (lanes >= CODES), upward, 0.0)
            )
            plane_ref[h] = plane.astype(bf16)
        proj_ref[...] = jnp.zeros_like(proj_ref)

    x = tokens_ref[...].astype(f32)
    factor = lax.rsqrt(jnp.mean(x * x, axis=-1, keepdims=True) + EPSILON)
    normed = (x * factor * gain_ref[...].astype(f32)).astype(bf16)
    normed_ref[...] = normed

    codes = codes_ref[...]
    codes_lines = lax.broadcasted_iota(jnp.int32, (BLOCK, CHUNK), 0)
    hot_t = jnp.where(
        codes_lines == jnp.broadcast_to(codes[0:1], (BLOCK, CHUNK)),
        1.0,
        jnp.where(codes_lines - CODES == jnp.broadcast_to(codes[1:2], (BLOCK, CHUNK)), 1.0, 0.0),
    )
    hot_f = hot_t.T
    hot = hot_f.astype(bf16)

    lanes = lax.broadcasted_iota(jnp.int32, (CHUNK, BLOCK), 1)
    rows = lax.broadcasted_iota(jnp.int32, (CHUNK, BLOCK), 0) + step * CHUNK
    block = rows // BLOCK
    blocks = pl.num_programs(0) * (CHUNK // BLOCK)
    start = jnp.clip(block - 1, 0, blocks - 3)
    far = (lanes >= FAR) & (lanes < MASK)
    far_left = far & (lanes - FAR < start)
    far_right = far & (lanes - FAR > start + 2)
    key_side = jnp.where(
        (far & (lanes - FAR == block))
        | ((lanes == MASK) & (rows >= length_ref[0]))
        | ((lanes >= LSE) & (lanes < LSE + 3)),
        1.0,
        0.0,
    )
    low = lanes < FAR

    def part(h):
        if h % 2 == 0:
            return proj_ref[:, h // 2 * BLOCK : h // 2 * BLOCK + BLOCK]
        return pltpu.roll(proj_ref[:, h // 2 * BLOCK : h // 2 * BLOCK + BLOCK], BLOCK - 64, 1)

    proj_ref[:, :width] = dot(normed, w_ref[0])
    for h in range(heads):
        left = expanded[h : h + 1, 0:1]
        right = expanded[h : h + 1, WIDE - BLOCK - 1 : WIDE - BLOCK]
        query_side = jnp.where(far_left, left, jnp.where(far_right, right, jnp.where(lanes == MASK, DEAD, 0.0)))
        q_ref[h, :, :BLOCK] = dot(hot, plane_ref[h]).astype(bf16)
        q_ref[h, :, BLOCK:] = jnp.where(low, part(h).astype(bf16).astype(f32) * 0.125, query_side).astype(bf16)
    proj_ref[:, :width] = dot(normed, w_ref[1])
    for h in range(heads):
        second = jnp.where(low, part(h), key_side)
        k_ref[h, :, :BLOCK] = hot
        k_ref[h, :, BLOCK:] = second.astype(bf16)
        kt_ref[h, :BLOCK, :] = hot_t.astype(bf16)
        kt_ref[h, BLOCK:, :] = second.T.astype(bf16)
    proj_ref[:, :width] = dot(normed, w_ref[2])
    for h in range(heads):
        v_ref[h] = jnp.where(low, part(h), 1.0).astype(bf16)


def prep(tokens, lengths, codes, gain, w_qkv, bias_tables):
    rows, model = tokens.shape
    heads = bias_tables.shape[1]
    tables = jnp.pad(bias_tables.T, ((0, 8 - heads), (0, 0)))
    expand = jnp.asarray(expansion(), bf16)
    full = pl.BlockSpec(memory_space=pltpu.VMEM)
    return pl.pallas_call(
        prep_kernel,
        grid=(rows // CHUNK,),
        in_specs=[
            pl.BlockSpec(memory_space=pltpu.SMEM),
            pl.BlockSpec((CHUNK, model), lambda i: (i, 0)),
            full,
            full,
            pl.BlockSpec((2, CHUNK), lambda i: (0, i)),
            full,
            full,
        ],
        out_specs=[
            pl.BlockSpec((CHUNK, model), lambda i: (i, 0)),
            pl.BlockSpec((heads, CHUNK, 256), lambda i: (0, i, 0)),
            pl.BlockSpec((heads, CHUNK, 256), lambda i: (0, i, 0)),
            pl.BlockSpec((heads, 256, CHUNK), lambda i: (0, 0, i)),
            pl.BlockSpec((heads, CHUNK, BLOCK), lambda i: (0, i, 0)),
            pl.BlockSpec((heads, BLOCK, WIDE), lambda i: (0, 0, 0)),
            pl.BlockSpec((heads, WIDE, BLOCK), lambda i: (0, 0, 0)),
        ],
        out_shape=[
            jax.ShapeDtypeStruct((rows, model), bf16),
            jax.ShapeDtypeStruct((heads, rows, 256), bf16),
            jax.ShapeDtypeStruct((heads, rows, 256), bf16),
            jax.ShapeDtypeStruct((heads, 256, rows), bf16),
            jax.ShapeDtypeStruct((heads, rows, BLOCK), bf16),
            jax.ShapeDtypeStruct((heads, BLOCK, WIDE), f32),
            jax.ShapeDtypeStruct((heads, WIDE, BLOCK), f32),
        ],
        scratch_shapes=[pltpu.VMEM((heads, BLOCK, BLOCK), bf16), pltpu.VMEM((CHUNK, 256), f32)],
        compiler_params=pltpu.CompilerParams(vmem_limit_bytes=40 * MIB),
        name="prep",
    )(lengths, tokens, gain.reshape(1, model), w_qkv, codes, tables, expand)


def attend_kernel(q_ref, kt_ref, v_ref, band_ref, w_ref, att_ref, qt_ref, partial_ref, s_ref):
    heads, _, keys = kt_ref.shape
    step = pl.program_id(0)
    blocks = keys // BLOCK
    low = lax.broadcasted_iota(jnp.int32, (CHUNK, BLOCK), 1) < FAR
    lanes = lax.broadcasted_iota(jnp.int32, (CHUNK, BLOCK), 1)
    results = []
    for h in range(heads):
        s_ref[...] = dot(q_ref[h], kt_ref[h])
        for p in range(CHUNK // BLOCK):
            block = step * (CHUNK // BLOCK) + p
            start = jnp.clip(block - 1, 0, blocks - 3)
            at = pl.ds(pl.multiple_of(start * BLOCK, BLOCK), BAND)
            of = pl.ds(pl.multiple_of((start - block + 2) * BLOCK, BLOCK), BAND)
            s_ref[p * BLOCK : (p + 1) * BLOCK, at] += band_ref[h, :, of]
        s = s_ref[...]
        top = jnp.max(s, axis=1, keepdims=True)
        weights = jnp.exp(s - top).astype(bf16)
        mixed = dot(weights, v_ref[h])
        sums = pltpu.roll(mixed, 64, 1)
        results.append(jnp.where(low, mixed / sums, 0.0))
        total = -(top + jnp.log(mixed[:, 64:65]))
        high, middle, rest = split3(total)
        second = q_ref[h, :, BLOCK:].astype(f32)
        second = jnp.where(
            lanes == LSE, high, jnp.where(lanes == LSE + 1, middle, jnp.where(lanes == LSE + 2, rest, second))
        )
        qt_ref[h, :BLOCK, :] = q_ref[h, :, :BLOCK].astype(f32).T.astype(bf16)
        qt_ref[h, BLOCK:, :] = second.T.astype(bf16)
    pairs = []
    for h in range(0, heads, 2):
        pair = results[h]
        if h + 1 < heads:
            pair = jnp.where(low, pair, pltpu.roll(results[h + 1], 64, 1))
        pairs.append(pair.astype(bf16))
    att = jnp.concatenate(pairs, axis=1)
    width = heads * 64
    att_ref[...] = att[:, :width]
    partial_ref[...] = dot(att[:, :width], w_ref[...]).astype(bf16)


def attend(q, kt, v, band, w_output):
    heads, rows, _ = q.shape
    width, model = w_output.shape
    full = pl.BlockSpec(memory_space=pltpu.VMEM)
    return pl.pallas_call(
        attend_kernel,
        grid=(rows // CHUNK,),
        in_specs=[pl.BlockSpec((heads, CHUNK, 256), lambda i: (0, i, 0)), full, full, full, full],
        out_specs=[
            pl.BlockSpec((CHUNK, width), lambda i: (i, 0)),
            pl.BlockSpec((heads, 256, CHUNK), lambda i: (0, 0, i)),
            pl.BlockSpec((CHUNK, model), lambda i: (i, 0)),
        ],
        out_shape=[
            jax.ShapeDtypeStruct((rows, width), bf16),
            jax.ShapeDtypeStruct((heads, 256, rows), bf16),
            jax.ShapeDtypeStruct((rows, model), bf16),
        ],
        scratch_shapes=[pltpu.VMEM((CHUNK, rows), f32)],
        compiler_params=pltpu.CompilerParams(vmem_limit_bytes=56 * MIB),
        name="attend",
    )(q, kt, v, band, w_output)


def back_kernel(
    ghl_ref, w_ref, att_ref, q_ref, qt_ref, k_ref, kt_ref, v_ref, band_t_ref,
    grad_ref, sums_ref,
    da_ref, dat_ref, s_ref, g_ref, pt_ref, gt_ref, dqt_ref, dk_ref, dv_ref, bands_ref, pad_ref,
):
    heads, rows, _ = k_ref.shape
    blocks = rows // BLOCK
    chunks = rows // CHUNK
    width = heads * 64
    lanes = lax.broadcasted_iota(jnp.int32, (CHUNK, BLOCK), 1)
    low = lanes < FAR
    pad_ref[...] = jnp.zeros_like(pad_ref)

    def prologue(c, carry):
        at = pl.ds(pl.multiple_of(c * CHUNK, CHUNK), CHUNK)
        pad_ref[:, :width] = dot_nt(ghl_ref[at, :], w_ref[...]).astype(bf16).astype(f32)
        pad_ref[:, 256 : 256 + width] = att_ref[at, :].astype(f32)
        for h in range(heads):
            base = h // 2 * BLOCK
            grad = pad_ref[:, base : base + BLOCK]
            out = pad_ref[:, 256 + base : 256 + base + BLOCK]
            if h % 2 == 1:
                grad = pltpu.roll(grad, 64, 1)
                out = pltpu.roll(out, 64, 1)
            total = -jnp.sum(jnp.where(low, grad * out, 0.0), axis=1, keepdims=True)
            high, middle, rest = split3(total)
            grad = jnp.where(
                low,
                grad,
                jnp.where(
                    lanes == FAR, high, jnp.where(lanes == FAR + 1, middle, jnp.where(lanes == FAR + 2, rest, 0.0))
                ),
            )
            da_ref[h, at, :] = grad.astype(bf16)
            dat_ref[h, :, at] = grad.T.astype(bf16)
        return carry

    lax.fori_loop(0, chunks, prologue, 0)
    dk_ref[...] = jnp.zeros_like(dk_ref)
    dv_ref[...] = jnp.zeros_like(dv_ref)
    bands_ref[...] = jnp.zeros_like(bands_ref)

    def main(i, carry):
        h = i // chunks
        c = i % chunks
        at = pl.ds(pl.multiple_of(c * CHUNK, CHUNK), CHUNK)
        s_ref[...] = dot(k_ref[h], qt_ref[h, :, at])
        for p in range(CHUNK // BLOCK):
            block = c * (CHUNK // BLOCK) + p
            start = jnp.clip(block - 1, 0, blocks - 3)
            keys = pl.ds(pl.multiple_of(start * BLOCK, BLOCK), BAND)
            of = pl.ds(pl.multiple_of((start - block + 2) * BLOCK, BLOCK), BAND)
            s_ref[keys, p * BLOCK : (p + 1) * BLOCK] += band_t_ref[h, of, :]
        probs = jnp.exp(s_ref[...])
        pt_ref[...] = probs.astype(bf16)
        gt_ref[...] = (probs * dot(v_ref[h], dat_ref[h, :, at])).astype(bf16)
        dv_ref[h] += dot(pt_ref[...], da_ref[h, at, :])
        dk_ref[h] += dot(gt_ref[...], q_ref[h, at, BLOCK:])
        dqt_ref[h, :, at] = dot(kt_ref[h], gt_ref[...])
        for p in range(CHUNK // BLOCK):
            block = c * (CHUNK // BLOCK) + p
            start = jnp.clip(block - 1, 0, blocks - 3)
            keys = pl.ds(pl.multiple_of(start * BLOCK, BLOCK), BAND)
            of = pl.ds(pl.multiple_of((start - block + 2) * BLOCK, BLOCK), BAND)
            bands_ref[h, of, :] += gt_ref[keys, p * BLOCK : (p + 1) * BLOCK].astype(f32)
        return carry

    lax.fori_loop(0, heads * chunks, main, 0)

    def pack(k, parts):
        merged = []
        for h in range(0, heads, 2):
            pair = parts[h]
            pair_low = lax.broadcasted_iota(jnp.int32, pair.shape, 1) < 64
            if h + 1 < heads:
                pair = jnp.where(pair_low, pair, pltpu.roll(parts[h + 1], 64, 1))
            merged.append(pair.astype(bf16))
        grad_ref[k] = jnp.concatenate(merged, axis=1)[:, :width]

    pack(0, [dqt_ref[h, BLOCK:, :].T * 0.125 for h in range(heads)])
    pack(1, [dk_ref[h] for h in range(heads)])
    pack(2, [dv_ref[h] for h in range(heads)])

    sums_ref[...] = jnp.zeros_like(sums_ref)
    lines16 = lax.broadcasted_iota(jnp.int32, (16, rows), 0)
    block = lax.broadcasted_iota(jnp.int32, (16, rows), 1) // BLOCK
    start = jnp.clip(block - 1, 0, blocks - 3)
    real = lines16 < blocks
    plane_rows = lax.broadcasted_iota(jnp.int32, (BLOCK, BLOCK), 0)
    plane_lanes = lax.broadcasted_iota(jnp.int32, (BLOCK, BLOCK), 1)

    def fold(value):
        total = value[:, :BLOCK]
        for b in range(1, value.shape[1] // BLOCK):
            total = total + value[:, b * BLOCK : (b + 1) * BLOCK]
        return jnp.sum(total, axis=0, keepdims=True)

    for h in range(heads):
        band = roll_rows(bands_ref[h].T, False)
        sums_ref[h : h + 1, :WIDE] = jnp.sum(band, axis=0, keepdims=True)
        spread = dqt_ref[h, :BLOCK, :]
        high = spread.astype(bf16)
        rest = (spread - high.astype(f32)).astype(bf16)
        hot = k_ref[h, :, :BLOCK]
        plane = (dot(high, hot) + dot(rest, hot)).T
        plane = jnp.where((plane_rows < CODES) == (plane_lanes < CODES), plane, 0.0)
        plane = roll_rows(plane, False)
        sums_ref[h : h + 1, WIDE : WIDE + BLOCK] = jnp.sum(plane[:CODES], axis=0, keepdims=True)
        sums_ref[h : h + 1, WIDE + BLOCK : WIDE + 2 * BLOCK] = jnp.sum(plane[CODES:], axis=0, keepdims=True)
        far = dqt_ref[h, BLOCK + FAR : BLOCK + FAR + 16, :]
        sums_ref[h : h + 1, WIDE + 2 * BLOCK : WIDE + 3 * BLOCK] = fold(jnp.where(real & (lines16 < start), far, 0.0))
        sums_ref[h : h + 1, WIDE + 3 * BLOCK :] = fold(jnp.where(real & (lines16 > start + 2), far, 0.0))


def attend_back(ghl, w_output, att, q, qt, k, kt, v, band_t):
    heads, rows, _ = q.shape
    full = pl.BlockSpec(memory_space=pltpu.VMEM)
    return pl.pallas_call(
        back_kernel,
        in_specs=[full] * 9,
        out_specs=[full] * 2,
        out_shape=[
            jax.ShapeDtypeStruct((3, rows, heads * 64), bf16),
            jax.ShapeDtypeStruct((8, WIDE + 4 * BLOCK), f32),
        ],
        scratch_shapes=[
            pltpu.VMEM((heads, rows, BLOCK), bf16),
            pltpu.VMEM((heads, BLOCK, rows), bf16),
            pltpu.VMEM((rows, CHUNK), f32),
            pltpu.VMEM((rows, CHUNK), f32),
            pltpu.VMEM((rows, CHUNK), bf16),
            pltpu.VMEM((rows, CHUNK), bf16),
            pltpu.VMEM((heads, 256, rows), f32),
            pltpu.VMEM((heads, rows, BLOCK), f32),
            pltpu.VMEM((heads, rows, BLOCK), f32),
            pltpu.VMEM((heads, WIDE, BLOCK), f32),
            pltpu.VMEM((CHUNK, 512), f32),
        ],
        compiler_params=pltpu.CompilerParams(vmem_limit_bytes=60 * MIB),
        name="attend_back",
    )(ghl, w_output, att, q, qt, k, kt, v, band_t)


def factor_of(rows):
    return lax.rsqrt(jnp.mean(rows * rows, axis=-1, keepdims=True) + EPSILON)


def norm_back(inputs, grad_normed, gain):
    factor = factor_of(inputs)
    hat = inputs * factor
    scaled = grad_normed * gain
    back = factor * (scaled - hat * jnp.mean(scaled * hat, axis=-1, keepdims=True))
    return back, jnp.sum(grad_normed * hat, axis=0)


def local(
    tokens, lengths, horizontal, vertical, gain_attn, w_qkv, bias_tables, w_output, gain_ffn, w_inner, w_outer, cotangent
):
    rows, model = tokens.shape
    heads = bias_tables.shape[1]
    width = w_qkv.shape[2]
    share = rows // lax.axis_size("mp")
    mp = lax.axis_index("mp")
    gain_a = gain_attn.astype(f32)
    gain_f = gain_ffn.astype(f32)
    codes = jnp.stack([horizontal, vertical])
    normed_a, q, k, kt, v, band, band_t = prep(tokens, lengths, codes, gain_attn, w_qkv, bias_tables)
    att, qt, partial = attend(q, kt, v, band, w_output)

    def mine(x):
        return lax.dynamic_slice_in_dim(x, mp * share, share, 0)

    def scatter(x):
        return lax.psum_scatter(x, "mp", scatter_dimension=0, tiled=True).astype(f32)

    def gather(x):
        return lax.all_gather(x, "mp", axis=0, tiled=True)

    tokens_share = mine(tokens).astype(f32)
    hidden = tokens_share + scatter(partial)
    normed_f = gather((hidden * factor_of(hidden) * gain_f).astype(bf16))
    inner = dot(normed_f, w_inner)
    gelu, gelu_back = jax.vjp(jax.nn.gelu, inner)
    activated = gelu.astype(bf16)
    partial_ffn = dot(activated, w_outer).astype(bf16)
    grad_act = dot_nt(cotangent, w_outer)
    grad_inner_low = gelu_back(grad_act)[0].astype(bf16)
    partial_norm = dot_nt(grad_inner_low, w_inner).astype(bf16)
    grad_outer = lax.dot_general(activated, cotangent, (((0,), (0,)), ((), ())), preferred_element_type=f32)
    grad_inner = lax.dot_general(normed_f, grad_inner_low, (((0,), (0,)), ((), ())), preferred_element_type=f32)
    mixed = (hidden + scatter(partial_ffn)).astype(bf16)
    back_f, gain_f_grad = norm_back(hidden, scatter(partial_norm), gain_f)
    grad_hidden = mine(cotangent).astype(f32) + back_f
    ghl = gather(grad_hidden.astype(bf16))
    grad_output = lax.dot_general(att, ghl, (((0,), (0,)), ((), ())), preferred_element_type=f32)
    grads, sums = attend_back(ghl, w_output, att, q, qt, k, kt, v, band_t)
    grad_qkv = lax.dot_general(normed_a, grads, (((0,), (1,)), ((), ())), preferred_element_type=f32)
    grad_qkv = jnp.transpose(grad_qkv, (1, 0, 2))
    partial_a = (dot_nt(grads[0], w_qkv[0]) + dot_nt(grads[1], w_qkv[1]) + dot_nt(grads[2], w_qkv[2])).astype(bf16)
    back_a, gain_a_grad = norm_back(tokens_share, scatter(partial_a), gain_a)
    input_grad = grad_hidden + back_a
    tables = lax.dot_general(
        jnp.asarray(collapse(), f32), sums[:heads], (((0,), (1,)), ((), ())), precision=lax.Precision.HIGHEST
    )
    gains = lax.psum(jnp.stack([gain_a_grad, gain_f_grad]), ("dp", "mp"))
    tables = lax.psum(tables, "dp")

    def spread(x, axis):
        return lax.psum_scatter(x, "dp", scatter_dimension=axis, tiled=True)

    return (
        mixed,
        input_grad,
        spread(grad_qkv, 1),
        spread(grad_output, 1),
        spread(grad_inner, 0),
        spread(grad_outer, 1),
        gains[0],
        gains[1],
        tables,
    )


def solution(mesh):
    return jax.shard_map(
        local,
        mesh=mesh,
        in_specs=(
            P("dp", None), P("dp"), P("dp"), P("dp"), P(), P(None, None, "mp"), P(None, "mp"), P("mp", None), P(),
            P(None, "mp"), P("mp", None), P("dp", None),
        ),
        out_specs=(
            P(("dp", "mp"), None), P(("dp", "mp"), None), P(None, "dp", "mp"), P("mp", "dp"), P("dp", "mp"),
            P("mp", "dp"), P(), P(), P(None, "mp"),
        ),
        check_vma=False,
    )
```

time: 1310 us -> 558 us (0.43)
  other arithmetic: 369 us -> 13.3 us
  matrix products: 384 us -> 49.1 us
  waiting for transfers between devices: 412 us -> 304 us
  Pallas kernels: 0 us -> 67.5 us
  loops' own time: 40.7 us -> 0 us
  blocking collectives: 40.3 us -> 61.4 us
    dot_general x49 -> x10, matrix products: 380 us -> 41 us  [the longest x2 15.9 us: dot(): return jnp.dot(a, b, preferred_element_type=f32)]
    psum x3 -> x0, waiting for transfers between devices: 241 us -> none  [the longest x1 90.6 us: local(): hidden_in = tokens_f + lax.psum(partial_attn, 'mp')]
    reduce_sum x16 -> x3, other arithmetic: 203 us -> 4.89 us  [the longest x2 3.55 us: norm_back(): return (back, jnp.sum(grad_normed * hat, axis=0))]
    eq x7 -> x0, other arithmetic: 145 us -> none  [the longest x6 144 us: line_bias(): bucket_ids == bucket]
    pallas_call x0 -> x3, Pallas kernels: none -> 67.5 us  [the longest x1 37.8 us: attend_back(): pl.pallas_call(back_kernel, in_specs=[full] * 9, out_specs=[full] * 2, ou...]
    reduce_scatter x3 -> x6, waiting for transfers between devices: 170 us -> 236 us  [the longest x2 135 us: spread(): return lax.psum_scatter(x, 'dp', scatter_dimension=axis, tiled=True)]
    all_gather x0 -> x2, waiting for transfers between devices: none -> 42 us  [gather(): return lax.all_gather(x, 'mp', axis=0, tiled=True)]
    another operation x2 -> x0, loops' own time: 40.7 us -> none  [the longest x1 34 us: local(): lax.scan(backward_step, initial, jnp.arange(block_count, dtype=jnp.int32))]
  transfers between devices with their start and end apart: 7 -> 10, of which waited for: 6 -> 8; matrix products, arithmetic and copies ran while one was open for 38% -> 10% of each run, Pallas kernels for 0% -> 7%
where the time goes in v1:
time: 558 us; the launch traced here: 550 us
  waiting for transfers between devices  304 us (54%)
  Pallas kernels  67.5 us (12%)
  blocking collectives  61.4 us (11%)
  matrix products  49.1 us (9%)
  local copies, waits for them, and re-layouts  38.5 us (7%)
  between operations  15.5 us (3%)
  other arithmetic  13.3 us (2%)
    reduce_scatter x2, waiting for transfers between devices, spread(): return lax.psum_scatter(x, 'dp', scatter_dimension=axis, tiled=True)  135 us
    reduce_scatter x4, waiting for transfers between devices, scatter(): lax.psum_scatter(x, 'mp', scatter_dimension=0, tiled=True).astype(f32)  101 us
    all_gather x2, waiting for transfers between devices, gather(): return lax.all_gather(x, 'mp', axis=0, tiled=True)  42 us
    psum x1, blocking collectives, local(): gains = lax.psum(jnp.stack([gain_a_grad, gain_f_grad]), ('dp', 'mp'))  39.5 us
    pallas_call x1, Pallas kernels, attend_back(): pl.pallas_call(back_kernel, in_specs=[full] * 9, out_specs=[full] * 2, ou...  37.8 us
    unnamed x56, local copies, waits for them, and re-layouts  30.9 us
    unnamed x12, waiting for transfers between devices  25.3 us
    psum x1, blocking collectives, local(): tables = lax.psum(tables, 'dp')  21.9 us
  transfers between devices with their start and end apart: 10, of which 8 were waited for; matrix products, arithmetic and copies ran while one was open for 10% of the time, Pallas kernels for 7%

profile of v1, /device:TPU:0, one launch (start us, length us, event | category | flops | bytes accessed | tf_op | source)
XLA Modules:
  0.0 550.1 jit_solution(6943750644518861500)
XLA Ops:
  10.1 1.5 copy.26.w_ref
  12.3 0.9 copy-done.8
  13.2 11.7 %prep.1 = (bf16[1536,768]{1,0:T(8,128)(2,1)S(1)}, bf16[3,1536,256]{2,1,0:T(8,128)(2,1)S(1)}, bf16[3,1536,256]{2,1,0:T(8,128)(2,1)S(1)}, bf16[3,256,1536]{2,1,0:T...) custom-call(s32[1]{0:T(128)S(6)} %copy.34.length_ref, ...), custom_call_target="tpu_custom_call" | custom-call | tf_op jit(solution)/shard_map/prep/pallas_call | solution.py:161
  25.0 1.4 copy-done.2
  26.4 1.4 copy-done.3
  27.8 1.0 copy-done.4
  28.8 1.4 copy-done.5
  30.2 1.0 copy-done.6
  31.2 1.0 copy-done.7
  32.2 1.4 copy-done.9
  33.7 18.0 %attend.1 = (bf16[1536,192]{1,0:T(8,128)(2,1)}, bf16[3,256,1536]{2,1,0:T(8,128)(2,1)}, bf16[1536,768]{1,0:T(8,128)(2,1)}) custom-call(bf16[3,1536,256]{2,1,0:T(8,128)(2,1)} %copy-done.2, bf16[3,256,1536]{2,1,0:T(8,128)(2,1)} %copy-done.3, bf16[3,1536,128]{2,1,0:T(8,128)(2,1)} %copy-done.4, f32[3,128,768]{2,1,0:T(8,128)} %copy-done.6, bf16[192,768]{1,0:T(8,128)(2,1)} %w_ref.4), custom_call_target="tpu_custom_call" | custom-call | tf_op jit(solution)/shard_map/attend/pallas_call | solution.py:242
  52.3 35.2 %reduce-scatter.13.cloned.1.call-done = bf16[384,768]{1,0:T(8,128)(2,1)} async-done(((bf16[1536,768]{1,0:T(8,128)(2,1)}), bf16[384,768]{1,0:T(8,128)(2,1)}) %reduce-scatter.13.cloned.1.call-update) | async-done | bytes 589840 | tf_op jit(solution)/shard_map/reduce_scatter | solution.py:435
  87.6 1.3 multiply_reduce_fusion
  88.9 2.1 multiply_convert_fusion.1
  91.3 6.1 %fusion.41 = f32[1536,768]{1,0:T(8,128)} fusion(bf16[1536,768]{1,0:T(8,128)(2,1)} %param.25, bf16[768,768]{1,0:T(8,128)(2,1)} %param.24), kind=kOutput, calls=%fused_computation.66 | convolution fusion | flops 1811939328 | bytes 8257536 | tf_op jit(solution)/shard_map/dot_general | solution.py:62
  97.4 17.9 %all-gather.3.cloned.1.call-done = bf16[1536,768]{1,0:T(8,128)(2,1)} async-done(((bf16[384,768]{1,0:T(8,128)(2,1)}), bf16[1536,768]{1,0:T(8,128)(2,1)}) %all-gather.3.cloned.1.call-update) | async-done | bytes 2359312 | tf_op jit(solution)/shard_map/all_gather | solution.py:438
  115.3 9.2 %fusion.6 = (bf16[1536,768]{1,0:T(8,128)(2,1)S(1)}, f32[1536,768]{1,0:T(8,128)}) fusion(f32[1536,768]{1,0:T(8,128)} %fusion.41, bf16[1536,768]{1,0:T(8,128)(2,1)} %all-gather.3.cloned.1.call-done, bf16[768,768]{1,0:T(8,128)(2,1)S(1)} %copy-done), kind=kOutput, calls=%fused_computation.8 | convolution fusion | flops 1835532288 | bytes 15335424 | tf_op jit(solution)/shard_map/dot_general | solution.py:58
  124.5 1.4 copy-done.18
  125.9 3.5 convolution_convert_fusion
  129.5 33.2 %reduce-scatter.17.cloned.1.call-done = bf16[384,768]{1,0:T(8,128)(2,1)} async-done(((bf16[1536,768]{1,0:T(8,128)(2,1)}), bf16[384,768]{1,0:T(8,128)(2,1)}) %reduce-scatter.17.cloned.1.call-update) | async-done | bytes 589840 | tf_op jit(solution)/shard_map/reduce_scatter | solution.py:435
  162.7 1.8 fusion.18
  164.4 2.5 fusion.39
  167.0 24.2 %all-gather.5.cloned.1.call-done.ghl_ref = bf16[1536,768]{1,0:T(8,128)(2,1)} async-done(((bf16[384,768]{1,0:T(8,128)(2,1)}), bf16[1536,768]{1,0:T(8,128)(2,1)}) %all-gather.5.cloned.1.call-update) | async-done | bytes 2359312 | tf_op jit(solution)/shard_map/all_gather | solution.py:438
  191.2 3.8 convolution_bitcast_fusion
  195.3 37.8 %attend_back.1 = (bf16[3,1536,192]{2,1,0:T(8,128)(2,1)}, f32[8,1280]{1,0:T(8,128)}) custom-call(bf16[1536,768]{1,0:T(8,128)(2,1)} %all-gather.5.cloned.1.call-done.ghl_ref, bf16[192,768]{1,0:T(8,128)(2,1)} %w_ref.4, bf16[1536,192]{1,0:T(8,128)(2,1)} %get-tuple-element.26.att_ref, bf16[3,1536,256]{2,1,0:T(8,128)(2,1)} %copy-done.2, ...), custom_call_target="tpu_custom_call" | custom-call | tf_op jit(solution)/shard_map/attend_back/pallas_call | solution.py:379
  233.1 4.2 copy.27
  237.3 4.2 fusion.43
  241.5 4.2 copy.29
  245.7 4.8 reshape.50
  250.6 0.8 fusion.24
  252.2 2.2 add_convert_fusion
  254.7 0.9 copy-done.24
  255.6 6.7 %convolution_convert_fusion.1 = bf16[1536,768]{1,0:T(8,128)(2,1)} fusion(bf16[768,768]{1,0:T(8,128)(2,1)S(1)} %copy-done.24, f32[1536,768]{1,0:T(8,128)} %get-tuple-element.61), kind=kOutput, calls=%fused_computation.12 | convolution fusion | flops 1823735808 | bytes 8257536 | tf_op jit(solution)/shard_map/dot_general | solution.py:58
  262.4 1.6 copy-done.17
  264.0 5.1 fusion.42
  269.2 1.6 copy-done.20
  270.8 6.2 %fusion.40 = f32[768,768]{0,1:T(8,128)} fusion(bf16[1536,768]{1,0:T(8,128)(2,1)S(1)} %copy-done.20, f32[1536,768]{1,0:T(8,128)} %get-tuple-element.61), kind=kOutput, calls=%fused_computation.65 | convolution fusion | flops 1822556160 | bytes 9437184 | tf_op jit(solution)/shard_map/dot_general | solution.py:450
  278.5 21.9 %psum.15 = f32[96,3]{0,1:T(4,128)} all-reduce(f32[96,3]{0,1:T(4,128)S(1)} %fusion.37), channel_id=1, replica_groups=mesh['dp'=8,'mp'=4] {'dp'}, use_global_device_ids=true, to_apply=%region_15.16 | all-reduce | flops 288 | bytes 2304 | tf_op jit(solution)/shard_map/psum | solution.py:467
  300.5 1.6 copy.32
  302.1 25.1 %reduce-scatter.25.cloned.1.call-done = f32[96,576]{1,0:T(8,128)} async-done(((f32[768,576]{1,0:T(8,128)}), f32[96,576]{1,0:T(8,128)}) %reduce-scatter.25.cloned.1.call-update) | async-done | bytes 221200
  327.3 1.1 reshape.51
  328.4 0.8 copy.28
  329.2 32.7 %reduce-scatter.19.cloned.1.call-done = bf16[384,768]{1,0:T(8,128)(2,1)} async-done(((bf16[1536,768]{1,0:T(8,128)(2,1)}), bf16[384,768]{1,0:T(8,128)(2,1)}) %reduce-scatter.19.cloned.1.call-update) | async-done | bytes 589840 | tf_op jit(solution)/shard_map/reduce_scatter | solution.py:435
  361.8 1.8 fusion.20
  363.6 39.5 %psum.14 = f32[2,768]{1,0:T(2,128)S(1)} all-reduce(f32[2,768]{1,0:T(2,128)S(1)} %pad_maximum_fusion), channel_id=1, replica_groups=mesh['dp'=8,'mp'=4] {'dp','mp'}, use_global_device_ids=true, to_apply=%region_14.15 | all-reduce | flops 1536 | bytes 12288 | tf_op jit(solution)/shard_map/psum | solution.py:466
  403.7 3.8 fusion.14
  407.5 63.3 %reduce-scatter.21.cloned.1.call-done = f32[96,768]{1,0:T(8,128)} async-done(((f32[768,768]{1,0:T(8,128)}), f32[96,768]{1,0:T(8,128)}) %reduce-scatter.21.cloned.1.call-update) | async-done | bytes 294928 | tf_op jit(solution)/shard_map/reduce_scatter | solution.py:470
  470.8 72.0 %reduce-scatter.23.cloned.1.call-done = f32[768,96]{0,1:T(8,128)} async-done(((f32[768,768]{0,1:T(8,128)}), f32[768,96]{0,1:T(8,128)}) %reduce-scatter.23.cloned.1.call-update) | async-done | bytes 294928 | tf_op jit(solution)/shard_map/reduce_scatter | solution.py:470
  (77 shorter events, 7.6 us)
Async XLA Ops:
  7.2 108.1 %copy-start = (bf16[768,768]{1,0:T(8,128)(2,1)S(1)}, bf16[768,768]{1,0:T(8,128)(2,1)}, u32[]{:S(2)}) copy-start(bf16[768,768]{1,0:T(8,128)(2,1)} %param.23) | copy-start | bytes 3538948
  7.2 80.4 %reduce-scatter.13.cloned.1.call-start = ((), (), s32[]{:S(2)}) async-start(), calls=%async_computation.8 | async-start | bytes 2949120 | tf_op jit(solution)/shard_map/reduce_scatter | solution.py:435
  12.3 0.9 copy-start.8
  25.0 1.4 copy-start.2
  26.4 1.4 copy-start.3
  27.8 1.0 copy-start.4
  28.8 1.4 copy-start.5
  30.2 1.0 copy-start.6
  31.2 1.0 copy-start.7
  32.2 1.4 copy-start.9
  51.6 0.7 copy-start.23
  51.6 35.9 %copy-start.13 = (bf16[1536,768]{1,0:T(8,128)(2,1)S(1)}, bf16[1536,768]{1,0:T(8,128)(2,1)}, u32[]{:S(2)}) copy-start(bf16[1536,768]{1,0:T(8,128)(2,1)} %tokens_ref.1) | copy-start | bytes 7077892
  51.7 63.6 %all-gather.3.cloned.1.call-start = ((), (), s32[]{:S(2)}) async-start(), calls=%async_computation.9 | async-start | bytes 2949120 | tf_op jit(solution)/shard_map/all_gather | solution.py:438
  91.1 71.6 %reduce-scatter.17.cloned.1.call-start = ((), (), s32[]{:S(2)}) async-start(), calls=%async_computation.11 | async-start | bytes 2949120 | tf_op jit(solution)/shard_map/reduce_scatter | solution.py:435
  124.5 1.4 copy-start.18
  129.4 33.3 %copy-start.11 = (bf16[384,768]{1,0:T(8,128)(2,1)S(1)}, bf16[384,768]{1,0:T(8,128)(2,1)}, u32[]{:S(2)}) copy-start(bf16[384,768]{1,0:T(8,128)(2,1)} %reduce-scatter.13.cloned.1.call-done) | copy-start | bytes 1769476
  129.4 61.8 %all-gather.5.cloned.1.call-start = ((), (), s32[]{:S(2)}) async-start(), calls=%async_computation.12 | async-start | bytes 2949120 | tf_op jit(solution)/shard_map/all_gather | solution.py:438
  167.0 133.5 %reduce-scatter.27.cloned.1.call-start = ((), (), s32[]{:S(2)}) async-start(), calls=%async_computation.17 | async-start | bytes 884736
  195.0 132.2 %reduce-scatter.25.cloned.1.call-start = ((), (), s32[]{:S(2)}) async-start(), calls=%async_computation.16 | async-start | bytes 2211840
  233.1 4.2 copy-start.10
  245.7 4.9 copy-start.14
  245.7 4.9 copy-start.16
  250.6 111.3 %reduce-scatter.19.cloned.1.call-start = ((), (), s32[]{:S(2)}) async-start(), calls=%async_computation.13 | async-start | bytes 2949120 | tf_op jit(solution)/shard_map/reduce_scatter | solution.py:435
  254.3 1.3 copy-start.24
  254.4 149.4 %reduce-scatter.15.cloned.1.call-start = ((), (), s32[]{:S(2)}) async-start(), calls=%async_computation.10 | async-start | bytes 2949120 | tf_op jit(solution)/shard_map/reduce_scatter | solution.py:435
  262.3 1.7 copy-start.17
  262.3 208.5 %reduce-scatter.21.cloned.1.call-start = ((), (), s32[]{:S(2)}) async-start(), calls=%async_computation.14 | async-start | bytes 2654208 | tf_op jit(solution)/shard_map/reduce_scatter | solution.py:470
  269.1 1.7 copy-start.20
  269.1 273.7 %reduce-scatter.23.cloned.1.call-start = ((), (), s32[]{:S(2)}) async-start(), calls=%async_computation.15 | async-start | bytes 2654208 | tf_op jit(solution)/shard_map/reduce_scatter | solution.py:470
  277.0 0.7 copy-start.22
  277.0 1.1 copy-start.19
  277.0 1.1 copy-start.21
  277.0 126.7 %copy-start.12 = (bf16[384,768]{1,0:T(8,128)(2,1)S(1)}, bf16[384,768]{1,0:T(8,128)(2,1)}, u32[]{:S(2)}) copy-start(bf16[384,768]{1,0:T(8,128)(2,1)} %reduce-scatter.13.cloned.1.call-done) | copy-start | bytes 1769476
  277.0 126.7 %copy-start.15 = (bf16[384,768]{1,0:T(8,128)(2,1)S(1)}, bf16[384,768]{1,0:T(8,128)(2,1)}, u32[]{:S(2)}) copy-start(bf16[384,768]{1,0:T(8,128)(2,1)} %reduce-scatter.17.cloned.1.call-done) | copy-start | bytes 1769476
  403.7 139.1 %copy-start.1 = (bf16[768,768]{1,0:T(8,128)(2,1)S(1)}, bf16[768,768]{1,0:T(8,128)(2,1)}, u32[]{:S(2)}) copy-start(bf16[768,768]{1,0:T(8,128)(2,1)} %param.23) | copy-start | bytes 3538948
Sparse Core Ops, SparseCore 0:
  51.8 35.7 reduce-scatter.12
  91.2 24.0 all-gather.2
  129.5 33.0 reduce-scatter.16
  167.1 24.0 all-gather.4
  195.2 62.4 reduce-scatter.26
  261.4 65.7 reduce-scatter.24
  329.8 31.9 reduce-scatter.18
  364.5 33.1 reduce-scatter.14
  401.8 68.9 reduce-scatter.20
  474.7 68.0 reduce-scatter.22

commit v2 on v1

--- a/solution.py
+++ b/solution.py
@@ -194,75 +194,10 @@
     )(lengths, tokens, gain.reshape(1, model), w_qkv, codes, tables, expand)
 
 
-def attend_kernel(q_ref, kt_ref, v_ref, band_ref, w_ref, att_ref, qt_ref, partial_ref, s_ref):
-    heads, _, keys = kt_ref.shape
-    step = pl.program_id(0)
-    blocks = keys // BLOCK
-    low = lax.broadcasted_iota(jnp.int32, (CHUNK, BLOCK), 1) < FAR
-    lanes = lax.broadcasted_iota(jnp.int32, (CHUNK, BLOCK), 1)
-    results = []
-    for h in range(heads):
-        s_ref[...] = dot(q_ref[h], kt_ref[h])
-        for p in range(CHUNK // BLOCK):
-            block = step * (CHUNK // BLOCK) + p
-            start = jnp.clip(block - 1, 0, blocks - 3)
-            at = pl.ds(pl.multiple_of(start * BLOCK, BLOCK), BAND)
-            of = pl.ds(pl.multiple_of((start - block + 2) * BLOCK, BLOCK), BAND)
-            s_ref[p * BLOCK : (p + 1) * BLOCK, at] += band_ref[h, :, of]
-        s = s_ref[...]
-        top = jnp.max(s, axis=1, keepdims=True)
-        weights = jnp.exp(s - top).astype(bf16)
-        mixed = dot(weights, v_ref[h])
-        sums = pltpu.roll(mixed, 64, 1)
-        results.append(jnp.where(low, mixed / sums, 0.0))
-        total = -(top + jnp.log(mixed[:, 64:65]))
-        high, middle, rest = split3(total)
-        second = q_ref[h, :, BLOCK:].astype(f32)
-        second = jnp.where(
-            lanes == LSE, high, jnp.where(lanes == LSE + 1, middle, jnp.where(lanes == LSE + 2, rest, second))
-        )
-        qt_ref[h, :BLOCK, :] = q_ref[h, :, :BLOCK].astype(f32).T.astype(bf16)
-        qt_ref[h, BLOCK:, :] = second.T.astype(bf16)
-    pairs = []
-    for h in range(0, heads, 2):
-        pair = results[h]
-        if h + 1 < heads:
-            pair = jnp.where(low, pair, pltpu.roll(results[h + 1], 64, 1))
-        pairs.append(pair.astype(bf16))
-    att = jnp.concatenate(pairs, axis=1)
-    width = heads * 64
-    att_ref[...] = att[:, :width]
-    partial_ref[...] = dot(att[:, :width], w_ref[...]).astype(bf16)
-
-
-def attend(q, kt, v, band, w_output):
-    heads, rows, _ = q.shape
-    width, model = w_output.shape
-    full = pl.BlockSpec(memory_space=pltpu.VMEM)
-    return pl.pallas_call(
-        attend_kernel,
-        grid=(rows // CHUNK,),
-        in_specs=[pl.BlockSpec((heads, CHUNK, 256), lambda i: (0, i, 0)), full, full, full, full],
-        out_specs=[
-            pl.BlockSpec((CHUNK, width), lambda i: (i, 0)),
-            pl.BlockSpec((heads, 256, CHUNK), lambda i: (0, 0, i)),
-            pl.BlockSpec((CHUNK, model), lambda i: (i, 0)),
-        ],
-        out_shape=[
-            jax.ShapeDtypeStruct((rows, width), bf16),
-            jax.ShapeDtypeStruct((heads, 256, rows), bf16),
-            jax.ShapeDtypeStruct((rows, model), bf16),
-        ],
-        scratch_shapes=[pltpu.VMEM((CHUNK, rows), f32)],
-        compiler_params=pltpu.CompilerParams(vmem_limit_bytes=56 * MIB),
-        name="attend",
-    )(q, kt, v, band, w_output)
-
-
 def back_kernel(
     ghl_ref, w_ref, att_ref, q_ref, qt_ref, k_ref, kt_ref, v_ref, band_t_ref,
     grad_ref, sums_ref,
-    da_ref, dat_ref, s_ref, g_ref, pt_ref, gt_ref, dqt_ref, dk_ref, dv_ref, bands_ref, pad_ref,
+    da_ref, dat_ref, s_ref, pt_ref, gt_ref, dqt_ref, dk_ref, dv_ref, bands_ref, pad_ref,
 ):
     heads, rows, _ = k_ref.shape
     blocks = rows // BLOCK
@@ -305,9 +240,9 @@
         h = i // chunks
         c = i % chunks
         at = pl.ds(pl.multiple_of(c * CHUNK, CHUNK), CHUNK)
-        s_ref[...] = dot(k_ref[h], qt_ref[h, :, at])
+        s_ref[...] = dot(k_ref[h], qt_ref[h, c])
         for p in range(CHUNK // BLOCK):
-            block = c * (CHUNK // BLOCK) + p
+            block = p * chunks + c
             start = jnp.clip(block - 1, 0, blocks - 3)
             keys = pl.ds(pl.multiple_of(start * BLOCK, BLOCK), BAND)
             of = pl.ds(pl.multiple_of((start - block + 2) * BLOCK, BLOCK), BAND)
@@ -316,10 +251,13 @@
         pt_ref[...] = probs.astype(bf16)
         gt_ref[...] = (probs * dot(v_ref[h], dat_ref[h, :, at])).astype(bf16)
         dv_ref[h] += dot(pt_ref[...], da_ref[h, at, :])
-        dk_ref[h] += dot(gt_ref[...], q_ref[h, at, BLOCK:])
-        dqt_ref[h, :, at] = dot(kt_ref[h], gt_ref[...])
+        places = [pl.ds(pl.multiple_of((p * chunks + c) * BLOCK, BLOCK), BLOCK) for p in range(CHUNK // BLOCK)]
+        dk_ref[h] += dot(gt_ref[...], jnp.concatenate([q_ref[h, place, BLOCK:] for place in places], axis=0))
+        dq = dot(kt_ref[h], gt_ref[...])
         for p in range(CHUNK // BLOCK):
-            block = c * (CHUNK // BLOCK) + p
+            dqt_ref[h, :, places[p]] = dq[:, p * BLOCK : (p + 1) * BLOCK]
+        for p in range(CHUNK // BLOCK):
+            block = p * chunks + c
             start = jnp.clip(block - 1, 0, blocks - 3)
             keys = pl.ds(pl.multiple_of(start * BLOCK, BLOCK), BAND)
             of = pl.ds(pl.multiple_of((start - block + 2) * BLOCK, BLOCK), BAND)
@@ -388,7 +326,6 @@
             pltpu.VMEM((heads, rows, BLOCK), bf16),
             pltpu.VMEM((heads, BLOCK, rows), bf16),
             pltpu.VMEM((rows, CHUNK), f32),
-            pltpu.VMEM((rows, CHUNK), f32),
             pltpu.VMEM((rows, CHUNK), bf16),
             pltpu.VMEM((rows, CHUNK), bf16),
             pltpu.VMEM((heads, 256, rows), f32),
@@ -402,8 +339,371 @@
     )(ghl, w_output, att, q, qt, k, kt, v, band_t)
 
 
+def mp_places():
+    mp = lax.axis_index("mp")
+    y, core = mp // 2, mp % 2
+    return mp, y, core, y * 2 + (1 - core), (1 - y) * 2 + core
+
+
+def remote(src, dst, send, recv, mp):
+    return pltpu.make_async_remote_copy(
+        src_ref=src,
+        dst_ref=dst,
+        send_sem=send,
+        recv_sem=recv,
+        device_id=(lax.axis_index("dp"), mp),
+        device_id_type=pl.DeviceIdType.MESH,
+    )
+
+
+def meet():
+    _, _, _, sibling, across = mp_places()
+    barrier = pltpu.get_barrier_semaphore()
+    for other in (sibling, across):
+        pl.semaphore_signal(
+            barrier, inc=1, device_id=(lax.axis_index("dp"), other), device_id_type=pl.DeviceIdType.MESH
+        )
+    pl.semaphore_wait(barrier, 2)
+
+
+class Scatter:
+
+    def __init__(self, part, near, out, far, send, recv):
+        self.part, self.near, self.out, self.far, self.send, self.recv = part, near, out, far, send, recv
+
+    def first(self, c):
+        _, _, core, sibling, _ = mp_places()
+        return remote(self.part.at[c, 1 - core], self.near.at[c], self.send.at[c, 0], self.recv.at[c, 0], sibling)
+
+    def second(self, c):
+        _, _, _, _, across = mp_places()
+        return remote(self.out.at[c], self.far.at[c], self.send.at[c, 1], self.recv.at[c, 1], across)
+
+    def start(self, c):
+        self.first(c).start()
+
+    def middle(self, c):
+        _, y, core, _, _ = mp_places()
+        self.first(c).wait_recv()
+        self.out[c] = (self.part[c, core, 1 - y].astype(f32) + self.near[c, 1 - y].astype(f32)).astype(bf16)
+        self.second(c).start()
+
+    def finish(self, c):
+        _, y, core, _, _ = mp_places()
+        self.second(c).wait_recv()
+        own = self.part[c, core, y].astype(f32) + self.near[c, y].astype(f32)
+        return own + self.far[c].astype(f32)
+
+    def drain(self, c):
+        self.first(c).wait_send()
+        self.second(c).wait_send()
+
+
+class Gather:
+
+    def __init__(self, full, send, recv):
+        self.full, self.send, self.recv = full, send, recv
+
+    def copy(self, c, kind):
+        mp, _, _, sibling, across = mp_places()
+        at = self.full.at[c, across if kind == 2 else mp]
+        return remote(at, at, self.send.at[c, kind], self.recv.at[c, kind], across if kind == 1 else sibling)
+
+    def start(self, c):
+        self.copy(c, 1).start()
+        self.copy(c, 0).start()
+
+    def forward(self, c):
+        self.copy(c, 1).wait_recv()
+        self.copy(c, 2).start()
+
+    def finish(self, c):
+        self.copy(c, 0).wait_recv()
+        self.copy(c, 2).wait_recv()
+
+    def drain(self, c):
+        for kind in range(3):
+            self.copy(c, kind).wait_send()
+
+
+def scatter_scratch(chunks, piece, model):
+    return [
+        pltpu.VMEM((chunks, 2, 2, piece, model), bf16),
+        pltpu.VMEM((chunks, 2, piece, model), bf16),
+        pltpu.VMEM((chunks, piece, model), bf16),
+        pltpu.VMEM((chunks, piece, model), bf16),
+        pltpu.SemaphoreType.DMA((chunks, 2)),
+        pltpu.SemaphoreType.DMA((chunks, 2)),
+    ]
+
+
+def gather_scratch(chunks, piece, model):
+    return [
+        pltpu.VMEM((chunks, 4, piece, model), bf16),
+        pltpu.SemaphoreType.DMA((chunks, 3)),
+        pltpu.SemaphoreType.DMA((chunks, 3)),
+    ]
+
+
+ROOT = float(np.sqrt(2.0 / np.pi))
+CUBE = 0.044715
+
+
 def factor_of(rows):
     return lax.rsqrt(jnp.mean(rows * rows, axis=-1, keepdims=True) + EPSILON)
+
+
+def main_kernel(
+    q_ref, kt_ref, v_ref, band_ref, w_output_ref, tokens_ref, gain_ref, w_inner_ref, w_outer_ref, cot_ref,
+    qt_ref, att_ref, hidden_ref, ffn_ref, grad_hidden_ref, ghl_out_ref, grad_outer_ref, grad_inner_ref, gain_sum_ref,
+    s_ref, res_ref, low_ref, grad_low_ref, sum_ffn_ref, sum_norm_ref,
+    *comm,
+):
+    heads, _, rows = kt_ref.shape
+    pieces = 4
+    chunks = rows // CHUNK
+    blocks = rows // BLOCK
+    width = heads * 64
+    mp, _, _, _, _ = mp_places()
+    attn = Scatter(*comm[0:6])
+    norm = Scatter(*comm[6:12])
+    normed = Gather(*comm[12:15])
+    grads = Gather(*comm[15:18])
+    low = lax.broadcasted_iota(jnp.int32, (CHUNK, BLOCK), 1) < FAR
+    lanes = lax.broadcasted_iota(jnp.int32, (CHUNK, BLOCK), 1)
+    gain = gain_ref[...].astype(f32)
+    meet()
+
+    def place(m, c):
+        return pl.ds(pl.multiple_of((m * chunks + c) * BLOCK, BLOCK), BLOCK)
+
+    def own(c):
+        return pl.ds(pl.multiple_of(c * BLOCK, BLOCK), BLOCK)
+
+    def hidden_of(c):
+        hidden = tokens_ref[own(c), :].astype(f32) + attn.finish(c)
+        hidden_ref[own(c), :] = hidden
+        normed.full[c, mp] = (hidden * factor_of(hidden) * gain).astype(bf16)
+        normed.start(c)
+
+    def grad_of(c):
+        grad_normed = norm.finish(c)
+        hidden = hidden_ref[own(c), :]
+        factor = factor_of(hidden)
+        hat = hidden * factor
+        scaled = grad_normed * gain
+        back = factor * (scaled - hat * jnp.mean(scaled * hat, axis=-1, keepdims=True))
+        grad = cot_ref[place(mp, c), :].astype(f32) + back
+        grad_hidden_ref[own(c), :] = grad
+        gain_sum_ref[0:1, :] += jnp.sum(grad_normed * hat, axis=0, keepdims=True)
+        grads.full[c, mp] = grad.astype(bf16)
+        grads.start(c)
+
+    gain_sum_ref[...] = jnp.zeros_like(gain_sum_ref)
+
+    def attend(t, carry):
+        c = t // heads
+        h = t % heads
+        query = jnp.concatenate([q_ref[h, place(m, c), :] for m in range(pieces)], axis=0)
+        s_ref[...] = dot(query, kt_ref[h])
+        for m in range(pieces):
+            block = m * chunks + c
+            start = jnp.clip(block - 1, 0, blocks - 3)
+            at = pl.ds(pl.multiple_of(start * BLOCK, BLOCK), BAND)
+            of = pl.ds(pl.multiple_of((start - block + 2) * BLOCK, BLOCK), BAND)
+            s_ref[m * BLOCK : (m + 1) * BLOCK, at] += band_ref[h, :, of]
+        s = s_ref[...]
+        top = jnp.max(s, axis=1, keepdims=True)
+        weights = jnp.exp(s - top).astype(bf16)
+        mixed = dot(weights, v_ref[h])
+        sums = pltpu.roll(mixed, 64, 1)
+        res_ref[h] = jnp.where(low, mixed / sums, 0.0)
+        total = -(top + jnp.log(mixed[:, 64:65]))
+        high, middle, rest = split3(total)
+        second = query[:, BLOCK:].astype(f32)
+        second = jnp.where(
+            lanes == LSE, high, jnp.where(lanes == LSE + 1, middle, jnp.where(lanes == LSE + 2, rest, second))
+        )
+        qt_ref[h, c, :BLOCK, :] = query[:, :BLOCK].astype(f32).T.astype(bf16)
+        qt_ref[h, c, BLOCK:, :] = second.T.astype(bf16)
+
+        @pl.when((h == 0) & (c >= 1))
+        def _():
+            attn.middle(c - 1)
+
+        @pl.when((h == 0) & (c >= 2))
+        def _():
+            hidden_of(c - 2)
+
+        @pl.when(h == heads - 1)
+        def _():
+            pairs = []
+            for g in range(0, heads, 2):
+                pair = res_ref[g]
+                if g + 1 < heads:
+                    pair = jnp.where(low, pair, pltpu.roll(res_ref[g + 1], 64, 1))
+                pairs.append(pair.astype(bf16))
+            att = jnp.concatenate(pairs, axis=1)[:, :width]
+            att_ref[c] = att
+            partial = dot(att, w_output_ref[...]).astype(bf16)
+            for m in range(pieces):
+                attn.part[c, m % 2, m // 2] = partial[m * BLOCK : (m + 1) * BLOCK]
+            attn.start(c)
+
+        return carry
+
+    lax.fori_loop(0, chunks * heads, attend, 0)
+    normed.forward(0)
+    hidden_of(1)
+
+    steps = w_inner_ref.shape[1] // 256
+
+    def feed(t, carry):
+        c = t // steps
+        b = t % steps
+
+        @pl.when(b == 0)
+        def _():
+            normed.finish(c)
+
+        at = pl.ds(pl.multiple_of(b * 256, 256), 256)
+        x = jnp.concatenate([normed.full[c, m] for m in range(pieces)], axis=0)
+        cot = jnp.concatenate([cot_ref[place(m, c), :] for m in range(pieces)], axis=0)
+        inner = dot(x, w_inner_ref[:, at])
+        grad_act = dot_nt(cot, w_outer_ref[at, :])
+        square = inner * inner
+        tanh = jnp.tanh(ROOT * inner * (1.0 + CUBE * square))
+        half = 0.5 * (1.0 + tanh)
+        slope = half + 0.5 * inner * (1.0 - tanh * tanh) * (ROOT + 3.0 * CUBE * ROOT * square)
+        activated = (inner * half).astype(bf16)
+        grad_low = (slope * grad_act).astype(bf16)
+        low_ref[c, :, at] = activated
+        grad_low_ref[c, :, at] = grad_low
+        part_ffn = dot(activated, w_outer_ref[at, :])
+        part_norm = dot_nt(grad_low, w_inner_ref[:, at])
+
+        @pl.when(b == 0)
+        def _():
+            sum_ffn_ref[...] = part_ffn
+            sum_norm_ref[...] = part_norm
+
+        @pl.when(b > 0)
+        def _():
+            sum_ffn_ref[...] += part_ffn
+            sum_norm_ref[...] += part_norm
+
+        @pl.when((b == 0) & (c == 0))
+        def _():
+            attn.middle(2)
+
+        @pl.when((b == 0) & (c >= 1))
+        def _():
+            norm.middle(c - 1)
+
+        @pl.when((b == 1) & (c < 2))
+        def _():
+            normed.forward(c + 1)
+
+        @pl.when((b == steps - 1) & (c == 0))
+        def _():
+            hidden_of(2)
+
+        @pl.when((b == steps - 1) & (c >= 1))
+        def _():
+            grad_of(c - 1)
+
+        @pl.when((b == 1) & (c == 2))
+        def _():
+            grads.forward(0)
+
+        @pl.when(b == steps - 1)
+        def _():
+            for m in range(pieces):
+                ffn_ref[place(m, c), :] = sum_ffn_ref[m * BLOCK : (m + 1) * BLOCK, :].astype(bf16)
+                norm.part[c, m % 2, m // 2] = sum_norm_ref[m * BLOCK : (m + 1) * BLOCK, :].astype(bf16)
+            norm.start(c)
+
+        return carry
+
+    lax.fori_loop(0, chunks * steps, feed, 0)
+
+    def weights_of(b, carry):
+        at = pl.ds(pl.multiple_of(b * 256, 256), 256)
+        outer = jnp.zeros((256, cot_ref.shape[1]), f32)
+        inner = jnp.zeros((cot_ref.shape[1], 256), f32)
+        for c in range(chunks):
+            x = jnp.concatenate([normed.full[c, m] for m in range(pieces)], axis=0)
+            cot = jnp.concatenate([cot_ref[place(m, c), :] for m in range(pieces)], axis=0)
+            outer = outer + dot_tn(low_ref[c, :, at], cot)
+            inner = inner + dot_tn(x, grad_low_ref[c, :, at])
+        grad_outer_ref[at, :] = outer.astype(grad_outer_ref.dtype)
+        grad_inner_ref[:, at] = inner.astype(grad_inner_ref.dtype)
+
+        @pl.when(b == 0)
+        def _():
+            norm.middle(2)
+            grads.forward(1)
+
+        @pl.when(b == steps - 1)
+        def _():
+            grad_of(2)
+
+        return carry
+
+    lax.fori_loop(0, steps, weights_of, 0)
+    grads.forward(2)
+    for c in range(chunks):
+        grads.finish(c)
+    ghl_out_ref[...] = grads.full[...]
+    for c in range(chunks):
+        attn.drain(c)
+        norm.drain(c)
+        normed.drain(c)
+        grads.drain(c)
+
+
+def dot_tn(a, b):
+    return lax.dot_general(a, b, (((0,), (0,)), ((), ())), preferred_element_type=f32)
+
+
+def main_call(q, kt, v, band, w_output, tokens_share, gain, w_inner, w_outer, cotangent):
+    heads, rows, _ = q.shape
+    width, model = w_output.shape
+    share = tokens_share.shape[0]
+    chunks = rows // CHUNK
+    full = pl.BlockSpec(memory_space=pltpu.VMEM)
+    comm = (
+        scatter_scratch(chunks, BLOCK, model) * 2 + gather_scratch(chunks, BLOCK, model) * 2
+    )
+    return pl.pallas_call(
+        main_kernel,
+        in_specs=[full] * 10,
+        out_specs=[full] * 9,
+        out_shape=[
+            jax.ShapeDtypeStruct((heads, chunks, 256, CHUNK), bf16),
+            jax.ShapeDtypeStruct((chunks, CHUNK, width), bf16),
+            jax.ShapeDtypeStruct((share, model), f32),
+            jax.ShapeDtypeStruct((rows, model), bf16),
+            jax.ShapeDtypeStruct((share, model), f32),
+            jax.ShapeDtypeStruct((chunks, 4, BLOCK, model), bf16),
+            jax.ShapeDtypeStruct((w_outer.shape[0], model), f32),
+            jax.ShapeDtypeStruct((model, w_inner.shape[1]), f32),
+            jax.ShapeDtypeStruct((8, model), f32),
+        ],
+        scratch_shapes=[
+            pltpu.VMEM((CHUNK, rows), f32),
+            pltpu.VMEM((heads, CHUNK, BLOCK), f32),
+            pltpu.VMEM((chunks, CHUNK, w_inner.shape[1]), bf16),
+            pltpu.VMEM((chunks, CHUNK, w_inner.shape[1]), bf16),
+            pltpu.VMEM((CHUNK, model), f32),
+            pltpu.VMEM((CHUNK, model), f32),
+            *comm,
+        ],
+        compiler_params=pltpu.CompilerParams(
+            vmem_limit_bytes=63 * MIB, collective_id=1, has_side_effects=True
+        ),
+        name="forward_and_feed",
+    )(q, kt, v, band, w_output, tokens_share, gain.reshape(1, model), w_inner, w_outer, cotangent)
 
 
 def norm_back(inputs, grad_normed, gain):
@@ -423,36 +723,21 @@
     share = rows // lax.axis_size("mp")
     mp = lax.axis_index("mp")
     gain_a = gain_attn.astype(f32)
-    gain_f = gain_ffn.astype(f32)
     codes = jnp.stack([horizontal, vertical])
     normed_a, q, k, kt, v, band, band_t = prep(tokens, lengths, codes, gain_attn, w_qkv, bias_tables)
-    att, qt, partial = attend(q, kt, v, band, w_output)
-
-    def mine(x):
-        return lax.dynamic_slice_in_dim(x, mp * share, share, 0)
+    token_share = lax.dynamic_slice_in_dim(tokens, mp * share, share, 0)
+    qt, att, hidden, partial_ffn, grad_hidden, ghl, grad_outer, grad_inner, gain_sums = main_call(
+        q, kt, v, band, w_output, token_share, gain_ffn, w_inner, w_outer, cotangent
+    )
+    att = att.reshape(rows, width)
+    ghl = ghl.reshape(rows, model)
 
     def scatter(x):
         return lax.psum_scatter(x, "mp", scatter_dimension=0, tiled=True).astype(f32)
 
-    def gather(x):
-        return lax.all_gather(x, "mp", axis=0, tiled=True)
-
-    tokens_share = mine(tokens).astype(f32)
-    hidden = tokens_share + scatter(partial)
-    normed_f = gather((hidden * factor_of(hidden) * gain_f).astype(bf16))
-    inner = dot(normed_f, w_inner)
-    gelu, gelu_back = jax.vjp(jax.nn.gelu, inner)
-    activated = gelu.astype(bf16)
-    partial_ffn = dot(activated, w_outer).astype(bf16)
-    grad_act = dot_nt(cotangent, w_outer)
-    grad_inner_low = gelu_back(grad_act)[0].astype(bf16)
-    partial_norm = dot_nt(grad_inner_low, w_inner).astype(bf16)
-    grad_outer = lax.dot_general(activated, cotangent, (((0,), (0,)), ((), ())), preferred_element_type=f32)
-    grad_inner = lax.dot_general(normed_f, grad_inner_low, (((0,), (0,)), ((), ())), preferred_element_type=f32)
+    tokens_share = token_share.astype(f32)
+    gain_f_grad = gain_sums[0]
     mixed = (hidden + scatter(partial_ffn)).astype(bf16)
-    back_f, gain_f_grad = norm_back(hidden, scatter(partial_norm), gain_f)
-    grad_hidden = mine(cotangent).astype(f32) + back_f
-    ghl = gather(grad_hidden.astype(bf16))
     grad_output = lax.dot_general(att, ghl, (((0,), (0,)), ((), ())), preferred_element_type=f32)
     grads, sums = attend_back(ghl, w_output, att, q, qt, k, kt, v, band_t)
     grad_qkv = lax.dot_general(normed_a, grads, (((0,), (1,)), ((), ())), preferred_element_type=f32)

time: 558 us -> 479 us (0.86); the launches traced: 550 us -> 478 us
  waiting for transfers between devices: 304 us -> 210 us
  Pallas kernels: 67.5 us -> 135 us
  matrix products: 49.1 us -> 13.5 us
  local copies, waits for them, and re-layouts: 38.5 us -> 31.7 us
    unnamed x12 -> x9, waiting for transfers between devices: 25.3 us -> 117 us
    reduce_scatter x2 -> x1, waiting for transfers between devices: 135 us -> 60.7 us  [spread(): return lax.psum_scatter(x, 'dp', scatter_dimension=axis, tiled=True)]
    reduce_scatter x4 -> x2, waiting for transfers between devices: 101 us -> 32.6 us  [scatter(): lax.psum_scatter(x, 'mp', scatter_dimension=0, tiled=True).astype(f32)]
    pallas_call x1, Pallas kernels: 18 us -> 85.4 us  [main_call(): pl.pallas_call(main_kernel, in_specs=[full] * 10, out_specs=[full] * 9, o...]
    all_gather x2 -> x0, waiting for transfers between devices: 42 us -> none  [gather(): return lax.all_gather(x, 'mp', axis=0, tiled=True)]
    dot_general x4 -> x0, matrix products: 27.2 us -> none  [the longest x2 15.9 us: dot(): return jnp.dot(a, b, preferred_element_type=f32)]
    dot_general x5 -> x3, matrix products: 13.3 us -> 4.91 us  [dot_nt(): lax.dot_general(a, b, (((1,), (1,)), ((), ())), preferred_element_type=f32)]
    unnamed x56 -> x53, local copies, waits for them, and re-layouts: 30.9 us -> 24.2 us
  transfers between devices with their start and end apart: 10 -> 6, of which waited for: 8 -> 4; matrix products, arithmetic and copies ran while one was open for 10% -> 7% of each run, Pallas kernels for 7% -> 8%
where the time goes in v2:
time: 479 us; the launch traced here: 478 us
  waiting for transfers between devices  210 us (44%)
  Pallas kernels  135 us (28%)
  blocking collectives  61.9 us (13%)
  local copies, waits for them, and re-layouts  31.7 us (7%)
  between operations  15 us (3%)
  matrix products  13.5 us (3%)
  other arithmetic  9.59 us (2%)
    unnamed x9, waiting for transfers between devices  117 us
    pallas_call x1, Pallas kernels, main_call(): pl.pallas_call(main_kernel, in_specs=[full] * 10, out_specs=[full] * 9, o...  85.4 us
    reduce_scatter x1, waiting for transfers between devices, spread(): return lax.psum_scatter(x, 'dp', scatter_dimension=axis, tiled=True)  60.7 us
    psum x1, blocking collectives, local(): gains = lax.psum(jnp.stack([gain_a_grad, gain_f_grad]), ('dp', 'mp'))  39.6 us
    pallas_call x1, Pallas kernels, attend_back(): pl.pallas_call(back_kernel, in_specs=[full] * 9, out_specs=[full] * 2, ou...  38.2 us
    reduce_scatter x2, waiting for transfers between devices, scatter(): lax.psum_scatter(x, 'mp', scatter_dimension=0, tiled=True).astype(f32)  32.6 us
    unnamed x53, local copies, waits for them, and re-layouts  24.2 us
    psum x1, blocking collectives, local(): tables = lax.psum(tables, 'dp')  22.3 us
  transfers between devices with their start and end apart: 6, of which 4 were waited for; matrix products, arithmetic and copies ran while one was open for 7% of the time, Pallas kernels for 8%

profile of v2, /device:TPU:0, one launch (start us, length us, event | category | flops | bytes accessed | tf_op | source)
XLA Modules:
  0.0 477.9 jit_solution(10381085138578446584)
XLA Ops:
  8.0 0.7 reshape.43.gain_ref
  8.6 1.5 copy.27.w_ref
  10.2 0.6 reshape.44.gain_ref
  10.9 2.0 fusion.6
  12.8 11.7 %prep.1 = (bf16[1536,768]{1,0:T(8,128)(2,1)S(1)}, bf16[3,1536,256]{2,1,0:T(8,128)(2,1)S(1)}, bf16[3,1536,256]{2,1,0:T(8,128)(2,1)S(1)}, bf16[3,256,1536]{2,1,0:T...) custom-call(s32[1]{0:T(128)S(6)} %copy.38.length_ref, ...), custom_call_target="tpu_custom_call" | custom-call | tf_op jit(solution)/shard_map/prep/pallas_call | solution.py:161
  24.6 1.4 copy-done
  26.0 1.5 copy-done.1
  27.5 1.0 copy-done.2
  28.5 1.4 copy-done.3
  29.9 1.1 copy-done.4
  30.9 1.0 copy-done.5
  31.9 1.5 copy-done.7
  33.4 85.4 %forward_and_feed.1 = (bf16[3,3,256,512]{3,2,1,0:T(8,128)(2,1)}, bf16[3,512,192]{2,1,0:T(8,128)(2,1)}, f32[384,768]{1,0:T(8,128)}, bf16[1536,768]{1,0:T(8,128)(2...) custom-call(bf16[3,1536,256]{2,1,0:T(8,128)(2,1)} %copy-done, ...), custom_call_target="tpu_custom_call" | custom-call | tf_op jit(solution)/shard_map/forward_and_feed/pallas_call | solution.py:678
  118.8 3.8 convolution_bitcast_fusion
  122.6 0.0 reduce-scatter.19.cloned.1.call-start
  122.7 38.2 %attend_back.1 = (bf16[3,1536,192]{2,1,0:T(8,128)(2,1)}, f32[8,1280]{1,0:T(8,128)}) custom-call(bf16[1536,768]{1,0:T(8,128)(2,1)} %bitcast.43, bf16[192,768]{1,0:T(8,128)(2,1)} %w_ref.2, bf16[1536,192]{1,0:T(8,128)(2,1)} %bitcast.48, bf16[3,1536,256]{2,1,0:T(8,128)(2,1)} %copy-done, bf16[3,3,256,512]{3,2,1,0:T(8,128)(2,1)} %get-tuple-element.36.qt_ref, ...), custom_call_target="tpu_custom_call" | custom-call | tf_op jit(solution)/shard_map/attend_back/pallas_call | solution.py:317
  160.9 4.2 copy.28
  165.0 4.3 fusion.24
  169.4 2.9 copy.31
  172.3 2.8 reshape.49
  175.2 0.3 reduce-scatter.15.cloned.1.call-start
  175.5 0.9 copy-done.11
  176.3 1.9 fusion.11
  178.2 0.8 fusion.9
  179.0 2.2 add_convert_fusion
  181.3 0.0 reduce-scatter.13.cloned.1.call-start
  181.3 0.5 reduce-scatter.13.cloned.1.call-update
  181.9 0.5 reduce-scatter.17.cloned.1.call-update
  182.5 1.0 copy-done.13
  183.5 2.0 copy.35
  185.5 0.6 copy-done.20
  186.2 1.4 slice.36
  187.6 0.4 fusion.22
  188.1 22.3 %psum.15 = f32[96,3]{0,1:T(4,128)} all-reduce(f32[96,3]{0,1:T(4,128)S(1)} %fusion.22), channel_id=1, replica_groups=mesh['dp'=8,'mp'=4] {'dp'}, use_global_device_ids=true, to_apply=%region_10.11 | all-reduce | flops 288 | bytes 2304 | tf_op jit(solution)/shard_map/psum | solution.py:752
  210.4 1.6 copy.34
  212.0 44.0 %reduce-scatter.19.cloned.1.call-done = f32[96,576]{1,0:T(8,128)} async-done(((f32[768,576]{1,0:T(8,128)}), f32[96,576]{1,0:T(8,128)}) %reduce-scatter.19.cloned.1.call-update) | async-done | bytes 221200
  256.0 1.1 reshape.50
  257.2 0.8 copy.29
  257.9 32.6 %reduce-scatter.15.cloned.1.call-done = bf16[384,768]{1,0:T(8,128)(2,1)} async-done(((bf16[1536,768]{1,0:T(8,128)(2,1)}), bf16[384,768]{1,0:T(8,128)(2,1)}) %reduce-scatter.15.cloned.1.call-update) | async-done | bytes 589840 | tf_op jit(solution)/shard_map/reduce_scatter | solution.py:736
  290.5 2.3 fusion.7
  292.8 1.3 pad_maximum_fusion
  294.1 39.6 %psum.14 = f32[2,768]{1,0:T(2,128)S(1)} all-reduce(f32[2,768]{1,0:T(2,128)} %pad_maximum_fusion), channel_id=1, replica_groups=mesh['dp'=8,'mp'=4] {'dp','mp'}, use_global_device_ids=true, to_apply=%region_9.10 | all-reduce | flops 1536 | bytes 12288 | tf_op jit(solution)/shard_map/psum | solution.py:751
  333.7 0.6 slice_reduce_fusion
  334.3 0.7 broadcast_multiply_fusion
  335.0 2.0 add_convert_fusion.1
  337.0 1.4 fusion.4
  338.3 60.7 %reduce-scatter.17.cloned.1.call-done = f32[96,768]{1,0:T(8,128)} async-done(((f32[768,768]{1,0:T(8,128)}), f32[96,768]{1,0:T(8,128)}) %reduce-scatter.17.cloned.1.call-update) | async-done | bytes 294928 | tf_op jit(solution)/shard_map/reduce_scatter | solution.py:755
  399.1 72.0 %reduce-scatter.23.cloned.1.call-done = f32[96,768]{1,0:T(8,128)} async-done(((f32[768,768]{1,0:T(8,128)}), f32[96,768]{1,0:T(8,128)}) %reduce-scatter.23.cloned.1.call-update) | async-done | bytes 294928
  (52 shorter events, 0.3 us)
Async XLA Ops:
  7.2 5.7 %copy-start.6 = (bf16[96,1024]{1,0:T(8,128)(2,1)S(1)}, bf16[96,1024]{1,0:T(8,128)(2,1)}, u32[]{:S(2)}) copy-start(bf16[96,1024]{1,0:T(8,128)(2,1)} %constant.24.clone.expand_ref) | copy-start | bytes 589828
  7.2 3.0 copy-start.18
  7.2 3.0 copy-start.19
  7.2 3.0 copy-start.21
  7.2 3.6 copy-start.22
  7.2 203.2 %reduce-scatter.21.cloned.1.call-start = ((), (), s32[]{:S(2)}) async-start(), calls=%async_computation.10 | async-start | bytes 884736
  24.6 1.4 copy-start
  26.0 1.5 copy-start.1
  27.5 1.0 copy-start.2
  28.5 1.4 copy-start.3
  29.9 1.1 copy-start.4
  30.9 1.0 copy-start.5
  31.9 1.5 copy-start.7
  122.6 133.4 %reduce-scatter.19.cloned.1.call-start = ((), (), s32[]{:S(2)}) async-start(), calls=%async_computation.9 | async-start | bytes 2211840
  160.9 4.2 copy-start.8
  175.1 1.2 copy-start.11
  175.2 3.0 copy-start.10
  175.2 115.3 %reduce-scatter.15.cloned.1.call-start = ((), (), s32[]{:S(2)}) async-start(), calls=%async_computation.7 | async-start | bytes 2949120 | tf_op jit(solution)/shard_map/reduce_scatter | solution.py:736
  181.3 153.7 %reduce-scatter.13.cloned.1.call-start = ((), (), s32[]{:S(2)}) async-start(), calls=%async_computation.6 | async-start | bytes 2949120 | tf_op jit(solution)/shard_map/reduce_scatter | solution.py:736
  181.8 1.7 copy-start.13
  181.9 217.2 %reduce-scatter.17.cloned.1.call-start = ((), (), s32[]{:S(2)}) async-start(), calls=%async_computation.8 | async-start | bytes 2654208 | tf_op jit(solution)/shard_map/reduce_scatter | solution.py:755
  182.4 288.6 %reduce-scatter.23.cloned.1.call-start = ((), (), s32[]{:S(2)}) async-start(), calls=%async_computation.11 | async-start | bytes 2654208
  185.5 0.7 copy-start.20
  185.5 2.1 copy-start.16
  185.5 2.1 copy-start.17
  185.5 105.0 %copy-start.9 = (bf16[384,768]{1,0:T(8,128)(2,1)S(1)}, bf16[384,768]{1,0:T(8,128)(2,1)}, u32[]{:S(2)}) copy-start(bf16[384,768]{1,0:T(8,128)(2,1)} %get-tuple-element.68.tokens_ref) | copy-start | bytes 1769476
  186.2 148.8 %copy-start.15 = (f32[384,768]{1,0:T(8,128)S(1)}, f32[384,768]{1,0:T(8,128)}, u32[]{:S(2)}) copy-start(f32[384,768]{1,0:T(8,128)} %get-tuple-element.31) | copy-start | bytes 3538948
  257.9 79.1 %copy-start.14 = (f32[384,768]{1,0:T(8,128)S(1)}, f32[384,768]{1,0:T(8,128)}, u32[]{:S(2)}) copy-start(f32[384,768]{1,0:T(8,128)} %get-tuple-element.33) | copy-start | bytes 3538948
  290.5 46.5 %copy-start.12 = (bf16[384,768]{1,0:T(8,128)(2,1)S(1)}, bf16[384,768]{1,0:T(8,128)(2,1)}, u32[]{:S(2)}) copy-start(bf16[384,768]{1,0:T(8,128)(2,1)} %reduce-scatter.15.cloned.1.call-done) | copy-start | bytes 1769476
Sparse Core Ops, SparseCore 0:
  122.8 63.2 reduce-scatter.20
  190.0 66.0 reduce-scatter.18
  258.6 31.8 reduce-scatter.14
  293.1 33.1 reduce-scatter.12
  330.1 68.8 reduce-scatter.16
  403.0 68.0 reduce-scatter.22

commit v3 on v2

--- a/solution.py
+++ b/solution.py
@@ -194,151 +194,6 @@
     )(lengths, tokens, gain.reshape(1, model), w_qkv, codes, tables, expand)
 
 
-def back_kernel(
-    ghl_ref, w_ref, att_ref, q_ref, qt_ref, k_ref, kt_ref, v_ref, band_t_ref,
-    grad_ref, sums_ref,
-    da_ref, dat_ref, s_ref, pt_ref, gt_ref, dqt_ref, dk_ref, dv_ref, bands_ref, pad_ref,
-):
-    heads, rows, _ = k_ref.shape
-    blocks = rows // BLOCK
-    chunks = rows // CHUNK
-    width = heads * 64
-    lanes = lax.broadcasted_iota(jnp.int32, (CHUNK, BLOCK), 1)
-    low = lanes < FAR
-    pad_ref[...] = jnp.zeros_like(pad_ref)
-
-    def prologue(c, carry):
-        at = pl.ds(pl.multiple_of(c * CHUNK, CHUNK), CHUNK)
-        pad_ref[:, :width] = dot_nt(ghl_ref[at, :], w_ref[...]).astype(bf16).astype(f32)
-        pad_ref[:, 256 : 256 + width] = att_ref[at, :].astype(f32)
-        for h in range(heads):
-            base = h // 2 * BLOCK
-            grad = pad_ref[:, base : base + BLOCK]
-            out = pad_ref[:, 256 + base : 256 + base + BLOCK]
-            if h % 2 == 1:
-                grad = pltpu.roll(grad, 64, 1)
-                out = pltpu.roll(out, 64, 1)
-            total = -jnp.sum(jnp.where(low, grad * out, 0.0), axis=1, keepdims=True)
-            high, middle, rest = split3(total)
-            grad = jnp.where(
-                low,
-                grad,
-                jnp.where(
-                    lanes == FAR, high, jnp.where(lanes == FAR + 1, middle, jnp.where(lanes == FAR + 2, rest, 0.0))
-                ),
-            )
-            da_ref[h, at, :] = grad.astype(bf16)
-            dat_ref[h, :, at] = grad.T.astype(bf16)
-        return carry
-
-    lax.fori_loop(0, chunks, prologue, 0)
-    dk_ref[...] = jnp.zeros_like(dk_ref)
-    dv_ref[...] = jnp.zeros_like(dv_ref)
-    bands_ref[...] = jnp.zeros_like(bands_ref)
-
-    def main(i, carry):
-        h = i // chunks
-        c = i % chunks
-        at = pl.ds(pl.multiple_of(c * CHUNK, CHUNK), CHUNK)
-        s_ref[...] = dot(k_ref[h], qt_ref[h, c])
-        for p in range(CHUNK // BLOCK):
-            block = p * chunks + c
-            start = jnp.clip(block - 1, 0, blocks - 3)
-            keys = pl.ds(pl.multiple_of(start * BLOCK, BLOCK), BAND)
-            of = pl.ds(pl.multiple_of((start - block + 2) * BLOCK, BLOCK), BAND)
-            s_ref[keys, p * BLOCK : (p + 1) * BLOCK] += band_t_ref[h, of, :]
-        probs = jnp.exp(s_ref[...])
-        pt_ref[...] = probs.astype(bf16)
-        gt_ref[...] = (probs * dot(v_ref[h], dat_ref[h, :, at])).astype(bf16)
-        dv_ref[h] += dot(pt_ref[...], da_ref[h, at, :])
-        places = [pl.ds(pl.multiple_of((p * chunks + c) * BLOCK, BLOCK), BLOCK) for p in range(CHUNK // BLOCK)]
-        dk_ref[h] += dot(gt_ref[...], jnp.concatenate([q_ref[h, place, BLOCK:] for place in places], axis=0))
-        dq = dot(kt_ref[h], gt_ref[...])
-        for p in range(CHUNK // BLOCK):
-            dqt_ref[h, :, places[p]] = dq[:, p * BLOCK : (p + 1) * BLOCK]
-        for p in range(CHUNK // BLOCK):
-            block = p * chunks + c
-            start = jnp.clip(block - 1, 0, blocks - 3)
-            keys = pl.ds(pl.multiple_of(start * BLOCK, BLOCK), BAND)
-            of = pl.ds(pl.multiple_of((start - block + 2) * BLOCK, BLOCK), BAND)
-            bands_ref[h, of, :] += gt_ref[keys, p * BLOCK : (p + 1) * BLOCK].astype(f32)
-        return carry
-
-    lax.fori_loop(0, heads * chunks, main, 0)
-
-    def pack(k, parts):
-        merged = []
-        for h in range(0, heads, 2):
-            pair = parts[h]
-            pair_low = lax.broadcasted_iota(jnp.int32, pair.shape, 1) < 64
-            if h + 1 < heads:
-                pair = jnp.where(pair_low, pair, pltpu.roll(parts[h + 1], 64, 1))
-            merged.append(pair.astype(bf16))
-        grad_ref[k] = jnp.concatenate(merged, axis=1)[:, :width]
-
-    pack(0, [dqt_ref[h, BLOCK:, :].T * 0.125 for h in range(heads)])
-    pack(1, [dk_ref[h] for h in range(heads)])
-    pack(2, [dv_ref[h] for h in range(heads)])
-
-    sums_ref[...] = jnp.zeros_like(sums_ref)
-    lines16 = lax.broadcasted_iota(jnp.int32, (16, rows), 0)
-    block = lax.broadcasted_iota(jnp.int32, (16, rows), 1) // BLOCK
-    start = jnp.clip(block - 1, 0, blocks - 3)
-    real = lines16 < blocks
-    plane_rows = lax.broadcasted_iota(jnp.int32, (BLOCK, BLOCK), 0)
-    plane_lanes = lax.broadcasted_iota(jnp.int32, (BLOCK, BLOCK), 1)
-
-    def fold(value):
-        total = value[:, :BLOCK]
-        for b in range(1, value.shape[1] // BLOCK):
-            total = total + value[:, b * BLOCK : (b + 1) * BLOCK]
-        return jnp.sum(total, axis=0, keepdims=True)
-
-    for h in range(heads):
-        band = roll_rows(bands_ref[h].T, False)
-        sums_ref[h : h + 1, :WIDE] = jnp.sum(band, axis=0, keepdims=True)
-        spread = dqt_ref[h, :BLOCK, :]
-        high = spread.astype(bf16)
-        rest = (spread - high.astype(f32)).astype(bf16)
-        hot = k_ref[h, :, :BLOCK]
-        plane = (dot(high, hot) + dot(rest, hot)).T
-        plane = jnp.where((plane_rows < CODES) == (plane_lanes < CODES), plane, 0.0)
-        plane = roll_rows(plane, False)
-        sums_ref[h : h + 1, WIDE : WIDE + BLOCK] = jnp.sum(plane[:CODES], axis=0, keepdims=True)
-        sums_ref[h : h + 1, WIDE + BLOCK : WIDE + 2 * BLOCK] = jnp.sum(plane[CODES:], axis=0, keepdims=True)
-        far = dqt_ref[h, BLOCK + FAR : BLOCK + FAR + 16, :]
-        sums_ref[h : h + 1, WIDE + 2 * BLOCK : WIDE + 3 * BLOCK] = fold(jnp.where(real & (lines16 < start), far, 0.0))
-        sums_ref[h : h + 1, WIDE + 3 * BLOCK :] = fold(jnp.where(real & (lines16 > start + 2), far, 0.0))
-
-
-def attend_back(ghl, w_output, att, q, qt, k, kt, v, band_t):
-    heads, rows, _ = q.shape
-    full = pl.BlockSpec(memory_space=pltpu.VMEM)
-    return pl.pallas_call(
-        back_kernel,
-        in_specs=[full] * 9,
-        out_specs=[full] * 2,
-        out_shape=[
-            jax.ShapeDtypeStruct((3, rows, heads * 64), bf16),
-            jax.ShapeDtypeStruct((8, WIDE + 4 * BLOCK), f32),
-        ],
-        scratch_shapes=[
-            pltpu.VMEM((heads, rows, BLOCK), bf16),
-            pltpu.VMEM((heads, BLOCK, rows), bf16),
-            pltpu.VMEM((rows, CHUNK), f32),
-            pltpu.VMEM((rows, CHUNK), bf16),
-            pltpu.VMEM((rows, CHUNK), bf16),
-            pltpu.VMEM((heads, 256, rows), f32),
-            pltpu.VMEM((heads, rows, BLOCK), f32),
-            pltpu.VMEM((heads, rows, BLOCK), f32),
-            pltpu.VMEM((heads, WIDE, BLOCK), f32),
-            pltpu.VMEM((CHUNK, 512), f32),
-        ],
-        compiler_params=pltpu.CompilerParams(vmem_limit_bytes=60 * MIB),
-        name="attend_back",
-    )(ghl, w_output, att, q, qt, k, kt, v, band_t)
-
-
 def mp_places():
     mp = lax.axis_index("mp")
     y, core = mp // 2, mp % 2
@@ -454,6 +309,7 @@
 
 
 def main_kernel(
+    fast,
     q_ref, kt_ref, v_ref, band_ref, w_output_ref, tokens_ref, gain_ref, w_inner_ref, w_outer_ref, cot_ref,
     qt_ref, att_ref, hidden_ref, ffn_ref, grad_hidden_ref, ghl_out_ref, grad_outer_ref, grad_inner_ref, gain_sum_ref,
     s_ref, res_ref, low_ref, grad_low_ref, sum_ffn_ref, sum_norm_ref,
@@ -619,7 +475,7 @@
         @pl.when(b == steps - 1)
         def _():
             for m in range(pieces):
-                ffn_ref[place(m, c), :] = sum_ffn_ref[m * BLOCK : (m + 1) * BLOCK, :].astype(bf16)
+                ffn_ref[c, m % 2, m // 2] = sum_ffn_ref[m * BLOCK : (m + 1) * BLOCK, :].astype(bf16)
                 norm.part[c, m % 2, m // 2] = sum_norm_ref[m * BLOCK : (m + 1) * BLOCK, :].astype(bf16)
             norm.start(c)
 
@@ -627,30 +483,31 @@
 
     lax.fori_loop(0, chunks * steps, feed, 0)
 
-    def weights_of(b, carry):
-        at = pl.ds(pl.multiple_of(b * 256, 256), 256)
-        outer = jnp.zeros((256, cot_ref.shape[1]), f32)
-        inner = jnp.zeros((cot_ref.shape[1], 256), f32)
+    model = cot_ref.shape[1]
+
+    def weights_of(b):
+        at = slice(b * (model // 2), (b + 1) * (model // 2))
+        outer = jnp.zeros((model // 2, low_ref.shape[2]), f32)
+        inner = jnp.zeros((model // 2, low_ref.shape[2]), f32)
         for c in range(chunks):
-            x = jnp.concatenate([normed.full[c, m] for m in range(pieces)], axis=0)
-            cot = jnp.concatenate([cot_ref[place(m, c), :] for m in range(pieces)], axis=0)
-            outer = outer + dot_tn(low_ref[c, :, at], cot)
-            inner = inner + dot_tn(x, grad_low_ref[c, :, at])
-        grad_outer_ref[at, :] = outer.astype(grad_outer_ref.dtype)
-        grad_inner_ref[:, at] = inner.astype(grad_inner_ref.dtype)
-
-        @pl.when(b == 0)
-        def _():
-            norm.middle(2)
-            grads.forward(1)
-
-        @pl.when(b == steps - 1)
-        def _():
-            grad_of(2)
-
-        return carry
-
-    lax.fori_loop(0, steps, weights_of, 0)
+            x = jnp.concatenate([normed.full[c, m, :, at] for m in range(pieces)], axis=0)
+            cot = jnp.concatenate([cot_ref[place(m, c), at] for m in range(pieces)], axis=0)
+            outer = outer + dot_tn(cot, low_ref[c])
+            inner = inner + dot_tn(x, grad_low_ref[c])
+        for ref, value in ((grad_outer_ref, outer), (grad_inner_ref, inner)):
+            if fast:
+                each = model // 8
+                for r in range(4):
+                    j = b * 4 + r
+                    ref[j % 2, j // 2] = value[r * each : (r + 1) * each].astype(bf16)
+            else:
+                ref[at, :] = value
+
+    weights_of(0)
+    norm.middle(2)
+    grads.forward(1)
+    weights_of(1)
+    grad_of(2)
     grads.forward(2)
     for c in range(chunks):
         grads.finish(c)
@@ -666,7 +523,7 @@
     return lax.dot_general(a, b, (((0,), (0,)), ((), ())), preferred_element_type=f32)
 
 
-def main_call(q, kt, v, band, w_output, tokens_share, gain, w_inner, w_outer, cotangent):
+def main_call(fast, q, kt, v, band, w_output, tokens_share, gain, w_inner, w_outer, cotangent):
     heads, rows, _ = q.shape
     width, model = w_output.shape
     share = tokens_share.shape[0]
@@ -675,19 +532,22 @@
     comm = (
         scatter_scratch(chunks, BLOCK, model) * 2 + gather_scratch(chunks, BLOCK, model) * 2
     )
+    weights = jax.ShapeDtypeStruct((model, w_inner.shape[1]), f32)
+    if fast:
+        weights = jax.ShapeDtypeStruct((2, 4, model // 8, w_inner.shape[1]), bf16)
     return pl.pallas_call(
-        main_kernel,
+        functools.partial(main_kernel, fast),
         in_specs=[full] * 10,
         out_specs=[full] * 9,
         out_shape=[
             jax.ShapeDtypeStruct((heads, chunks, 256, CHUNK), bf16),
             jax.ShapeDtypeStruct((chunks, CHUNK, width), bf16),
             jax.ShapeDtypeStruct((share, model), f32),
-            jax.ShapeDtypeStruct((rows, model), bf16),
+            jax.ShapeDtypeStruct((chunks, 2, 2, BLOCK, model), bf16),
             jax.ShapeDtypeStruct((share, model), f32),
             jax.ShapeDtypeStruct((chunks, 4, BLOCK, model), bf16),
-            jax.ShapeDtypeStruct((w_outer.shape[0], model), f32),
-            jax.ShapeDtypeStruct((model, w_inner.shape[1]), f32),
+            weights,
+            weights,
             jax.ShapeDtypeStruct((8, model), f32),
         ],
         scratch_shapes=[
@@ -706,70 +566,520 @@
     )(q, kt, v, band, w_output, tokens_share, gain.reshape(1, model), w_inner, w_outer, cotangent)
 
 
-def norm_back(inputs, grad_normed, gain):
-    factor = factor_of(inputs)
-    hat = inputs * factor
-    scaled = grad_normed * gain
-    back = factor * (scaled - hat * jnp.mean(scaled * hat, axis=-1, keepdims=True))
-    return back, jnp.sum(grad_normed * hat, axis=0)
+def dp_places():
+    dp = lax.axis_index("dp")
+    return dp // 2, dp % 2
+
+
+def remote_dp(src, dst, send, recv, dp):
+    return pltpu.make_async_remote_copy(
+        src_ref=src,
+        dst_ref=dst,
+        send_sem=send,
+        recv_sem=recv,
+        device_id=(dp, lax.axis_index("mp")),
+        device_id_type=pl.DeviceIdType.MESH,
+    )
+
+
+def meet_all(fast):
+    mp, _, _, sibling, across = mp_places()
+    dp = lax.axis_index("dp")
+    z, x = dp_places()
+    others = [(dp, sibling), (dp, across)]
+    if fast:
+        others.append((z * 2 + 1 - x, mp))
+        others.extend(((z + d) % 4 * 2 + x, mp) for d in (1, 2, 3))
+    barrier = pltpu.get_barrier_semaphore()
+    for other in others:
+        pl.semaphore_signal(barrier, inc=1, device_id=other, device_id_type=pl.DeviceIdType.MESH)
+    pl.semaphore_wait(barrier, len(others))
+
+
+class Spread:
+
+    def __init__(self, part, near, out, far, send, recv):
+        self.part, self.near, self.out, self.far, self.send, self.recv = part, near, out, far, send, recv
+
+    def first(self):
+        z, x = dp_places()
+        return remote_dp(self.part.at[1 - x], self.near, self.send.at[0], self.recv.at[0], z * 2 + 1 - x)
+
+    def second(self, d):
+        z, x = dp_places()
+        to = (z + d) % 4
+        return remote_dp(self.out.at[to], self.far.at[d - 1], self.send.at[d], self.recv.at[d], to * 2 + x)
+
+    def start(self):
+        self.first().start()
+
+    def middle(self):
+        z, x = dp_places()
+        self.first().wait_recv()
+        for d in range(1, 4):
+            to = (z + d) % 4
+            self.out[to] = (self.part[x, to].astype(f32) + self.near[to].astype(f32)).astype(bf16)
+            self.second(d).start()
+
+    def finish(self):
+        z, x = dp_places()
+        total = self.part[x, z].astype(f32) + self.near[z].astype(f32)
+        for d in range(1, 4):
+            self.second(d).wait_recv()
+            total = total + self.far[d - 1].astype(f32)
+        return total
+
+    def drain(self):
+        self.first().wait_send()
+        for d in range(1, 4):
+            self.second(d).wait_send()
+
+
+def spread_scratch(rows, columns, lead=(), part=True):
+    buffers = [pltpu.VMEM((*lead, 2, 4, rows, columns), bf16)] if part else []
+    return buffers + [
+        pltpu.VMEM((*lead, 4, rows, columns), bf16),
+        pltpu.VMEM((*lead, 4, rows, columns), bf16),
+        pltpu.VMEM((*lead, 3, rows, columns), bf16),
+        pltpu.SemaphoreType.DMA((*lead, 4)),
+        pltpu.SemaphoreType.DMA((*lead, 4)),
+    ]
+
+
+class Total:
+
+    def __init__(self, value, near, far, across, send, recv):
+        self.value, self.near, self.far, self.across, self.send, self.recv = value, near, far, across, send, recv
+
+    def copy(self, kind):
+        z, x = dp_places()
+        mp, _, _, sibling, across = mp_places()
+        send, recv = self.send.at[kind], self.recv.at[kind]
+        if kind == 0:
+            return remote_dp(self.value.at[0], self.near, send, recv, z * 2 + 1 - x)
+        if kind < 4:
+            return remote_dp(self.value.at[1], self.far.at[kind - 1], send, recv, (z + kind) % 4 * 2 + x)
+        if kind == 4:
+            return remote(self.value.at[2], self.across.at[0], send, recv, sibling)
+        return remote(self.value.at[3], self.across.at[1], send, recv, across)
+
+    def start(self):
+        self.copy(0).start()
+
+    def over_z(self):
+        self.copy(0).wait_recv()
+        self.value[1] = self.value[0] + self.near[...]
+        for kind in range(1, 4):
+            self.copy(kind).start()
+
+    def over_core(self):
+        total = self.value[1]
+        for kind in range(1, 4):
+            self.copy(kind).wait_recv()
+            total = total + self.far[kind - 1]
+        self.value[2] = total
+        self.copy(4).start()
+
+    def over_y(self):
+        self.copy(4).wait_recv()
+        self.value[3] = self.value[2] + self.across[0]
+        self.copy(5).start()
+
+    def finish(self):
+        self.copy(5).wait_recv()
+        return self.value[3] + self.across[1]
+
+    def drain(self):
+        for kind in range(6):
+            self.copy(kind).wait_send()
+
+
+def total_scratch(rows, columns):
+    return [
+        pltpu.VMEM((4, rows, columns), f32),
+        pltpu.VMEM((rows, columns), f32),
+        pltpu.VMEM((3, rows, columns), f32),
+        pltpu.VMEM((2, rows, columns), f32),
+        pltpu.SemaphoreType.DMA((6,)),
+        pltpu.SemaphoreType.DMA((6,)),
+    ]
+
+
+def back_kernel(
+    fast,
+    ghl_ref, w_ref, att_ref, q_ref, qt_ref, k_ref, kt_ref, v_ref, band_t_ref,
+    ffn_ref, hidden_ref, grad_hidden_ref, tokens_ref, normed_ref, w_qkv_ref, gain_ref, gain_sum_ref,
+    outer_ref, inner_ref, collapse_ref,
+    *rest,
+):
+    outs, scratch = rest[: 9 if fast else 6], rest[9 if fast else 6 :]
+    if fast:
+        mixed_ref, input_ref, o_qkv_ref, o_output_ref, o_inner_ref, o_outer_ref, o_gain_a_ref, o_gain_f_ref, o_tables_ref = outs
+    else:
+        mixed_ref, input_ref, o_qkv_ref, o_output_ref, o_sums_ref, o_gains_ref = outs
+    da_ref, dat_ref, s_ref, pt_ref, gt_ref, dqt_ref, dk_ref, dv_ref, bands_ref, pad_ref, grads_ref, wt_ref, sums_ref = scratch[:13]
+    comm = scratch[13:]
+    heads, rows, _ = k_ref.shape
+    blocks = rows // BLOCK
+    chunks = rows // CHUNK
+    pieces = CHUNK // BLOCK
+    model = w_ref.shape[1]
+    width = heads * 64
+    feed = Scatter(ffn_ref, *comm[0:5])
+    norm = Scatter(*comm[5:11])
+    comm = comm[11:]
+    if fast:
+        outer = Spread(outer_ref, *comm[0:5])
+        inner = Spread(inner_ref, *comm[5:10])
+        output = Spread(*comm[10:16])
+        qkv_refs = comm[16:22]
+        small = Total(*comm[22:28])
+
+        def qkv(h):
+            return Spread(*[ref.at[h] for ref in qkv_refs])
+
+    lanes = lax.broadcasted_iota(jnp.int32, (CHUNK, BLOCK), 1)
+    low = lanes < FAR
+    meet_all(fast)
+    for c in range(chunks):
+        feed.start(c)
+    if fast:
+        outer.start()
+        inner.start()
+    pad_ref[...] = jnp.zeros_like(pad_ref)
+    sums_ref[...] = jnp.zeros_like(sums_ref)
+
+    def own(c):
+        return pl.ds(pl.multiple_of(c * BLOCK, BLOCK), BLOCK)
+
+    def put(ref, first_row, value):
+        each = model // 8
+        for r in range(value.shape[0] // each):
+            j = first_row // each + r
+            ref[j % 2, j // 2] = value[r * each : (r + 1) * each].astype(bf16)
+
+    def prologue(c, carry):
+        at = pl.ds(pl.multiple_of(c * CHUNK, CHUNK), CHUNK)
+        pad_ref[:, :width] = dot_nt(ghl_ref[at, :], w_ref[...]).astype(bf16).astype(f32)
+        pad_ref[:, 256 : 256 + width] = att_ref[at, :].astype(f32)
+        for h in range(heads):
+            base = h // 2 * BLOCK
+            grad = pad_ref[:, base : base + BLOCK]
+            out = pad_ref[:, 256 + base : 256 + base + BLOCK]
+            if h % 2 == 1:
+                grad = pltpu.roll(grad, 64, 1)
+                out = pltpu.roll(out, 64, 1)
+            total = -jnp.sum(jnp.where(low, grad * out, 0.0), axis=1, keepdims=True)
+            high, middle, last = split3(total)
+            grad = jnp.where(
+                low,
+                grad,
+                jnp.where(
+                    lanes == FAR, high, jnp.where(lanes == FAR + 1, middle, jnp.where(lanes == FAR + 2, last, 0.0))
+                ),
+            )
+            da_ref[h, at, :] = grad.astype(bf16)
+            dat_ref[h, :, at] = grad.T.astype(bf16)
+        return carry
+
+    lax.fori_loop(0, chunks, prologue, 0)
+    pad_ref[:, 256:] = jnp.zeros_like(pad_ref[:, 256:])
+    for b in range(2):
+        cols = slice(b * (model // 2), (b + 1) * (model // 2))
+        grad_output = dot_tn(ghl_ref[:, cols], att_ref[...])
+        if fast:
+            padded = jnp.concatenate([grad_output, jnp.zeros((model // 2, 256 - width), f32)], axis=1)
+            put(output.part, b * (model // 2), padded)
+        else:
+            o_output_ref[cols, :] = grad_output
+    if fast:
+        output.start()
+    for k in range(3):
+        turned = w_qkv_ref[k].astype(f32).T.astype(bf16)
+        for h in range(heads):
+            wt_ref[h, k * 64 : (k + 1) * 64, :] = turned[h * 64 : (h + 1) * 64]
+    wt_ref[:, 192:, :] = jnp.zeros_like(wt_ref[:, 192:, :])
+
+    lines16 = lax.broadcasted_iota(jnp.int32, (16, rows), 0)
+    block16 = lax.broadcasted_iota(jnp.int32, (16, rows), 1) // BLOCK
+    start16 = jnp.clip(block16 - 1, 0, blocks - 3)
+    real = lines16 < blocks
+    plane_rows = lax.broadcasted_iota(jnp.int32, (BLOCK, BLOCK), 0)
+    plane_lanes = lax.broadcasted_iota(jnp.int32, (BLOCK, BLOCK), 1)
+    tall_low = lax.broadcasted_iota(jnp.int32, (rows, BLOCK), 1) < 64
+
+    def fold(value):
+        total = value[:, :BLOCK]
+        for b in range(1, value.shape[1] // BLOCK):
+            total = total + value[:, b * BLOCK : (b + 1) * BLOCK]
+        return jnp.sum(total, axis=0, keepdims=True)
+
+    def head(h, carry):
+        dk_ref[...] = jnp.zeros_like(dk_ref)
+        dv_ref[...] = jnp.zeros_like(dv_ref)
+        bands_ref[...] = jnp.zeros_like(bands_ref)
+
+        def chunk(c, carry):
+            at = pl.ds(pl.multiple_of(c * CHUNK, CHUNK), CHUNK)
+            places = [pl.ds(pl.multiple_of((p * chunks + c) * BLOCK, BLOCK), BLOCK) for p in range(pieces)]
+            bands = []
+            for p in range(pieces):
+                block = p * chunks + c
+                start = jnp.clip(block - 1, 0, blocks - 3)
+                keys = pl.ds(pl.multiple_of(start * BLOCK, BLOCK), BAND)
+                of = pl.ds(pl.multiple_of((start - block + 2) * BLOCK, BLOCK), BAND)
+                bands.append((keys, of))
+            s_ref[...] = dot(k_ref[h], qt_ref[h, c])
+            for p, (keys, of) in enumerate(bands):
+                s_ref[keys, p * BLOCK : (p + 1) * BLOCK] += band_t_ref[h, of, :]
+            probs = jnp.exp(s_ref[...])
+            pt_ref[...] = probs.astype(bf16)
+            gt_ref[...] = (probs * dot(v_ref[h], dat_ref[h, :, at])).astype(bf16)
+            dv_ref[...] += dot(pt_ref[...], da_ref[h, at, :])
+            dk_ref[...] += dot(gt_ref[...], jnp.concatenate([q_ref[h, place, BLOCK:] for place in places], axis=0))
+            dq = dot(kt_ref[h], gt_ref[...])
+            for p in range(pieces):
+                dqt_ref[:, places[p]] = dq[:, p * BLOCK : (p + 1) * BLOCK]
+            for p, (keys, of) in enumerate(bands):
+                bands_ref[of, :] += gt_ref[keys, p * BLOCK : (p + 1) * BLOCK].astype(f32)
+
+            for k in range(chunks):
+
+                @pl.when((h == 0) & (c == k))
+                def _(k=k):
+                    feed.middle(k)
+
+                @pl.when((h == 1) & (c == k))
+                def _(k=k):
+                    rows_of = slice(k * BLOCK, (k + 1) * BLOCK)
+                    mixed_ref[rows_of, :] = (hidden_ref[rows_of, :] + feed.finish(k)).astype(bf16)
+
+            if fast:
+
+                @pl.when((h == 1) & (c == 0))
+                def _():
+                    outer.middle()
+
+                @pl.when((h == 2) & (c == 0))
+                def _():
+                    inner.middle()
+
+                @pl.when((h == 2) & (c == 1))
+                def _():
+                    output.middle()
+                    qkv(0).middle()
+
+            return carry
+
+        lax.fori_loop(0, chunks, chunk, 0)
+
+        dq = dqt_ref[BLOCK:, :].T * 0.125
+        grads_ref[h, :, :BLOCK] = jnp.where(tall_low, dq, pltpu.roll(dk_ref[...], 64, 1)).astype(bf16)
+        grads_ref[h, :, BLOCK:] = jnp.where(tall_low, dv_ref[...], 0.0).astype(bf16)
+        for b in range(2):
+            cols = slice(b * (model // 2), (b + 1) * (model // 2))
+            grad_qkv = dot_tn(normed_ref[:, cols], grads_ref[h])
+            if fast:
+                put(qkv_refs[0].at[h], b * (model // 2), grad_qkv)
+            else:
+                o_qkv_ref[h, cols, :] = grad_qkv
+        if fast:
+            qkv(h).start()
+
+        band = roll_rows(bands_ref[...].T, False)
+        spread = dqt_ref[:BLOCK, :]
+        high = spread.astype(bf16)
+        last = (spread - high.astype(f32)).astype(bf16)
+        hot = k_ref[h, :, :BLOCK]
+        plane = (dot(high, hot) + dot(last, hot)).T
+        plane = jnp.where((plane_rows < CODES) == (plane_lanes < CODES), plane, 0.0)
+        plane = roll_rows(plane, False)
+        far = dqt_ref[BLOCK + FAR : BLOCK + FAR + 16, :]
+        line = jnp.concatenate(
+            [
+                jnp.sum(band, axis=0, keepdims=True),
+                jnp.sum(plane[:CODES], axis=0, keepdims=True),
+                jnp.sum(plane[CODES:], axis=0, keepdims=True),
+                fold(jnp.where(real & (lines16 < start16), far, 0.0)),
+                fold(jnp.where(real & (lines16 > start16 + 2), far, 0.0)),
+            ],
+            axis=1,
+        )
+        sums_ref[...] += jnp.where(lax.broadcasted_iota(jnp.int32, sums_ref.shape, 0) == h, line, 0.0)
+        return carry
+
+    lax.fori_loop(0, heads, head, 0)
+
+    sums_ref[4:5, :model] = gain_sum_ref[0:1, :]
+    gain = gain_ref[...].astype(f32)
+    gain_total = jnp.zeros((1, model), f32)
+    for c in range(chunks):
+        for m in range(pieces):
+            at = pl.ds((m * chunks + c) * BLOCK, BLOCK)
+            partial = dot(grads_ref[0, at, :], wt_ref[0])
+            for h in range(1, heads):
+                partial = partial + dot(grads_ref[h, at, :], wt_ref[h])
+            gain_total = gain_total + jnp.sum(partial * normed_ref[at, :].astype(f32), axis=0, keepdims=True)
+            norm.part[c, m % 2, m // 2] = partial.astype(bf16)
+        norm.start(c)
+    sums_ref[3:4, :model] = gain_total / gain
+    if fast:
+        small.value[0] = sums_ref[...]
+        small.start()
+        outer_sum = outer.finish()
+        o_outer_ref[...] = outer_sum.T
+    for c in range(chunks):
+        norm.middle(c)
+    if fast:
+        qkv(1).middle()
+        small.over_z()
+        o_inner_ref[...] = inner.finish()
+        qkv(2).middle()
+        o_output_ref[...] = output.finish()[:, :width].T
+        small.over_core()
+    for c in range(chunks):
+        x = tokens_ref[own(c), :].astype(f32)
+        grad_normed = norm.finish(c)
+        factor = factor_of(x)
+        hat = x * factor
+        scaled = grad_normed * gain
+        back = factor * (scaled - hat * jnp.mean(scaled * hat, axis=-1, keepdims=True))
+        input_ref[own(c), :] = grad_hidden_ref[own(c), :] + back
+        if fast and c == 0:
+            small.over_y()
+    if fast:
+        each = model // 8
+        low_each = lax.broadcasted_iota(jnp.int32, (each, BLOCK), 1) < 64
+        parts = [qkv(h).finish() for h in range(heads)]
+        for k in range(3):
+            for h in range(0, heads, 2):
+                at = slice(0, BLOCK) if k < 2 else slice(BLOCK, 2 * BLOCK)
+                one = parts[h][:, at]
+                one = pltpu.roll(one, 64, 1) if k == 1 else one
+                if h + 1 < heads:
+                    two = parts[h + 1][:, at]
+                    two = two if k == 1 else pltpu.roll(two, 64, 1)
+                    o_qkv_ref[k, :, h * 64 : (h + 2) * 64] = jnp.where(low_each, one, two)
+                else:
+                    o_qkv_ref[k, :, h * 64 :] = one[:, :64]
+        totals = small.finish()
+        o_gain_a_ref[...] = totals[3:4, :model]
+        o_gain_f_ref[...] = totals[4:5, :model]
+        high, middle, last = split3(small.value[2])
+        tables = sum(dot_nt(collapse_ref[...], part.astype(bf16)) for part in (high, middle, last))
+        o_tables_ref[...] = tables[:, :heads]
+        outer.drain()
+        inner.drain()
+        output.drain()
+        for h in range(heads):
+            qkv(h).drain()
+        small.drain()
+    else:
+        o_sums_ref[...] = sums_ref[...]
+        o_gains_ref[...] = sums_ref[...]
+    for c in range(chunks):
+        feed.drain(c)
+        norm.drain(c)
+
+
+def back_call(fast, *args):
+    ghl, w_output, att, q = args[:4]
+    heads, rows, _ = q.shape
+    width, model = w_output.shape
+    share = args[10].shape[0]
+    chunks = rows // CHUNK
+    each = model // 8
+    full = pl.BlockSpec(memory_space=pltpu.VMEM)
+    sums = (8, WIDE + 4 * BLOCK)
+    outs = [((share, model), bf16), ((share, model), f32)]
+    if fast:
+        hidden_units = args[17].shape[-1]
+        outs += [
+            ((3, each, width), f32), ((width, each), f32), ((each, hidden_units), f32), ((hidden_units, each), f32),
+            ((1, model), f32), ((1, model), f32), ((3 * BUCKETS, heads), f32),
+        ]
+    else:
+        outs += [((heads, model, 256), f32), ((model, width), f32), (sums, f32), (sums, f32)]
+    scratch = [
+        pltpu.VMEM((heads, rows, BLOCK), bf16),
+        pltpu.VMEM((heads, BLOCK, rows), bf16),
+        pltpu.VMEM((rows, CHUNK), f32),
+        pltpu.VMEM((rows, CHUNK), bf16),
+        pltpu.VMEM((rows, CHUNK), bf16),
+        pltpu.VMEM((256, rows), f32),
+        pltpu.VMEM((rows, BLOCK), f32),
+        pltpu.VMEM((rows, BLOCK), f32),
+        pltpu.VMEM((WIDE, BLOCK), f32),
+        pltpu.VMEM((CHUNK, 512), f32),
+        pltpu.VMEM((heads, rows, 256), bf16),
+        pltpu.VMEM((heads, 256, model), bf16),
+        pltpu.VMEM(sums, f32),
+        *scatter_scratch(chunks, BLOCK, model)[1:],
+        *scatter_scratch(chunks, BLOCK, model),
+    ]
+    if fast:
+        scratch += [
+            *spread_scratch(each, hidden_units, part=False),
+            *spread_scratch(each, hidden_units, part=False),
+            *spread_scratch(each, 256),
+            *spread_scratch(each, 256, lead=(heads,)),
+            *total_scratch(*sums),
+        ]
+    return pl.pallas_call(
+        functools.partial(back_kernel, fast),
+        in_specs=[full] * len(args),
+        out_specs=[full] * len(outs),
+        out_shape=[jax.ShapeDtypeStruct(*out) for out in outs],
+        scratch_shapes=scratch,
+        compiler_params=pltpu.CompilerParams(vmem_limit_bytes=63 * MIB, collective_id=2, has_side_effects=True),
+        name="backward",
+    )(*args)
 
 
 def local(
-    tokens, lengths, horizontal, vertical, gain_attn, w_qkv, bias_tables, w_output, gain_ffn, w_inner, w_outer, cotangent
+    fast,
+    tokens, lengths, horizontal, vertical, gain_attn, w_qkv, bias_tables, w_output, gain_ffn, w_inner, w_outer, cotangent,
 ):
     rows, model = tokens.shape
     heads = bias_tables.shape[1]
     width = w_qkv.shape[2]
     share = rows // lax.axis_size("mp")
     mp = lax.axis_index("mp")
-    gain_a = gain_attn.astype(f32)
     codes = jnp.stack([horizontal, vertical])
     normed_a, q, k, kt, v, band, band_t = prep(tokens, lengths, codes, gain_attn, w_qkv, bias_tables)
     token_share = lax.dynamic_slice_in_dim(tokens, mp * share, share, 0)
-    qt, att, hidden, partial_ffn, grad_hidden, ghl, grad_outer, grad_inner, gain_sums = main_call(
-        q, kt, v, band, w_output, token_share, gain_ffn, w_inner, w_outer, cotangent
+    qt, att, hidden, ffn, grad_hidden, ghl, grad_outer, grad_inner, gain_sums = main_call(
+        fast, q, kt, v, band, w_output, token_share, gain_ffn, w_inner, w_outer, cotangent
     )
-    att = att.reshape(rows, width)
-    ghl = ghl.reshape(rows, model)
-
-    def scatter(x):
-        return lax.psum_scatter(x, "mp", scatter_dimension=0, tiled=True).astype(f32)
-
-    tokens_share = token_share.astype(f32)
-    gain_f_grad = gain_sums[0]
-    mixed = (hidden + scatter(partial_ffn)).astype(bf16)
-    grad_output = lax.dot_general(att, ghl, (((0,), (0,)), ((), ())), preferred_element_type=f32)
-    grads, sums = attend_back(ghl, w_output, att, q, qt, k, kt, v, band_t)
-    grad_qkv = lax.dot_general(normed_a, grads, (((0,), (1,)), ((), ())), preferred_element_type=f32)
-    grad_qkv = jnp.transpose(grad_qkv, (1, 0, 2))
-    partial_a = (dot_nt(grads[0], w_qkv[0]) + dot_nt(grads[1], w_qkv[1]) + dot_nt(grads[2], w_qkv[2])).astype(bf16)
-    back_a, gain_a_grad = norm_back(tokens_share, scatter(partial_a), gain_a)
-    input_grad = grad_hidden + back_a
+    outs = back_call(
+        fast, ghl.reshape(rows, model), w_output, att.reshape(rows, width), q, qt, k, kt, v, band_t, ffn, hidden,
+        grad_hidden, token_share, normed_a, w_qkv, gain_attn.reshape(1, model), gain_sums, grad_outer, grad_inner,
+        jnp.asarray(collapse().T, bf16),
+    )
+    if fast:
+        mixed, input_grad, qkv, output, inner, outer, gain_a, gain_f, tables = outs
+        return mixed, input_grad, qkv, output, inner, outer, gain_a[0], gain_f[0], tables
+    mixed, input_grad, qkv, output, sums, _ = outs
+    qkv = qkv[:, :, : 3 * 64].reshape(heads, model, 3, 64).transpose(2, 1, 0, 3).reshape(3, model, width)
+    gains = lax.psum(sums[3:5, :model], ("dp", "mp"))
+    totals = lax.psum(sums[:heads], "dp")
     tables = lax.dot_general(
-        jnp.asarray(collapse(), f32), sums[:heads], (((0,), (1,)), ((), ())), precision=lax.Precision.HIGHEST
+        jnp.asarray(collapse(), f32), totals, (((0,), (1,)), ((), ())), precision=lax.Precision.HIGHEST
     )
-    gains = lax.psum(jnp.stack([gain_a_grad, gain_f_grad]), ("dp", "mp"))
-    tables = lax.psum(tables, "dp")
 
     def spread(x, axis):
         return lax.psum_scatter(x, "dp", scatter_dimension=axis, tiled=True)
 
     return (
-        mixed,
-        input_grad,
-        spread(grad_qkv, 1),
-        spread(grad_output, 1),
-        spread(grad_inner, 0),
-        spread(grad_outer, 1),
-        gains[0],
-        gains[1],
-        tables,
+        mixed, input_grad, spread(qkv, 1), spread(output.T, 1), spread(grad_inner, 0), spread(grad_outer.T, 1),
+        gains[0], gains[1], tables,
     )
 
 
 def solution(mesh):
+    fast = mesh.shape["dp"] == 8
     return jax.shard_map(
-        local,
+        functools.partial(local, fast),
         mesh=mesh,
         in_specs=(
             P("dp", None), P("dp"), P("dp"), P("dp"), P(), P(None, None, "mp"), P(None, "mp"), P("mp", None), P(),

time: 479 us -> 208 us (0.43)
  waiting for transfers between devices: 210 us -> 0 us
  blocking collectives: 61.9 us -> 0 us
  Pallas kernels: 135 us -> 179 us
  between operations: 15 us -> 1.47 us
  matrix products: 13.5 us -> 0 us
  local copies, waits for them, and re-layouts: 31.7 us -> 24.2 us
  other arithmetic: 9.59 us -> 2.57 us
    unnamed x9 -> x0, waiting for transfers between devices: 117 us -> none
    reduce_scatter x3 -> x0, waiting for transfers between devices: 93.3 us -> none  [the longest x1 60.7 us: spread(): return lax.psum_scatter(x, 'dp', scatter_dimension=axis, tiled=True)]
    psum x2 -> x0, blocking collectives: 61.9 us -> none  [the longest x1 39.6 us: local(): gains = lax.psum(jnp.stack([gain_a_grad, gain_f_grad]), ('dp', 'mp'))]
    pallas_call x2, Pallas kernels: 124 us -> 167 us  [the longest x1 84.8 us: main_call(): pl.pallas_call(functools.partial(main_kernel, fast), in_specs=[full] * 10...]
    unnamed x2 -> x0, matrix products: 8.16 us -> none
    unnamed x53 -> x38, local copies, waits for them, and re-layouts: 24.2 us -> 18.2 us
    dot_general x4 -> x0, matrix products: 5.36 us -> none  [the longest x3 4.91 us: dot_nt(): lax.dot_general(a, b, (((1,), (1,)), ((), ())), preferred_element_type=f32)]
  transfers between devices with their start and end apart: 6 -> 0, of which waited for: 4 -> 0; matrix products, arithmetic and copies ran while one was open for 7% -> 0% of each run, Pallas kernels for 8% -> 0%
where the time goes in v3:
time: 208 us; the launch traced here: 207 us
  Pallas kernels  179 us (86%)
  local copies, waits for them, and re-layouts  24.2 us (12%)
  other arithmetic  2.57 us (1%)
    pallas_call x1, Pallas kernels, main_call(): pl.pallas_call(functools.partial(main_kernel, fast), in_specs=[full] * 10...  84.8 us
    pallas_call x1, Pallas kernels, back_call(): pl.pallas_call(functools.partial(back_kernel, fast), in_specs=[full] * le...  82 us
    unnamed x38, local copies, waits for them, and re-layouts  18.2 us
    pallas_call x1, Pallas kernels, prep(): pl.pallas_call(prep_kernel, grid=(rows // CHUNK,), in_specs=[pl.BlockSpec...  12.2 us

profile of v3, /device:TPU:0, one launch (start us, length us, event | category | flops | bytes accessed | tf_op | source)
XLA Modules:
  0.0 207.1 jit_solution(2941640877734516261)
XLA Ops:
  0.6 0.0 copy-start.11
  1.4 0.7 pad.4.tables_ref
  2.1 0.7 reshape.31.gain_ref
  2.8 0.0 copy-start.9
  2.8 1.3 reshape.32.gain_ref
  4.0 0.7 stack.9
  4.7 0.7 stack.10
  5.4 1.9 constant_dynamic-slice_fusion.tokens_ref
  7.4 0.0 copy-done.11
  7.4 0.0 copy-start.8
  7.4 0.6 copy.23.w_ref.w_qkv_ref
  8.0 0.0 copy-done.9
  8.0 0.3 copy-done.8
  8.3 0.0 copy-start
  8.3 12.2 %prep.1 = (bf16[1536,768]{1,0:T(8,128)(2,1)S(1)}, bf16[3,1536,256]{2,1,0:T(8,128)(2,1)S(1)}, bf16[3,1536,256]{2,1,0:T(8,128)(2,1)S(1)}, bf16[3,256,1536]{2,1,0:T...) custom-call(s32[1]{0:T(128)S(6)} %copy.32.length_ref, ...), custom_call_target="tpu_custom_call" | custom-call | tf_op jit(solution)/shard_map/prep/pallas_call | solution.py:161
  20.5 0.0 copy-done
  20.5 0.0 copy-start.1
  20.5 1.4 copy-done.1
  21.9 0.0 copy-start.2
  21.9 1.4 copy-done.2
  23.3 0.0 copy-start.3
  23.3 1.0 copy-done.3
  24.3 0.0 copy-start.4
  24.3 1.5 copy-done.4
  25.8 0.0 copy-start.5
  25.8 1.4 copy-done.5
  27.2 0.0 copy-start.6
  27.2 1.0 copy-done.6
  28.2 0.0 copy-start.7
  28.2 1.0 copy-done.7
  29.3 84.8 %forward_and_feed.1 = (bf16[3,3,256,512]{3,2,1,0:T(8,128)(2,1)}, bf16[3,512,192]{2,1,0:T(8,128)(2,1)}, f32[384,768]{1,0:T(8,128)}, bf16[3,2,2,128,768]{4,3,2,1,0...) custom-call(bf16[3,1536,256]{2,1,0:T(8,128)(2,1)} %copy-done.1, ...), custom_call_target="tpu_custom_call" | custom-call | tf_op jit(solution)/shard_map/forward_and_feed/pallas_call | solution.py:538
  114.0 82.0 %backward.1 = (bf16[384,768]{1,0:T(8,128)(2,1)}, f32[384,768]{1,0:T(8,128)}, f32[3,96,192]{2,1,0:T(8,128)}, f32[192,96]{1,0:T(8,128)}, f32[96,768]{1,0:T(8,128)}...) custom-call(bf16[1536,768]{1,0:T(8,128)(2,1)} %bitcast.3, ...), custom_call_target="tpu_custom_call" | custom-call | tf_op jit(solution)/shard_map/backward/pallas_call | solution.py:1028
  196.0 0.0 copy-start.10
  196.0 1.5 copy.26
  197.6 1.3 reduce
  198.9 1.3 reduce.1
  200.2 1.9 copy.25
  202.0 1.9 copy.33
  203.9 0.0 copy-done.10
  203.9 0.0 copy-start.13
  203.9 0.0 copy-start.14
  203.9 1.0 copy.34
  205.0 0.1 copy-done.13
  205.0 0.7 copy.35
  205.8 0.0 copy-done.14
  205.8 0.6 copy.36
  206.4 0.0 copy-done.12
  206.4 0.7 copy.37
  (2 shorter events, 0.0 us)
Async XLA Ops:
  0.6 6.7 %copy-start.11 = (bf16[3,768,192]{1,2,0:T(8,128)(2,1)S(1)}, bf16[3,768,192]{1,2,0:T(8,128)(2,1)}, u32[]{:S(2)}) copy-start(bf16[3,768,192]{1,2,0:T(8,128)(2,1)} %param.19) | copy-start | bytes 2654212
  2.8 5.2 %copy-start.9 = (bf16[1,768]{1,0:T(2,128)(2,1)}, bf16[1,768]{1,0:T(2,128)(2,1)S(1)}, u32[]{:S(2)}) copy-start(bf16[1,768]{1,0:T(2,128)(2,1)S(1)} %reshape.31.gain_ref) | copy-start | bytes 4612
  7.4 0.9 copy-start.8
  8.3 12.2 %copy-start = (bf16[3,768,192]{2,1,0:T(8,128)(2,1)}, bf16[3,768,192]{2,1,0:T(8,128)(2,1)S(1)}, u32[]{:S(2)}) copy-start(bf16[3,768,192]{2,1,0:T(8,128)(2,1)S(1)} %copy.23.w_ref.w_qkv_ref) | copy-start | bytes 2654212
  20.5 1.4 copy-start.1
  21.9 1.4 copy-start.2
  23.3 1.0 copy-start.3
  24.3 1.5 copy-start.4
  25.8 1.4 copy-start.5
  27.2 1.0 copy-start.6
  28.2 1.0 copy-start.7
  196.0 7.9 %copy-start.10 = (f32[384,768]{1,0:T(8,128)S(1)}, f32[384,768]{1,0:T(8,128)}, u32[]{:S(2)}) copy-start(f32[384,768]{1,0:T(8,128)} %get-tuple-element.78) | copy-start | bytes 3538948
  203.9 1.1 copy-start.13
  203.9 1.8 copy-start.14
  203.9 2.5 %copy-start.12 = (f32[96,768]{1,0:T(8,128)S(1)}, f32[96,768]{1,0:T(8,128)}, u32[]{:S(2)}) copy-start(f32[96,768]{1,0:T(8,128)} %get-tuple-element.81) | copy-start | bytes 884740

commit v4 on v1

v4 whole, which is shorter than its diff:
```python
import functools
import jax
import jax.numpy as jnp
import numpy as np
from jax import lax
from jax.experimental import pallas as pl
from jax.experimental.pallas import tpu as pltpu
from jax.sharding import PartitionSpec as P

BUCKETS = 32
CODES = 64
HALF = BUCKETS // 2
EPSILON = 1e-06
DEAD = -1e9
CHUNK = 512
BLOCK = 128
BAND = 3 * BLOCK
WIDE = 6 * BLOCK
FAR = 64
MASK = 76
LSE = 80
MIB = 2**20

f32 = jnp.float32
bf16 = jnp.bfloat16


def expansion():
    offsets = np.arange(WIDE) - 2 * BLOCK
    line = np.clip(offsets, -HALF, HALF - 1) + HALF
    line[5 * BLOCK :] = 0
    wrapped = np.arange(BLOCK)
    wrapped = np.where(wrapped < CODES, wrapped, wrapped - BLOCK)
    plane = np.clip(wrapped, -HALF, HALF - 1) + HALF
    buckets = np.concatenate([line, BUCKETS + plane, 2 * BUCKETS + plane])
    return (np.arange(3 * BUCKETS)[:, None] == buckets[None, :]).astype(np.float32)


def collapse():
    buckets = np.argmax(expansion(), axis=0)
    buckets[5 * BLOCK + 1 : WIDE] = 0
    buckets = np.concatenate([buckets, np.zeros(BLOCK, int), np.full(BLOCK, BUCKETS - 1)])
    return (buckets[:, None] == np.arange(3 * BUCKETS)[None, :]).astype(np.float32)


def roll_rows(value, right):
    rows, width = value.shape
    index = lax.broadcasted_iota(jnp.int32, value.shape, 0)
    step = 1
    while step < rows:
        shift = step if right else width - step
        value = jnp.where((index // step) % 2 == 1, pltpu.roll(value, shift, 1), value)
        step *= 2
    return value


def dot(a, b):
    return jnp.dot(a, b, preferred_element_type=f32)


def dot_nt(a, b):
    return lax.dot_general(a, b, (((1,), (1,)), ((), ())), preferred_element_type=f32)


def split3(value):
    high = value.astype(bf16).astype(f32)
    rest = value - high
    middle = rest.astype(bf16).astype(f32)
    return high, middle, rest - middle


def dot_tn(a, b):
    return lax.dot_general(a, b, (((0,), (0,)), ((), ())), preferred_element_type=f32)


ROOT = float(np.sqrt(2.0 / np.pi))
CUBE = 0.044715


def factor_of(rows):
    return lax.rsqrt(jnp.mean(rows * rows, axis=-1, keepdims=True) + EPSILON)


def mp_places():
    mp = lax.axis_index("mp")
    y, core = mp // 2, mp % 2
    return mp, y, core, y * 2 + (1 - core), (1 - y) * 2 + core


def dp_places():
    dp = lax.axis_index("dp")
    return dp // 2, dp % 2


def remote(src, dst, send, recv, mp=None, dp=None):
    return pltpu.make_async_remote_copy(
        src_ref=src,
        dst_ref=dst,
        send_sem=send,
        recv_sem=recv,
        device_id=(lax.axis_index("dp") if dp is None else dp, lax.axis_index("mp") if mp is None else mp),
        device_id_type=pl.DeviceIdType.MESH,
    )


def meet(fast):
    mp, dp = lax.axis_index("mp"), lax.axis_index("dp")
    z, x = dp_places()
    others = [(dp, (mp + d) % 4) for d in (1, 2, 3)]
    if fast:
        others.append((z * 2 + 1 - x, mp))
        others.extend(((z + d) % 4 * 2 + x, mp) for d in (1, 2, 3))
    barrier = pltpu.get_barrier_semaphore()
    for other in others:
        pl.semaphore_signal(barrier, inc=1, device_id=other, device_id_type=pl.DeviceIdType.MESH)
    pl.semaphore_wait(barrier, len(others))


def run(index, count=1, size=BLOCK):
    return pl.ds(pl.multiple_of(index * size, size), count * size)


class Scatter:

    def __init__(self, part, near, far, send, recv):
        self.part, self.near, self.far, self.send, self.recv = part, near, far, send, recv

    def block(self, c, core, y):
        return (c * 2 + core) * 2 + y

    def put(self, c, m, value):
        self.part[run(self.block(c, m % 2, m // 2)), :] = value.astype(bf16)

    def first(self, c):
        _, _, core, sibling, _ = mp_places()
        src = self.part.at[run(self.block(c, 1 - core, 0), 2)]
        return remote(src, self.near.at[run(c * 2, 2)], self.send.at[c, 0], self.recv.at[c, 0], sibling)

    def second(self, c):
        _, y, core, _, across = mp_places()
        src = self.part.at[run(self.block(c, core, 1 - y))]
        return remote(src, self.far.at[run(c)], self.send.at[c, 1], self.recv.at[c, 1], across)

    def start(self, c):
        self.first(c).start()

    def middle(self, c):
        _, y, core, _, _ = mp_places()
        self.first(c).wait_recv()
        at = run(self.block(c, core, 1 - y))
        self.part[at, :] = (self.part[at, :].astype(f32) + self.near[run(c * 2 + 1 - y), :].astype(f32)).astype(bf16)
        self.second(c).start()

    def finish(self, c):
        _, y, core, _, _ = mp_places()
        self.second(c).wait_recv()
        own = self.part[run(self.block(c, core, y)), :].astype(f32) + self.near[run(c * 2 + y), :].astype(f32)
        return own + self.far[run(c), :].astype(f32)

    def drain(self, c):
        self.first(c).wait_send()
        self.second(c).wait_send()


class Gather:

    def __init__(self, full, send, recv, size=BLOCK):
        self.full, self.send, self.recv, self.size = full, send, recv, size

    def at(self, c, m):
        return run(c * 4 + m, 1, self.size)

    def copy(self, c, kind):
        mp, _, _, sibling, across = mp_places()
        at = self.full.at[self.at(c, across if kind == 2 else mp)]
        return remote(at, at, self.send.at[c, kind], self.recv.at[c, kind], across if kind == 1 else sibling)

    def start(self, c):
        self.copy(c, 1).start()
        self.copy(c, 0).start()

    def forward(self, c):
        self.copy(c, 1).wait_recv()
        self.copy(c, 2).start()

    def finish(self, c):
        self.copy(c, 0).wait_recv()
        self.copy(c, 2).wait_recv()

    def drain(self, c):
        for kind in range(3):
            self.copy(c, kind).wait_send()


class Exchange:

    def __init__(self, given, at, taken, send, recv):
        self.given, self.at, self.taken, self.send, self.recv = given, at, taken, send, recv

    def copy(self, c, d):
        mp = lax.axis_index("mp")
        dst = self.taken.at[run(c * 4 + mp)]
        src = self.given.at[self.at(c, d)]
        return remote(src, dst, self.send.at[c, d - 1], self.recv.at[c, d - 1], (mp + d) % 4)

    def start(self, c):
        for d in (2, 1, 3):
            self.copy(c, d).start()

    def finish(self, c):
        for d in (1, 2, 3):
            self.copy(c, d).wait_recv()

    def drain(self, c):
        for d in (1, 2, 3):
            self.copy(c, d).wait_send()


class Spread:

    def __init__(self, part, near, far, send, recv):
        self.part, self.near, self.far, self.send, self.recv = part, near, far, send, recv
        self.each = part.shape[0] // 8

    def at(self, index, count=1):
        return run(index, count, self.each)

    def put(self, first_row, value):
        for r in range(value.shape[0] // self.each):
            j = first_row // self.each + r
            rows = value[r * self.each : (r + 1) * self.each]
            self.part[self.at(j % 2 * 4 + j // 2), :] = rows.astype(bf16)

    def first(self):
        z, x = dp_places()
        src = self.part.at[self.at((1 - x) * 4, 4)]
        return remote(src, self.near, self.send.at[0], self.recv.at[0], dp=z * 2 + 1 - x)

    def second(self, d):
        z, x = dp_places()
        to = (z + d) % 4
        src = self.part.at[self.at(x * 4 + to)]
        return remote(src, self.far.at[self.at(d - 1)], self.send.at[d], self.recv.at[d], dp=to * 2 + x)

    def start(self):
        self.first().start()

    def middle(self):
        z, x = dp_places()
        self.first().wait_recv()
        for d in range(1, 4):
            to = (z + d) % 4
            at = self.at(x * 4 + to)
            self.part[at, :] = (self.part[at, :].astype(f32) + self.near[self.at(to), :].astype(f32)).astype(bf16)
            self.second(d).start()

    def finish(self):
        z, x = dp_places()
        total = self.part[self.at(x * 4 + z), :].astype(f32) + self.near[self.at(z), :].astype(f32)
        for d in range(1, 4):
            self.second(d).wait_recv()
            total = total + self.far[self.at(d - 1), :].astype(f32)
        return total

    def drain(self):
        self.first().wait_send()
        for d in range(1, 4):
            self.second(d).wait_send()


class Total:

    def __init__(self, value, near, far, across, send, recv):
        self.value, self.near, self.far, self.across, self.send, self.recv = value, near, far, across, send, recv

    def copy(self, kind):
        z, x = dp_places()
        mp, _, _, sibling, across = mp_places()
        send, recv = self.send.at[kind], self.recv.at[kind]
        if kind == 0:
            return remote(self.value.at[0], self.near, send, recv, dp=z * 2 + 1 - x)
        if kind < 4:
            return remote(self.value.at[1], self.far.at[kind - 1], send, recv, dp=(z + kind) % 4 * 2 + x)
        if kind == 4:
            return remote(self.value.at[2], self.across.at[0], send, recv, sibling)
        return remote(self.value.at[3], self.across.at[1], send, recv, across)

    def start(self):
        self.copy(0).start()

    def over_z(self):
        self.copy(0).wait_recv()
        self.value[1] = self.value[0] + self.near[...]
        for kind in range(1, 4):
            self.copy(kind).start()

    def over_core(self):
        total = self.value[1]
        for kind in range(1, 4):
            self.copy(kind).wait_recv()
            total = total + self.far[kind - 1]
        self.value[2] = total
        self.copy(4).start()

    def over_y(self):
        self.copy(4).wait_recv()
        self.value[3] = self.value[2] + self.across[0]
        self.copy(5).start()

    def finish(self):
        self.copy(5).wait_recv()
        return self.value[3] + self.across[1]

    def drain(self):
        for kind in range(6):
            self.copy(kind).wait_send()


def layer_kernel(
    fast,
    length_ref, across_ref, upward_ref, gain_a_ref, gain_f_ref, tables_ref, expand_ref, collapse_ref,
    tokens_hbm, w_qkv_hbm, w_output_hbm, w_inner_hbm, w_outer_hbm, cot_hbm,
    *rest,
):
    outs, scratch = rest[: 9 if fast else 7], rest[9 if fast else 7 :]
    if fast:
        mixed_ref, input_ref, o_qkv_ref, o_output_ref, o_inner_ref, o_outer_ref, o_gain_a_ref, o_gain_f_ref, o_tables_ref = outs
    else:
        mixed_ref, input_ref, o_qkv_ref, o_output_ref, o_inner_ref, o_outer_ref, o_sums_ref = outs
    (
        x1, share_ref, w_qkv_ref, w_inner_ref, w_outer_ref, cot_ref, load_sem,
        plane_ref, hot_ref, hot_t_ref, qa_ref, qb_ref, k2_ref, kt2_ref, v_ref, band_ref, band_t_ref, qt_ref,
        s_ref, res_ref, dv_ref, dqt_ref, bands_ref, dat_ref, sums_ref, gain_sum_ref,
        att_ref, ax_ref, att_send, att_recv,
        es_ref, ga_ref, es_send, es_recv,
        wo_ref, wo_send, wo_recv,
        nf_ref, nf_send, nf_recv,
        ghl_ref, ghl_send, ghl_recv,
        feed_part, feed_near, feed_far, feed_send, feed_recv,
        norm_part, norm_near, norm_far, norm_send, norm_recv,
        last_send, last_recv,
        low_ref, grad_low_ref, hidden_ref,
        *spreads,
    ) = scratch
    heads = tables_ref.shape[0]
    rows, model = x1.shape
    width = heads * 64
    units = w_inner_ref.shape[1]
    pieces = 4
    chunks = rows // CHUNK
    blocks = rows // BLOCK
    half_model = model // 2
    mp = lax.axis_index("mp")
    da_ref, dk_ref, wt_ref = qa_ref, res_ref, w_inner_ref

    att = Exchange(att_ref, lambda c, d: run(c * 4 + (mp + d) % 4), ax_ref, att_send, att_recv)
    grad_att = Exchange(es_ref, lambda c, d: run(c * 3 + d - 1), ga_ref, es_send, es_recv)
    wo = Gather(wo_ref, wo_send, wo_recv, width)
    normed = Gather(nf_ref, nf_send, nf_recv)
    grads = Gather(ghl_ref, ghl_send, ghl_recv)
    feed = Scatter(feed_part, feed_near, feed_far, feed_send, feed_recv)
    norm = Scatter(norm_part, norm_near, norm_far, norm_send, norm_recv)
    last = Scatter(norm_part, norm_near, norm_far, last_send, last_recv)
    if fast:
        outer = Spread(w_outer_ref, *spreads[0:4])
        inner = Spread(*spreads[4:9])
        output = Spread(*spreads[9:14])
        small = Total(*spreads[19:25])

        def qkv(h):
            return Spread(*[ref.at[h] for ref in spreads[14:19]])

    loads = [
        pltpu.make_async_copy(src, dst, load_sem.at[i])
        for i, (src, dst) in enumerate(
            [
                (tokens_hbm, x1),
                (w_qkv_hbm, w_qkv_ref),
                (w_output_hbm, wo_ref.at[wo.at(0, mp)]),
                (tokens_hbm.at[run(mp * chunks, chunks)], share_ref),
                (w_inner_hbm, w_inner_ref),
                (w_outer_hbm, w_outer_ref),
                (cot_hbm, cot_ref),
            ]
        )
    ]
    for load in loads:
        load.start()
    meet(fast)

    def place(m, c):
        return run(m * chunks + c)

    def window(m, c):
        block = m * chunks + c
        start = jnp.clip(block - 1, 0, blocks - 3)
        return start, start - block + 2


    expanded = dot(tables_ref[...], expand_ref[...])
    square_rows = lax.broadcasted_iota(jnp.int32, (BLOCK, BLOCK), 0)
    square_lanes = lax.broadcasted_iota(jnp.int32, (BLOCK, BLOCK), 1)
    for h in range(heads):
        line = jnp.broadcast_to(expanded[h : h + 1, :WIDE], (BLOCK, WIDE))
        band = roll_rows(line, True)
        band_ref[h] = band.astype(bf16)
        band_t_ref[h] = band.T.astype(bf16)
        across = roll_rows(jnp.broadcast_to(expanded[h : h + 1, WIDE : WIDE + BLOCK], (BLOCK, BLOCK)), True)
        upward = roll_rows(jnp.broadcast_to(expanded[h : h + 1, WIDE + BLOCK :], (BLOCK, BLOCK)), True)
        plane = jnp.where(
            (square_rows < CODES) & (square_lanes < CODES),
            across,
            jnp.where((square_rows >= CODES) & (square_lanes >= CODES), upward, 0.0),
        )
        plane_ref[h] = plane.astype(bf16)
    loads[2].wait()
    wo.start(0)
    loads[1].wait()
    loads[0].wait()
    gain_a = gain_a_ref[...].astype(f32)
    gain_f = gain_f_ref[...].astype(f32)
    lanes = lax.broadcasted_iota(jnp.int32, (CHUNK, BLOCK), 1)
    low = lanes < FAR

    def prepare(j, carry):
        at = run(j, 1, CHUNK)
        x = x1[at, :].astype(f32)
        normed_rows = (x * factor_of(x) * gain_a).astype(bf16)
        x1[at, :] = normed_rows
        codes_lines = lax.broadcasted_iota(jnp.int32, (BLOCK, CHUNK), 0)
        hot_t = jnp.where(
            codes_lines == jnp.broadcast_to(across_ref[:, at], (BLOCK, CHUNK)),
            1.0,
            jnp.where(codes_lines - CODES == jnp.broadcast_to(upward_ref[:, at], (BLOCK, CHUNK)), 1.0, 0.0),
        )
        hot = hot_t.T.astype(bf16)
        hot_t_ref[:, at] = hot_t.astype(bf16)
        hot_ref[at, :] = hot
        row = lax.broadcasted_iota(jnp.int32, (CHUNK, BLOCK), 0) + j * CHUNK
        block = row // BLOCK
        start = jnp.clip(block - 1, 0, blocks - 3)
        far = (lanes >= FAR) & (lanes < MASK)
        far_left = far & (lanes - FAR < start)
        far_right = far & (lanes - FAR > start + 2)
        key_side = jnp.where(
            (far & (lanes - FAR == block))
            | ((lanes == MASK) & (row >= length_ref[0]))
            | ((lanes >= LSE) & (lanes < LSE + 3)),
            1.0,
            0.0,
        )

        def part(h):
            columns = s_ref[:CHUNK, h // 2 * BLOCK : h // 2 * BLOCK + BLOCK]
            return columns if h % 2 == 0 else pltpu.roll(columns, 64, 1)

        s_ref[:CHUNK, :width] = dot(normed_rows, w_qkv_ref[0])
        for h in range(heads):
            left = expanded[h : h + 1, 0:1]
            right = expanded[h : h + 1, WIDE - BLOCK - 1 : WIDE - BLOCK]
            query_side = jnp.where(far_left, left, jnp.where(far_right, right, jnp.where(lanes == MASK, DEAD, 0.0)))
            qa_ref[h, at, :] = dot(hot, plane_ref[h]).astype(bf16)
            qb_ref[h, at, :] = jnp.where(low, part(h).astype(bf16).astype(f32) * 0.125, query_side).astype(bf16)
        s_ref[:CHUNK, :width] = dot(normed_rows, w_qkv_ref[1])
        for h in range(heads):
            second = jnp.where(low, part(h), key_side)
            k2_ref[h, at, :] = second.astype(bf16)
            kt2_ref[h, :, at] = second.T.astype(bf16)
        s_ref[:CHUNK, :width] = dot(normed_rows, w_qkv_ref[2])
        for h in range(heads):
            v_ref[h, at, :] = jnp.where(low, part(h), 1.0).astype(bf16)
        return carry

    s_ref[:CHUNK, :] = jnp.zeros_like(s_ref[:CHUNK, :])
    lax.fori_loop(0, chunks, prepare, 0)
    wo.forward(0)
    loads[3].wait()
    gain_sum_ref[...] = jnp.zeros_like(gain_sum_ref)
    sums_ref[...] = jnp.zeros_like(sums_ref)

    def hidden_of(c):
        att.finish(c)
        hidden = share_ref[run(c), :].astype(f32)
        for m in range(pieces):
            hidden = hidden + dot(ax_ref[run(c * 4 + m), :width], wo_ref[m * width : (m + 1) * width, :])
        hidden_ref[run(c), :] = hidden
        nf_ref[normed.at(c, mp), :] = (hidden * factor_of(hidden) * gain_f).astype(bf16)
        normed.start(c)

    def grad_of(c):
        grad_normed = norm.finish(c)
        hidden = hidden_ref[run(c), :]
        factor = factor_of(hidden)
        hat = hidden * factor
        scaled = grad_normed * gain_f
        back = factor * (scaled - hat * jnp.mean(scaled * hat, axis=-1, keepdims=True))
        grad = cot_ref[place(mp, c), :].astype(f32) + back
        input_ref[run(c), :] = grad
        gain_sum_ref[0:1, :] += jnp.sum(grad_normed * hat, axis=0, keepdims=True)
        grad_low = grad.astype(bf16)
        ghl_ref[grads.at(c, mp), :] = grad_low

        def of(m):
            value = dot_nt(grad_low, wo_ref[run(m, 1, width), :])
            return jnp.concatenate([value, jnp.zeros((BLOCK, 256 - width), f32)], axis=1).astype(bf16)

        ga_ref[run(c * 4 + mp), :] = of(mp)
        for d in (1, 2, 3):
            es_ref[run(c * 3 + d - 1), :] = of((mp + d) % 4)
        grad_att.start(c)
        grads.start(c)

    def attend(t, carry):
        c = t // heads
        h = t % heads
        query_far = jnp.concatenate([qa_ref[h, place(m, c), :] for m in range(pieces)], axis=0)
        query_near = jnp.concatenate([qb_ref[h, place(m, c), :] for m in range(pieces)], axis=0)
        query = jnp.concatenate([query_far, query_near], axis=1)
        for j in range(chunks):
            cols = slice(j * CHUNK, (j + 1) * CHUNK)
            s_ref[cols, :] = dot(query, jnp.concatenate([hot_t_ref[:, cols], kt2_ref[h, :, cols]], axis=0))
        for m in range(pieces):
            start, of = window(m, c)
            for i in range(3):
                panel = (start + i) // pieces
                s_ref[run(panel * 4 + m), run((start + i) % pieces)] += band_ref[h, :, run(of + i)].astype(f32)
        panels = [s_ref[j * CHUNK : (j + 1) * CHUNK, :] for j in range(chunks)]
        top = jnp.max(functools.reduce(jnp.maximum, panels), axis=1, keepdims=True)
        mixed = jnp.zeros((CHUNK, BLOCK), f32)
        for j in range(chunks):
            weights = jnp.exp(panels[j] - top).astype(bf16)
            mixed = mixed + dot(weights, v_ref[h, j * CHUNK : (j + 1) * CHUNK, :])
        res_ref[run(h, 1, CHUNK), :] = jnp.where(low, mixed / pltpu.roll(mixed, 64, 1), 0.0)
        high, middle, rest = split3(-(top + jnp.log(mixed[:, 64:65])))
        second = jnp.where(
            lanes == LSE,
            high,
            jnp.where(lanes == LSE + 1, middle, jnp.where(lanes == LSE + 2, rest, query_near.astype(f32))),
        )
        qt_ref[h, c, :BLOCK, :] = query_far.astype(f32).T.astype(bf16)
        qt_ref[h, c, BLOCK:, :] = second.T.astype(bf16)

        @pl.when(h == heads - 1)
        def _():
            pairs = []
            for g in range(0, heads, 2):
                pair = res_ref[g * CHUNK : (g + 1) * CHUNK, :]
                if g + 1 < heads:
                    pair = jnp.where(low, pair, pltpu.roll(res_ref[(g + 1) * CHUNK : (g + 2) * CHUNK, :], 64, 1))
                pairs.append(pair.astype(bf16))
            merged = jnp.concatenate(pairs, axis=1)
            att_ref[run(c, 1, CHUNK), :] = merged
            ax_ref[run(c * 4 + mp), :] = att_ref[run(c * 4 + mp), :]
            att.start(c)

        @pl.when(t == 4)
        def _():
            wo.finish(0)
            hidden_of(0)

        @pl.when(t == 6)
        def _():
            normed.forward(0)

        @pl.when(t == 7)
        def _():
            hidden_of(1)

        return carry

    lax.fori_loop(0, chunks * heads, attend, 0)
    for load in loads[4:]:
        load.wait()
    normed.finish(0)

    steps = units // 256

    def feed_step(t, carry):
        c = t // steps
        b = t % steps

        @pl.when((b == 0) & (c > 0))
        def _():
            normed.finish(c)

        at = run(b, 1, 256)
        x = nf_ref[run(c, 1, CHUNK), :]
        cot = jnp.concatenate([cot_ref[place(m, c), :] for m in range(pieces)], axis=0)
        inner_units = dot(x, w_inner_ref[:, at])
        grad_act = dot_nt(cot, w_outer_ref[at, :])
        square = inner_units * inner_units
        tanh = jnp.tanh(ROOT * inner_units * (1.0 + CUBE * square))
        half = 0.5 * (1.0 + tanh)
        slope = half + 0.5 * inner_units * (1.0 - tanh * tanh) * (ROOT + 3.0 * CUBE * ROOT * square)
        activated = (inner_units * half).astype(bf16)
        grad_low = (slope * grad_act).astype(bf16)
        low_ref[run(c, 1, CHUNK), at] = activated
        grad_low_ref[run(c, 1, CHUNK), at] = grad_low
        part_ffn = dot(activated, w_outer_ref[at, :])
        part_norm = dot_nt(grad_low, w_inner_ref[:, at])

        @pl.when(b == 0)
        def _():
            for p in range(chunks):
                s_ref[p * CHUNK : (p + 1) * CHUNK, :256] = part_ffn[:, p * 256 : (p + 1) * 256]
                s_ref[p * CHUNK : (p + 1) * CHUNK, 256:] = part_norm[:, p * 256 : (p + 1) * 256]

        @pl.when(b > 0)
        def _():
            for p in range(chunks):
                s_ref[p * CHUNK : (p + 1) * CHUNK, :256] += part_ffn[:, p * 256 : (p + 1) * 256]
                s_ref[p * CHUNK : (p + 1) * CHUNK, 256:] += part_norm[:, p * 256 : (p + 1) * 256]

        @pl.when(b == steps - 1)
        def _():
            for m in range(pieces):
                parts = [s_ref[p * CHUNK + m * BLOCK : p * CHUNK + (m + 1) * BLOCK, :] for p in range(chunks)]
                feed.put(c, m, jnp.concatenate([p[:, :256] for p in parts], axis=1))
                norm.put(c, m, jnp.concatenate([p[:, 256:] for p in parts], axis=1))
            norm.start(c)
            feed.start(c)

        @pl.when(t == 1)
        def _():
            normed.forward(1)

        @pl.when(t == 2)
        def _():
            hidden_of(2)

        @pl.when(t == 3)
        def _():
            norm.middle(0)

        @pl.when(t == 5)
        def _():
            normed.forward(2)

        @pl.when(t == 6)
        def _():
            norm.middle(1)

        @pl.when(t == 7)
        def _():
            grad_of(0)

        return carry

    lax.fori_loop(0, chunks * steps, feed_step, 0)

    def weights_of(is_outer):
        for b in range(2):
            at = slice(b * half_model, (b + 1) * half_model)
            total = jnp.zeros((half_model, units), f32)
            for c in range(chunks):
                if is_outer:
                    left = jnp.concatenate([cot_ref[place(m, c), at] for m in range(pieces)], axis=0)
                    total = total + dot_tn(left, low_ref[run(c, 1, CHUNK), :])
                else:
                    total = total + dot_tn(nf_ref[run(c, 1, CHUNK), at], grad_low_ref[run(c, 1, CHUNK), :])
            if fast:
                (outer if is_outer else inner).put(b * half_model, total)
            else:
                (o_outer_ref if is_outer else o_inner_ref)[at, :] = total

    weights_of(True)
    if fast:
        outer.start()
    norm.middle(2)
    grad_of(1)
    weights_of(False)
    for c in range(chunks):
        normed.drain(c)
    wt_ref[...] = jnp.zeros_like(wt_ref)
    for k in range(3):
        turned = w_qkv_ref[k].astype(f32).T.astype(bf16)
        for h in range(heads):
            wt_ref[h * 256 + k * 64 : h * 256 + (k + 1) * 64, :] = turned[h * 64 : (h + 1) * 64]

    def receive(c):
        grad_att.finish(c)
        at = run(c, 1, CHUNK)
        for h in range(heads):
            pair = slice(h // 2 * BLOCK, h // 2 * BLOCK + BLOCK)
            grad = ga_ref[at, pair].astype(f32)
            out = att_ref[at, pair].astype(f32)
            if h % 2 == 1:
                grad = pltpu.roll(grad, 64, 1)
                out = pltpu.roll(out, 64, 1)
            high, middle, rest = split3(-jnp.sum(jnp.where(low, grad * out, 0.0), axis=1, keepdims=True))
            grad = jnp.where(
                low,
                grad,
                jnp.where(
                    lanes == FAR, high, jnp.where(lanes == FAR + 1, middle, jnp.where(lanes == FAR + 2, rest, 0.0))
                ),
            )
            da_ref[h, at, :] = grad.astype(bf16)
            dat_ref[h, :, at] = grad.T.astype(bf16)

    lines16 = lax.broadcasted_iota(jnp.int32, (16, rows), 0)
    block16 = lax.broadcasted_iota(jnp.int32, (16, rows), 1) // BLOCK
    start16 = jnp.clip(block16 - 1, 0, blocks - 3)
    real = lines16 < blocks
    tall_low = lax.broadcasted_iota(jnp.int32, (rows, BLOCK), 1) < 64

    def fold(value):
        total = value[:, :BLOCK]
        for b in range(1, value.shape[1] // BLOCK):
            total = total + value[:, b * BLOCK : (b + 1) * BLOCK]
        return jnp.sum(total, axis=0, keepdims=True)

    def head(h, carry):
        dk_ref[...] = jnp.zeros_like(dk_ref)
        dv_ref[...] = jnp.zeros_like(dv_ref)
        bands_ref[...] = jnp.zeros_like(bands_ref)

        def chunk(c, carry):
            @pl.when(h == 0)
            def _():
                receive(c)

            at = run(c, 1, CHUNK)
            s_ref[...] = dot(jnp.concatenate([hot_ref[...], k2_ref[h]], axis=1), qt_ref[h, c])
            for m in range(pieces):
                start, of = window(m, c)
                s_ref[run(start, 3), m * BLOCK : (m + 1) * BLOCK] += band_t_ref[h, run(of, 3), :].astype(f32)
            probs = jnp.exp(s_ref[...])
            low_ref[:, :CHUNK] = probs.astype(bf16)
            grad_low_ref[:, :CHUNK] = (probs * dot(v_ref[h], dat_ref[h, :, at])).astype(bf16)
            probs_t = low_ref[:, :CHUNK]
            grad_t = grad_low_ref[:, :CHUNK]
            dv_ref[...] += dot(probs_t, da_ref[h, at, :])
            dk_ref[...] += dot(grad_t, jnp.concatenate([qb_ref[h, place(m, c), :] for m in range(pieces)], axis=0))
            dq_far = dot(hot_t_ref[...], grad_t)
            dq_near = dot(kt2_ref[h], grad_t)
            for m in range(pieces):
                dqt_ref[:BLOCK, place(m, c)] = dq_far[:, m * BLOCK : (m + 1) * BLOCK]
                dqt_ref[BLOCK:, place(m, c)] = dq_near[:, m * BLOCK : (m + 1) * BLOCK]
                start, of = window(m, c)
                bands_ref[run(of, 3), :] += grad_low_ref[run(start, 3), m * BLOCK : (m + 1) * BLOCK].astype(f32)

            def when(head_index, chunk_index):
                return pl.when((h == head_index) & (c == chunk_index))

            def mix(k):
                mixed_ref[run(k), :] = (hidden_ref[run(k), :] + feed.finish(k)).astype(bf16)

            @when(0, 0)
            def _():
                grad_of(2)

            @when(0, 1)
            def _():
                grads.forward(0)
                feed.middle(0)

            @when(0, 2)
            def _():
                grads.forward(1)
                feed.middle(1)

            @when(1, 0)
            def _():
                grads.forward(2)
                feed.middle(2)
                mix(0)
                if fast:
                    outer.middle()
                    inner.start()

            @when(1, 1)
            def _():
                mix(1)

            @when(1, 2)
            def _():
                mix(2)

            if fast:

                @when(2, 0)
                def _():
                    inner.middle()

                @when(2, 1)
                def _():
                    qkv(0).middle()

                @when(2, 2)
                def _():
                    output.middle()
                    qkv(1).middle()

            return carry

        lax.fori_loop(0, chunks, chunk, 0)

        dq = dqt_ref[BLOCK:, :].T * 0.125
        grads_of = run(h, 1, 256)
        nf_ref[:, grads_of] = jnp.concatenate(
            [jnp.where(tall_low, dq, pltpu.roll(dk_ref[...], 64, 1)), jnp.where(tall_low, dv_ref[...], 0.0)], axis=1
        ).astype(bf16)
        for b in range(2):
            cols = slice(b * half_model, (b + 1) * half_model)
            grad_qkv = dot_tn(x1[:, cols], nf_ref[:, grads_of])
            if fast:
                qkv(h).put(b * half_model, grad_qkv)
            else:
                o_qkv_ref[h, cols, :] = grad_qkv
        if fast:
            qkv(h).start()

        @pl.when(h == 1)
        def _():
            for c in range(chunks):
                grads.finish(c)
            for b in range(2):
                cols = slice(b * half_model, (b + 1) * half_model)
                grad_output = dot_tn(ghl_ref[:, cols], att_ref[...])
                if fast:
                    output.put(b * half_model, grad_output)
                else:
                    o_output_ref[cols, :] = grad_output[:, :width]
            if fast:
                output.start()

        band = roll_rows(bands_ref[...].T, False)
        spread = dqt_ref[:BLOCK, :]
        high = spread.astype(bf16)
        rest = (spread - high.astype(f32)).astype(bf16)
        plane = (dot(high, hot_ref[...]) + dot(rest, hot_ref[...])).T
        plane = jnp.where((square_rows < CODES) == (square_lanes < CODES), plane, 0.0)
        plane = roll_rows(plane, False)
        far = dqt_ref[BLOCK + FAR : BLOCK + FAR + 16, :]
        line = jnp.concatenate(
            [
                jnp.sum(band, axis=0, keepdims=True),
                jnp.sum(plane[:CODES], axis=0, keepdims=True),
                jnp.sum(plane[CODES:], axis=0, keepdims=True),
                fold(jnp.where(real & (lines16 < start16), far, 0.0)),
                fold(jnp.where(real & (lines16 > start16 + 2), far, 0.0)),
            ],
            axis=1,
        )
        sums_ref[...] += jnp.where(lax.broadcasted_iota(jnp.int32, sums_ref.shape, 0) == h, line, 0.0)
        return carry

    lax.fori_loop(0, heads, head, 0)

    for c in range(chunks):
        norm.drain(c)
    gain_total = jnp.zeros((1, model), f32)
    for c in range(chunks):
        for m in range(pieces):
            at = place(m, c)
            partial = dot(nf_ref[at, :], wt_ref[...])
            gain_total = gain_total + jnp.sum(partial * x1[at, :].astype(f32), axis=0, keepdims=True)
            last.put(c, m, partial)
        last.start(c)
    sums_ref[3:4, :model] = gain_total / gain_a
    sums_ref[4:5, :model] = gain_sum_ref[0:1, :]
    if fast:
        small.value[0] = sums_ref[...]
        small.start()
        o_outer_ref[...] = outer.finish()
    for c in range(chunks):
        last.middle(c)
    if fast:
        qkv(2).middle()
        small.over_z()
        o_inner_ref[...] = inner.finish()
        o_output_ref[...] = output.finish()[:, :width].T
        small.over_core()
    for c in range(chunks):
        x = share_ref[run(c), :].astype(f32)
        grad_normed = last.finish(c)
        factor = factor_of(x)
        hat = x * factor
        scaled = grad_normed * gain_a
        back = factor * (scaled - hat * jnp.mean(scaled * hat, axis=-1, keepdims=True))
        input_ref[run(c), :] += back
        if fast and c == 0:
            small.over_y()
    if fast:
        low_each = lax.broadcasted_iota(jnp.int32, (model // 8, BLOCK), 1) < 64
        parts = [qkv(h).finish() for h in range(heads)]
        for k in range(3):
            for h in range(0, heads, 2):
                at = slice(0, BLOCK) if k < 2 else slice(BLOCK, 2 * BLOCK)
                one = parts[h][:, at]
                one = pltpu.roll(one, 64, 1) if k == 1 else one
                if h + 1 < heads:
                    two = parts[h + 1][:, at]
                    two = two if k == 1 else pltpu.roll(two, 64, 1)
                    o_qkv_ref[k, :, h * 64 : (h + 2) * 64] = jnp.where(low_each, one, two)
                else:
                    o_qkv_ref[k, :, h * 64 :] = one[:, :64]
        totals = small.finish()
        o_gain_a_ref[...] = totals[3:4, :model]
        o_gain_f_ref[...] = totals[4:5, :model]
        per_head = small.value[2]
        tables = sum(dot_nt(part.astype(bf16), collapse_ref[...]) for part in split3(per_head))
        o_tables_ref[...] = tables[:heads]
        outer.drain()
        inner.drain()
        output.drain()
        for h in range(heads):
            qkv(h).drain()
        small.drain()
    else:
        o_sums_ref[...] = sums_ref[...]
    wo.drain(0)
    for c in range(chunks):
        for each in (att, grad_att, grads, feed, last):
            each.drain(c)


def spread_scratch(rows, columns, lead=(), own_part=True):
    buffers = [pltpu.VMEM((*lead, 8 * rows, columns), bf16)] if own_part else []
    return buffers + [
        pltpu.VMEM((*lead, 4 * rows, columns), bf16),
        pltpu.VMEM((*lead, 3 * rows, columns), bf16),
        pltpu.SemaphoreType.DMA((*lead, 4)),
        pltpu.SemaphoreType.DMA((*lead, 4)),
    ]


def local(
    fast,
    tokens, lengths, horizontal, vertical, gain_attn, w_qkv, bias_tables, w_output, gain_ffn, w_inner, w_outer, cotangent,
):
    rows, model = tokens.shape
    heads = bias_tables.shape[1]
    width = w_qkv.shape[2]
    units = w_inner.shape[1]
    share = rows // lax.axis_size("mp")
    chunks = rows // CHUNK
    each = model // 8
    sums = (8, WIDE + 4 * BLOCK)

    def dma(*shape):
        return pltpu.SemaphoreType.DMA(shape)

    def vmem(*shape, dtype=bf16):
        return pltpu.VMEM(shape, dtype)

    scratch = [
        vmem(rows, model), vmem(share, model), vmem(3, model, width), vmem(model, units), vmem(units, model),
        vmem(rows, model), dma(7),
        vmem(heads, BLOCK, BLOCK), vmem(rows, BLOCK), vmem(BLOCK, rows), vmem(heads, rows, BLOCK),
        vmem(heads, rows, BLOCK), vmem(heads, rows, BLOCK), vmem(heads, BLOCK, rows), vmem(heads, rows, BLOCK),
        vmem(heads, BLOCK, WIDE), vmem(heads, WIDE, BLOCK),
        vmem(heads, chunks, 256, CHUNK),
        vmem(rows, CHUNK, dtype=f32), vmem(heads * CHUNK, BLOCK, dtype=f32), vmem(rows, BLOCK, dtype=f32),
        vmem(256, rows, dtype=f32), vmem(WIDE, BLOCK, dtype=f32), vmem(heads, BLOCK, rows),
        vmem(*sums, dtype=f32), vmem(8, model, dtype=f32),
        vmem(rows, 256), vmem(rows, 256), dma(chunks, 3), dma(chunks, 3),
        vmem(chunks * 3 * BLOCK, 256), vmem(rows, 256), dma(chunks, 3), dma(chunks, 3),
        vmem(4 * width, model), dma(1, 3), dma(1, 3),
        vmem(rows, model), dma(chunks, 3), dma(chunks, 3),
        vmem(rows, model), dma(chunks, 3), dma(chunks, 3),
        vmem(rows, model), vmem(rows // 2, model), vmem(share, model), dma(chunks, 2), dma(chunks, 2),
        vmem(rows, model), vmem(rows // 2, model), vmem(share, model), dma(chunks, 2), dma(chunks, 2),
        dma(chunks, 2), dma(chunks, 2),
        vmem(rows, units), vmem(rows, units), vmem(share, model, dtype=f32),
    ]
    outs = [((share, model), bf16), ((share, model), f32)]
    if fast:
        outs += [
            ((3, each, width), f32), ((width, each), f32), ((each, units), f32), ((each, units), f32),
            ((1, model), f32), ((1, model), f32), ((heads, 3 * BUCKETS), f32),
        ]
        scratch += [
            *spread_scratch(each, units, own_part=False), *spread_scratch(each, units), *spread_scratch(each, 256),
            *spread_scratch(each, 256, lead=(heads,)),
            vmem(4, *sums, dtype=f32), vmem(*sums, dtype=f32), vmem(3, *sums, dtype=f32), vmem(2, *sums, dtype=f32),
            dma(6), dma(6),
        ]
    else:
        outs += [
            ((heads, model, 256), f32), ((model, width), f32), ((model, units), f32), ((model, units), f32), (sums, f32),
        ]
    full = pl.BlockSpec(memory_space=pltpu.VMEM)
    anywhere = pl.BlockSpec(memory_space=pl.ANY)
    results = pl.pallas_call(
        functools.partial(layer_kernel, fast),
        in_specs=[pl.BlockSpec(memory_space=pltpu.SMEM)] + [full] * 7 + [anywhere] * 6,
        out_specs=[full] * len(outs),
        out_shape=[jax.ShapeDtypeStruct(*out) for out in outs],
        scratch_shapes=scratch,
        compiler_params=pltpu.CompilerParams(vmem_limit_bytes=64 * MIB, collective_id=1, has_side_effects=True),
        name="layer",
    )(
        lengths, horizontal.reshape(1, rows), vertical.reshape(1, rows), gain_attn.reshape(1, model),
        gain_ffn.reshape(1, model), bias_tables.T, jnp.asarray(expansion(), bf16), jnp.asarray(collapse().T, bf16),
        tokens, w_qkv, w_output, w_inner, w_outer, cotangent,
    )
    if fast:
        mixed, input_grad, qkv, output, inner, outer, gain_a, gain_f, tables = results
        return mixed, input_grad, qkv, output, inner, outer.T, gain_a[0], gain_f[0], tables.T
    mixed, input_grad, qkv, output, inner, outer, sums = results
    qkv = qkv[:, :, : 3 * 64].reshape(heads, model, 3, 64).transpose(2, 1, 0, 3).reshape(3, model, width)
    gains = lax.psum(sums[3:5, :model], ("dp", "mp"))
    tables = lax.dot_general(
        jnp.asarray(collapse(), f32),
        lax.psum(sums[:heads], "dp"),
        (((0,), (1,)), ((), ())),
        precision=lax.Precision.HIGHEST,
    )

    def spread(x, axis):
        return lax.psum_scatter(x, "dp", scatter_dimension=axis, tiled=True)

    return (
        mixed, input_grad, spread(qkv, 1), spread(output.T, 1), spread(inner, 0), spread(outer.T, 1),
        gains[0], gains[1], tables,
    )


def solution(mesh):
    fast = mesh.shape["dp"] == 8
    return jax.shard_map(
        functools.partial(local, fast),
        mesh=mesh,
        in_specs=(
            P("dp", None), P("dp"), P("dp"), P("dp"), P(), P(None, None, "mp"), P(None, "mp"), P("mp", None), P(),
            P(None, "mp"), P("mp", None), P("dp", None),
        ),
        out_specs=(
            P(("dp", "mp"), None), P(("dp", "mp"), None), P(None, "dp", "mp"), P("mp", "dp"), P("dp", "mp"),
            P("mp", "dp"), P(), P(), P(None, "mp"),
        ),
        check_vma=False,
    )
```

time: 558 us -> 169 us (0.30); the launches traced: 550 us -> 169 us
  waiting for transfers between devices: 304 us -> 0 us
  Pallas kernels: 67.5 us -> 151 us
  blocking collectives: 61.4 us -> 0 us
  matrix products: 49.1 us -> 0 us
  local copies, waits for them, and re-layouts: 38.5 us -> 13.8 us
  between operations: 15.5 us -> 1.32 us
  other arithmetic: 13.3 us -> 2.66 us
    reduce_scatter x6 -> x0, waiting for transfers between devices: 236 us -> none  [the longest x2 135 us: spread(): return lax.psum_scatter(x, 'dp', scatter_dimension=axis, tiled=True)]
    pallas_call x3 -> x1, Pallas kernels: 67.5 us -> 151 us  [local(): pl.pallas_call(functools.partial(layer_kernel, fast), in_specs=[pl.BlockS...]
    psum x2 -> x0, blocking collectives: 61.4 us -> none  [the longest x1 39.5 us: local(): gains = lax.psum(jnp.stack([gain_a_grad, gain_f_grad]), ('dp', 'mp'))]
    all_gather x2 -> x0, waiting for transfers between devices: 42 us -> none  [gather(): return lax.all_gather(x, 'mp', axis=0, tiled=True)]
    dot_general x10 -> x0, matrix products: 41 us -> none  [the longest x2 15.9 us: dot(): return jnp.dot(a, b, preferred_element_type=f32)]
    unnamed x12 -> x0, waiting for transfers between devices: 25.3 us -> none
    unnamed x56 -> x20, local copies, waits for them, and re-layouts: 30.9 us -> 8.71 us
    unnamed x2 -> x0, matrix products: 8.06 us -> none
  transfers between devices with their start and end apart: 10 -> 0, of which waited for: 8 -> 0; matrix products, arithmetic and copies ran while one was open for 10% -> 0% of each run, Pallas kernels for 7% -> 0%
where the time goes in v4:
time: 169 us
  Pallas kernels  151 us (89%)
  local copies, waits for them, and re-layouts  13.8 us (8%)
  other arithmetic  2.66 us (2%)
    pallas_call x1, Pallas kernels, local(): pl.pallas_call(functools.partial(layer_kernel, fast), in_specs=[pl.BlockS...  151 us
    unnamed x20, local copies, waits for them, and re-layouts  8.71 us

profile of v4, /device:TPU:0, one launch (start us, length us, event | category | flops | bytes accessed | tf_op | source)
XLA Modules:
  0.0 168.8 jit_solution(6915453046679354477)
XLA Ops:
  1.3 1.3 reshape.32.gain_a_ref
  2.6 1.3 reshape.33.gain_f_ref
  3.8 1.3 reshape.30.across_ref
  5.1 1.3 reshape.31.upward_ref
  6.4 2.3 %copy.23.w_qkv_hbm = bf16[3,768,192]{2,1,0:T(8,128)(2,1)} copy(bf16[3,768,192]{1,2,0:T(8,128)(2,1)} %param.19) | data formatting | bytes 1769472 | tf_op args[5]
  8.7 151.0 %layer.1 = (bf16[384,768]{1,0:T(8,128)(2,1)}, f32[384,768]{1,0:T(8,128)}, f32[3,96,192]{2,1,0:T(8,128)}, f32[192,96]{1,0:T(8,128)}, f32[96,768]{1,0:T(8,128)}, /...) custom-call(s32[1]{0:T(128)S(6)} %copy.31.length_ref, ...), custom_call_target="tpu_custom_call" | custom-call | tf_op jit(solution)/shard_map/layer/pallas_call | solution.py:986
  159.8 0.0 copy-start
  159.8 1.4 reduce
  161.2 1.3 reduce.1
  162.4 1.9 %copy.32 = bf16[384,768]{1,0:T(8,128)(2,1)} copy(bf16[384,768]{1,0:T(8,128)(2,1)} %get-tuple-element.36) | data formatting | bytes 1179648
  164.4 0.0 copy-done
  164.4 0.0 copy-start.3
  164.4 0.0 copy-start.4
  164.4 0.0 copy-start.2
  164.4 1.0 copy.33
  165.4 0.1 copy-done.3
  165.5 0.0 copy-start.1
  165.5 0.0 copy-start.5
  165.5 0.7 copy.34
  166.2 0.0 copy-done.4
  166.2 0.6 copy.35
  166.8 0.0 copy-done.2
  166.8 0.7 copy.36
  167.5 0.0 copy-done.1
  167.5 0.7 copy.37
  168.3 0.0 copy-done.5
  168.3 0.6 copy.38
Async XLA Ops:
  159.8 4.6 %copy-start = (f32[384,768]{1,0:T(8,128)S(1)}, f32[384,768]{1,0:T(8,128)}, u32[]{:S(2)}) copy-start(f32[384,768]{1,0:T(8,128)} %get-tuple-element.37) | copy-start | bytes 3538948
  164.4 1.1 copy-start.3
  164.4 1.8 %copy-start.4 = (f32[192,96]{1,0:T(8,128)S(1)}, f32[192,96]{1,0:T(8,128)}, u32[]{:S(2)}) copy-start(f32[192,96]{1,0:T(8,128)} %get-tuple-element.39) | copy-start | bytes 221188
  164.4 2.5 %copy-start.2 = (f32[96,768]{1,0:T(8,128)S(1)}, f32[96,768]{1,0:T(8,128)}, u32[]{:S(2)}) copy-start(f32[96,768]{1,0:T(8,128)} %get-tuple-element.40) | copy-start | bytes 884740
  165.5 2.1 %copy-start.1 = (f32[96,768]{1,0:T(8,128)S(1)}, f32[96,768]{1,0:T(8,128)}, u32[]{:S(2)}) copy-start(f32[96,768]{1,0:T(8,128)} %get-tuple-element.23) | copy-start | bytes 884740
  165.5 2.8 %copy-start.5 = (f32[3,96]{1,0:T(4,128)S(1)}, f32[3,96]{1,0:T(4,128)}, u32[]{:S(2)}) copy-start(f32[3,96]{1,0:T(4,128)} %get-tuple-element.26) | copy-start | bytes 3460

commit v5 on v4

--- a/solution.py
+++ b/solution.py
@@ -25,22 +25,31 @@
 bf16 = jnp.bfloat16
 
 
+def line_bucket(columns):
+    line = jnp.clip(columns - 2 * BLOCK, -HALF, HALF - 1) + HALF
+    line = jnp.where(columns < 5 * BLOCK, line, 0)
+    wrapped = columns % BLOCK
+    wrapped = jnp.where(wrapped < CODES, wrapped, wrapped - BLOCK)
+    plane = jnp.clip(wrapped, -HALF, HALF - 1) + HALF
+    return jnp.where(
+        columns < WIDE, line, jnp.where(columns < WIDE + BLOCK, BUCKETS + plane, 2 * BUCKETS + plane)
+    )
+
+
 def expansion():
-    offsets = np.arange(WIDE) - 2 * BLOCK
-    line = np.clip(offsets, -HALF, HALF - 1) + HALF
-    line[5 * BLOCK :] = 0
-    wrapped = np.arange(BLOCK)
-    wrapped = np.where(wrapped < CODES, wrapped, wrapped - BLOCK)
-    plane = np.clip(wrapped, -HALF, HALF - 1) + HALF
-    buckets = np.concatenate([line, BUCKETS + plane, 2 * BUCKETS + plane])
-    return (np.arange(3 * BUCKETS)[:, None] == buckets[None, :]).astype(np.float32)
+    rows = lax.broadcasted_iota(jnp.int32, (3 * BUCKETS, WIDE + 2 * BLOCK), 0)
+    columns = lax.broadcasted_iota(jnp.int32, (3 * BUCKETS, WIDE + 2 * BLOCK), 1)
+    return jnp.where(rows == line_bucket(columns), 1.0, 0.0).astype(bf16)
 
 
 def collapse():
-    buckets = np.argmax(expansion(), axis=0)
-    buckets[5 * BLOCK + 1 : WIDE] = 0
-    buckets = np.concatenate([buckets, np.zeros(BLOCK, int), np.full(BLOCK, BUCKETS - 1)])
-    return (buckets[:, None] == np.arange(3 * BUCKETS)[None, :]).astype(np.float32)
+    rows = lax.broadcasted_iota(jnp.int32, (3 * BUCKETS, WIDE + 4 * BLOCK), 0)
+    columns = lax.broadcasted_iota(jnp.int32, (3 * BUCKETS, WIDE + 4 * BLOCK), 1)
+    bucket = line_bucket(columns)
+    bucket = jnp.where(columns == 5 * BLOCK, BUCKETS - 1, bucket)
+    bucket = jnp.where(columns >= WIDE + 2 * BLOCK, 0, bucket)
+    bucket = jnp.where(columns >= WIDE + 3 * BLOCK, BUCKETS - 1, bucket)
+    return jnp.where(rows == bucket, 1.0, 0.0).astype(bf16)
 
 
 def roll_rows(value, right):
@@ -103,13 +112,16 @@
     )
 
 
+def beside(z):
+    return z // 2 * 2 + 1 - z % 2
+
+
 def meet(fast):
     mp, dp = lax.axis_index("mp"), lax.axis_index("dp")
     z, x = dp_places()
     others = [(dp, (mp + d) % 4) for d in (1, 2, 3)]
     if fast:
-        others.append((z * 2 + 1 - x, mp))
-        others.extend(((z + d) % 4 * 2 + x, mp) for d in (1, 2, 3))
+        others.extend([(z * 2 + 1 - x, mp), (beside(z) * 2 + x, mp), ((z + 2) % 4 * 2 + x, mp)])
     barrier = pltpu.get_barrier_semaphore()
     for other in others:
         pl.semaphore_signal(barrier, inc=1, device_id=other, device_id_type=pl.DeviceIdType.MESH)
@@ -194,13 +206,13 @@
 
 class Exchange:
 
-    def __init__(self, given, at, taken, send, recv):
-        self.given, self.at, self.taken, self.send, self.recv = given, at, taken, send, recv
+    def __init__(self, given, taken, size, send, recv):
+        self.given, self.taken, self.size, self.send, self.recv = given, taken, size, send, recv
 
     def copy(self, c, d):
         mp = lax.axis_index("mp")
-        dst = self.taken.at[run(c * 4 + mp)]
-        src = self.given.at[self.at(c, d)]
+        src = self.given.at[run(c * 3 + d - 1, 1, self.size)]
+        dst = self.taken.at[run(c * 4 + mp, 1, self.size)]
         return remote(src, dst, self.send.at[c, d - 1], self.recv.at[c, d - 1], (mp + d) % 4)
 
     def start(self, c):
@@ -218,8 +230,8 @@
 
 class Spread:
 
-    def __init__(self, part, near, far, send, recv):
-        self.part, self.near, self.far, self.send, self.recv = part, near, far, send, recv
+    def __init__(self, part, near, pair, far, send, recv):
+        self.part, self.near, self.pair, self.far, self.send, self.recv = part, near, pair, far, send, recv
         self.each = part.shape[0] // 8
 
     def at(self, index, count=1):
@@ -229,96 +241,86 @@
         for r in range(value.shape[0] // self.each):
             j = first_row // self.each + r
             rows = value[r * self.each : (r + 1) * self.each]
-            self.part[self.at(j % 2 * 4 + j // 2), :] = rows.astype(bf16)
-
-    def first(self):
+            self.part[self.at(j % 2 * 4 + j // 2 % 2 * 2 + j // 4), :] = rows.astype(bf16)
+
+    def copy(self, kind):
         z, x = dp_places()
-        src = self.part.at[self.at((1 - x) * 4, 4)]
-        return remote(src, self.near, self.send.at[0], self.recv.at[0], dp=z * 2 + 1 - x)
-
-    def second(self, d):
-        z, x = dp_places()
-        to = (z + d) % 4
-        src = self.part.at[self.at(x * 4 + to)]
-        return remote(src, self.far.at[self.at(d - 1)], self.send.at[d], self.recv.at[d], dp=to * 2 + x)
+        send, recv = self.send.at[kind], self.recv.at[kind]
+        if kind == 0:
+            src = self.part.at[self.at((1 - x) * 4, 4)]
+            return remote(src, self.near, send, recv, dp=z * 2 + 1 - x)
+        if kind == 1:
+            src = self.part.at[self.at(x * 4 + (1 - z % 2) * 2, 2)]
+            return remote(src, self.pair, send, recv, dp=beside(z) * 2 + x)
+        src = self.part.at[self.at(x * 4 + z % 2 * 2 + 1 - z // 2)]
+        return remote(src, self.far, send, recv, dp=(z + 2) % 4 * 2 + x)
 
     def start(self):
-        self.first().start()
+        self.copy(0).start()
 
     def middle(self):
         z, x = dp_places()
-        self.first().wait_recv()
-        for d in range(1, 4):
-            to = (z + d) % 4
-            at = self.at(x * 4 + to)
-            self.part[at, :] = (self.part[at, :].astype(f32) + self.near[self.at(to), :].astype(f32)).astype(bf16)
-            self.second(d).start()
+        self.copy(0).wait_recv()
+        at = self.at(x * 4 + (1 - z % 2) * 2, 2)
+        near = self.near[self.at((1 - z % 2) * 2, 2), :].astype(f32)
+        self.part[at, :] = (self.part[at, :].astype(f32) + near).astype(bf16)
+        self.copy(1).start()
+
+    def sum_of(self, half):
+        z, x = dp_places()
+        total = self.part[self.at(x * 4 + z % 2 * 2 + half), :].astype(f32)
+        total = total + self.near[self.at(z % 2 * 2 + half), :].astype(f32)
+        return total + self.pair[self.at(half), :].astype(f32)
+
+    def third(self):
+        z, x = dp_places()
+        self.copy(1).wait_recv()
+        self.part[self.at(x * 4 + z % 2 * 2 + 1 - z // 2), :] = self.sum_of(1 - z // 2).astype(bf16)
+        self.copy(2).start()
 
     def finish(self):
-        z, x = dp_places()
-        total = self.part[self.at(x * 4 + z), :].astype(f32) + self.near[self.at(z), :].astype(f32)
-        for d in range(1, 4):
-            self.second(d).wait_recv()
-            total = total + self.far[self.at(d - 1), :].astype(f32)
-        return total
+        z, _ = dp_places()
+        self.copy(2).wait_recv()
+        return self.sum_of(z // 2) + self.far[...].astype(f32)
 
     def drain(self):
-        self.first().wait_send()
-        for d in range(1, 4):
-            self.second(d).wait_send()
+        for kind in range(3):
+            self.copy(kind).wait_send()
 
 
 class Total:
 
-    def __init__(self, value, near, far, across, send, recv):
-        self.value, self.near, self.far, self.across, self.send, self.recv = value, near, far, across, send, recv
+    def __init__(self, value, taken, send, recv):
+        self.value, self.taken, self.send, self.recv = value, taken, send, recv
 
     def copy(self, kind):
         z, x = dp_places()
-        mp, _, _, sibling, across = mp_places()
-        send, recv = self.send.at[kind], self.recv.at[kind]
-        if kind == 0:
-            return remote(self.value.at[0], self.near, send, recv, dp=z * 2 + 1 - x)
-        if kind < 4:
-            return remote(self.value.at[1], self.far.at[kind - 1], send, recv, dp=(z + kind) % 4 * 2 + x)
-        if kind == 4:
-            return remote(self.value.at[2], self.across.at[0], send, recv, sibling)
-        return remote(self.value.at[3], self.across.at[1], send, recv, across)
-
-    def start(self):
+        _, _, _, sibling, across = mp_places()
+        mp = {3: sibling, 4: across}.get(kind)
+        dp = {0: z * 2 + 1 - x, 1: beside(z) * 2 + x, 2: (z + 2) % 4 * 2 + x}.get(kind)
+        return remote(self.value.at[kind], self.taken.at[kind], self.send.at[kind], self.recv.at[kind], mp, dp)
+
+    def start(self, value):
+        self.value[0] = value
         self.copy(0).start()
 
-    def over_z(self):
-        self.copy(0).wait_recv()
-        self.value[1] = self.value[0] + self.near[...]
-        for kind in range(1, 4):
-            self.copy(kind).start()
-
-    def over_core(self):
-        total = self.value[1]
-        for kind in range(1, 4):
-            self.copy(kind).wait_recv()
-            total = total + self.far[kind - 1]
-        self.value[2] = total
-        self.copy(4).start()
-
-    def over_y(self):
+    def turn(self, kind):
+        self.copy(kind - 1).wait_recv()
+        self.value[kind] = self.value[kind - 1] + self.taken[kind - 1]
+        self.copy(kind).start()
+
+    def finish(self):
         self.copy(4).wait_recv()
-        self.value[3] = self.value[2] + self.across[0]
-        self.copy(5).start()
-
-    def finish(self):
-        self.copy(5).wait_recv()
-        return self.value[3] + self.across[1]
+        return self.value[4] + self.taken[4]
 
     def drain(self):
-        for kind in range(6):
+        for kind in range(5):
             self.copy(kind).wait_send()
 
 
 def layer_kernel(
     fast,
-    length_ref, across_ref, upward_ref, gain_a_ref, gain_f_ref, tables_ref, expand_ref, collapse_ref,
+    length_ref, across_ref, upward_ref, gain_a_ref, gain_f_ref, tables_ref,
     tokens_hbm, w_qkv_hbm, w_output_hbm, w_inner_hbm, w_outer_hbm, cot_hbm,
     *rest,
 ):
@@ -328,17 +330,16 @@
     else:
         mixed_ref, input_ref, o_qkv_ref, o_output_ref, o_inner_ref, o_outer_ref, o_sums_ref = outs
     (
-        x1, share_ref, w_qkv_ref, w_inner_ref, w_outer_ref, cot_ref, load_sem,
-        plane_ref, hot_ref, hot_t_ref, qa_ref, qb_ref, k2_ref, kt2_ref, v_ref, band_ref, band_t_ref, qt_ref,
+        x1, w_qkv_ref, w_inner_ref, w_outer_ref, cot_ref, load_sem,
+        codes_ref, plane_ref, hot_ref, hot_t_ref, qa_ref, qb_ref, k2_ref, kt2_ref, v_ref, band_ref, band_t_ref, qt_ref,
         s_ref, res_ref, dv_ref, dqt_ref, bands_ref, dat_ref, sums_ref, gain_sum_ref,
-        att_ref, ax_ref, att_send, att_recv,
+        att_ref, af_ref, att_send, att_recv,
         es_ref, ga_ref, es_send, es_recv,
         wo_ref, wo_send, wo_recv,
-        nf_ref, nf_send, nf_recv,
+        nf_ref,
         ghl_ref, ghl_send, ghl_recv,
-        feed_part, feed_near, feed_far, feed_send, feed_recv,
-        norm_part, norm_near, norm_far, norm_send, norm_recv,
-        last_send, last_recv,
+        feed_part, feed_send, feed_recv, norm_part, norm_send, norm_recv, last_send, last_recv, near_ref, far_ref,
+        credit,
         low_ref, grad_low_ref, hidden_ref,
         *spreads,
     ) = scratch
@@ -350,25 +351,27 @@
     chunks = rows // CHUNK
     blocks = rows // BLOCK
     half_model = model // 2
-    mp = lax.axis_index("mp")
+    mp, _, _, sibling, across = mp_places()
     da_ref, dk_ref, wt_ref = qa_ref, res_ref, w_inner_ref
 
-    att = Exchange(att_ref, lambda c, d: run(c * 4 + (mp + d) % 4), ax_ref, att_send, att_recv)
-    grad_att = Exchange(es_ref, lambda c, d: run(c * 3 + d - 1), ga_ref, es_send, es_recv)
+    att = Gather(af_ref, att_send, att_recv, CHUNK + CHUNK // 2)
+    grad_att = Exchange(es_ref, ga_ref, BLOCK + BLOCK // 2, es_send, es_recv)
     wo = Gather(wo_ref, wo_send, wo_recv, width)
-    normed = Gather(nf_ref, nf_send, nf_recv)
     grads = Gather(ghl_ref, ghl_send, ghl_recv)
-    feed = Scatter(feed_part, feed_near, feed_far, feed_send, feed_recv)
-    norm = Scatter(norm_part, norm_near, norm_far, norm_send, norm_recv)
-    last = Scatter(norm_part, norm_near, norm_far, last_send, last_recv)
+    feed = Scatter(feed_part, near_ref, far_ref, feed_send, feed_recv)
+    norm = Scatter(norm_part, near_ref, far_ref, norm_send, norm_recv)
+    last = Scatter(norm_part, near_ref, far_ref, last_send, last_recv)
     if fast:
-        outer = Spread(w_outer_ref, *spreads[0:4])
-        inner = Spread(*spreads[4:9])
-        output = Spread(*spreads[9:14])
-        small = Total(*spreads[19:25])
+        outer = Spread(w_outer_ref, *spreads[0:5])
+        inner = Spread(*spreads[5:11])
+        output = Spread(*spreads[11:17])
+        small = Total(*spreads[23:27])
 
         def qkv(h):
-            return Spread(*[ref.at[h] for ref in spreads[14:19]])
+            return Spread(*[ref.at[h] for ref in spreads[17:23]])
+
+    def place(m, c):
+        return run(m * chunks + c)
 
     loads = [
         pltpu.make_async_copy(src, dst, load_sem.at[i])
@@ -377,19 +380,17 @@
                 (tokens_hbm, x1),
                 (w_qkv_hbm, w_qkv_ref),
                 (w_output_hbm, wo_ref.at[wo.at(0, mp)]),
-                (tokens_hbm.at[run(mp * chunks, chunks)], share_ref),
                 (w_inner_hbm, w_inner_ref),
                 (w_outer_hbm, w_outer_ref),
                 (cot_hbm, cot_ref),
+                *[(tokens_hbm.at[place(m, c)], low_ref.at[run(c * 4 + m)]) for c in range(chunks) for m in range(4)],
+                (tokens_hbm.at[run(mp * chunks, chunks)], cot_ref.at[run(0, chunks)]),
             ]
         )
     ]
-    for load in loads:
+    for load in loads[:-1]:
         load.start()
     meet(fast)
-
-    def place(m, c):
-        return run(m * chunks + c)
 
     def window(m, c):
         block = m * chunks + c
@@ -397,7 +398,7 @@
         return start, start - block + 2
 
 
-    expanded = dot(tables_ref[...], expand_ref[...])
+    expanded = dot(tables_ref[...], expansion())
     square_rows = lax.broadcasted_iota(jnp.int32, (BLOCK, BLOCK), 0)
     square_lanes = lax.broadcasted_iota(jnp.int32, (BLOCK, BLOCK), 1)
     for h in range(heads):
@@ -405,11 +406,11 @@
         band = roll_rows(line, True)
         band_ref[h] = band.astype(bf16)
         band_t_ref[h] = band.T.astype(bf16)
-        across = roll_rows(jnp.broadcast_to(expanded[h : h + 1, WIDE : WIDE + BLOCK], (BLOCK, BLOCK)), True)
+        level = roll_rows(jnp.broadcast_to(expanded[h : h + 1, WIDE : WIDE + BLOCK], (BLOCK, BLOCK)), True)
         upward = roll_rows(jnp.broadcast_to(expanded[h : h + 1, WIDE + BLOCK :], (BLOCK, BLOCK)), True)
         plane = jnp.where(
             (square_rows < CODES) & (square_lanes < CODES),
-            across,
+            level,
             jnp.where((square_rows >= CODES) & (square_lanes >= CODES), upward, 0.0),
         )
         plane_ref[h] = plane.astype(bf16)
@@ -417,8 +418,10 @@
     wo.start(0)
     loads[1].wait()
     loads[0].wait()
-    gain_a = gain_a_ref[...].astype(f32)
-    gain_f = gain_f_ref[...].astype(f32)
+    gain_a = gain_a_ref[...].reshape(1, model).astype(f32)
+    gain_f = gain_f_ref[...].reshape(1, model).astype(f32)
+    codes_ref[0:1, :] = across_ref[...].reshape(1, rows)
+    codes_ref[1:2, :] = upward_ref[...].reshape(1, rows)
     lanes = lax.broadcasted_iota(jnp.int32, (CHUNK, BLOCK), 1)
     low = lanes < FAR
 
@@ -429,9 +432,9 @@
         x1[at, :] = normed_rows
         codes_lines = lax.broadcasted_iota(jnp.int32, (BLOCK, CHUNK), 0)
         hot_t = jnp.where(
-            codes_lines == jnp.broadcast_to(across_ref[:, at], (BLOCK, CHUNK)),
+            codes_lines == jnp.broadcast_to(codes_ref[0:1, at], (BLOCK, CHUNK)),
             1.0,
-            jnp.where(codes_lines - CODES == jnp.broadcast_to(upward_ref[:, at], (BLOCK, CHUNK)), 1.0, 0.0),
+            jnp.where(codes_lines - CODES == jnp.broadcast_to(codes_ref[1:2, at], (BLOCK, CHUNK)), 1.0, 0.0),
         )
         hot = hot_t.T.astype(bf16)
         hot_t_ref[:, at] = hot_t.astype(bf16)
@@ -454,19 +457,19 @@
             columns = s_ref[:CHUNK, h // 2 * BLOCK : h // 2 * BLOCK + BLOCK]
             return columns if h % 2 == 0 else pltpu.roll(columns, 64, 1)
 
-        s_ref[:CHUNK, :width] = dot(normed_rows, w_qkv_ref[0])
+        s_ref[:CHUNK, :width] = dot_nt(normed_rows, w_qkv_ref[0])
         for h in range(heads):
             left = expanded[h : h + 1, 0:1]
             right = expanded[h : h + 1, WIDE - BLOCK - 1 : WIDE - BLOCK]
             query_side = jnp.where(far_left, left, jnp.where(far_right, right, jnp.where(lanes == MASK, DEAD, 0.0)))
             qa_ref[h, at, :] = dot(hot, plane_ref[h]).astype(bf16)
             qb_ref[h, at, :] = jnp.where(low, part(h).astype(bf16).astype(f32) * 0.125, query_side).astype(bf16)
-        s_ref[:CHUNK, :width] = dot(normed_rows, w_qkv_ref[1])
+        s_ref[:CHUNK, :width] = dot_nt(normed_rows, w_qkv_ref[1])
         for h in range(heads):
             second = jnp.where(low, part(h), key_side)
             k2_ref[h, at, :] = second.astype(bf16)
             kt2_ref[h, :, at] = second.T.astype(bf16)
-        s_ref[:CHUNK, :width] = dot(normed_rows, w_qkv_ref[2])
+        s_ref[:CHUNK, :width] = dot_nt(normed_rows, w_qkv_ref[2])
         for h in range(heads):
             v_ref[h, at, :] = jnp.where(low, part(h), 1.0).astype(bf16)
         return carry
@@ -474,18 +477,37 @@
     s_ref[:CHUNK, :] = jnp.zeros_like(s_ref[:CHUNK, :])
     lax.fori_loop(0, chunks, prepare, 0)
     wo.forward(0)
-    loads[3].wait()
     gain_sum_ref[...] = jnp.zeros_like(gain_sum_ref)
     sums_ref[...] = jnp.zeros_like(sums_ref)
 
+    half_low = lax.broadcasted_iota(jnp.int32, (CHUNK // 2, BLOCK), 1) < 64
+    quarter_low = lax.broadcasted_iota(jnp.int32, (BLOCK // 2, BLOCK), 1) < 64
+
+    def share_attended(c):
+        at = run(c, 1, CHUNK)
+        mine = att.at(c, mp).start
+        third = att_ref[at, BLOCK:].astype(f32)
+        af_ref[pl.ds(pl.multiple_of(mine, CHUNK // 2), CHUNK), :] = att_ref[at, :BLOCK]
+        beside_it = jnp.where(half_low, third[: CHUNK // 2], pltpu.roll(third[CHUNK // 2 :], 64, 1)).astype(bf16)
+        af_ref[pl.ds(pl.multiple_of(mine + CHUNK, CHUNK // 2), CHUNK // 2), :] = beside_it
+        att.start(c)
+
     def hidden_of(c):
         att.finish(c)
-        hidden = share_ref[run(c), :].astype(f32)
+        hidden = low_ref[run(c, 1, CHUNK), :].astype(f32)
         for m in range(pieces):
-            hidden = hidden + dot(ax_ref[run(c * 4 + m), :width], wo_ref[m * width : (m + 1) * width, :])
-        hidden_ref[run(c), :] = hidden
-        nf_ref[normed.at(c, mp), :] = (hidden * factor_of(hidden) * gain_f).astype(bf16)
-        normed.start(c)
+            first = (c * 4 + m) * (CHUNK + CHUNK // 2)
+            pair = af_ref[pl.ds(pl.multiple_of(first, CHUNK // 2), CHUNK), :]
+            third = af_ref[pl.ds(pl.multiple_of(first + CHUNK, CHUNK // 2), CHUNK // 2), :]
+            third = jnp.concatenate([third, pltpu.roll(third.astype(f32), 64, 1).astype(bf16)], axis=0)
+            weights = wo_ref[m * width : (m + 1) * width, :]
+            hidden = hidden + dot(jnp.concatenate([pair, third[:, :64]], axis=1), weights)
+        nf_ref[run(c, 1, CHUNK), :] = (hidden * factor_of(hidden) * gain_f).astype(bf16)
+        for m in range(pieces):
+
+            @pl.when(mp == m)
+            def _(m=m):
+                hidden_ref[run(c), :] = hidden[m * BLOCK : (m + 1) * BLOCK]
 
     def grad_of(c):
         grad_normed = norm.finish(c)
@@ -502,13 +524,15 @@
 
         def of(m):
             value = dot_nt(grad_low, wo_ref[run(m, 1, width), :])
-            return jnp.concatenate([value, jnp.zeros((BLOCK, 256 - width), f32)], axis=1).astype(bf16)
-
-        ga_ref[run(c * 4 + mp), :] = of(mp)
+            third = jnp.concatenate([value[:, BLOCK:], jnp.zeros((BLOCK, 64), f32)], axis=1)
+            third = jnp.where(quarter_low, third[: BLOCK // 2], pltpu.roll(third[BLOCK // 2 :], 64, 1))
+            return jnp.concatenate([value[:, :BLOCK], third], axis=0).astype(bf16)
+
+        size = BLOCK + BLOCK // 2
+        ga_ref[run(c * 4 + mp, 1, size), :] = of(mp)
         for d in (1, 2, 3):
-            es_ref[run(c * 3 + d - 1), :] = of((mp + d) % 4)
+            es_ref[run(c * 3 + d - 1, 1, size), :] = of((mp + d) % 4)
         grad_att.start(c)
-        grads.start(c)
 
     def attend(t, carry):
         c = t // heads
@@ -550,28 +574,22 @@
                 pairs.append(pair.astype(bf16))
             merged = jnp.concatenate(pairs, axis=1)
             att_ref[run(c, 1, CHUNK), :] = merged
-            ax_ref[run(c * 4 + mp), :] = att_ref[run(c * 4 + mp), :]
-            att.start(c)
+            share_attended(c)
 
         @pl.when(t == 4)
         def _():
-            wo.finish(0)
-            hidden_of(0)
-
-        @pl.when(t == 6)
-        def _():
-            normed.forward(0)
+            att.forward(0)
 
         @pl.when(t == 7)
         def _():
-            hidden_of(1)
+            att.forward(1)
 
         return carry
 
     lax.fori_loop(0, chunks * heads, attend, 0)
-    for load in loads[4:]:
+    for load in loads[3:-1]:
         load.wait()
-    normed.finish(0)
+    wo.finish(0)
 
     steps = units // 256
 
@@ -579,9 +597,9 @@
         c = t // steps
         b = t % steps
 
-        @pl.when((b == 0) & (c > 0))
-        def _():
-            normed.finish(c)
+        @pl.when(b == 0)
+        def _():
+            hidden_of(c)
 
         at = run(b, 1, 256)
         x = nf_ref[run(c, 1, CHUNK), :]
@@ -618,23 +636,14 @@
                 feed.put(c, m, jnp.concatenate([p[:, :256] for p in parts], axis=1))
                 norm.put(c, m, jnp.concatenate([p[:, 256:] for p in parts], axis=1))
             norm.start(c)
-            feed.start(c)
 
         @pl.when(t == 1)
         def _():
-            normed.forward(1)
-
-        @pl.when(t == 2)
-        def _():
-            hidden_of(2)
+            att.forward(2)
 
         @pl.when(t == 3)
         def _():
             norm.middle(0)
-
-        @pl.when(t == 5)
-        def _():
-            normed.forward(2)
 
         @pl.when(t == 6)
         def _():
@@ -669,20 +678,24 @@
     norm.middle(2)
     grad_of(1)
     weights_of(False)
-    for c in range(chunks):
-        normed.drain(c)
     wt_ref[...] = jnp.zeros_like(wt_ref)
     for k in range(3):
-        turned = w_qkv_ref[k].astype(f32).T.astype(bf16)
         for h in range(heads):
-            wt_ref[h * 256 + k * 64 : h * 256 + (k + 1) * 64, :] = turned[h * 64 : (h + 1) * 64]
+            wt_ref[h * 256 + k * 64 : h * 256 + (k + 1) * 64, :] = w_qkv_ref[k, h * 64 : (h + 1) * 64, :]
 
     def receive(c):
         grad_att.finish(c)
         at = run(c, 1, CHUNK)
+        pairs, thirds = [], []
+        for m in range(pieces):
+            first = (c * 4 + m) * (BLOCK + BLOCK // 2)
+            pairs.append(ga_ref[pl.ds(pl.multiple_of(first, BLOCK // 2), BLOCK), :])
+            third = ga_ref[pl.ds(pl.multiple_of(first + BLOCK, BLOCK // 2), BLOCK // 2), :].astype(f32)
+            thirds.extend([third, pltpu.roll(third, 64, 1)])
+        received = [jnp.concatenate(pairs, axis=0).astype(f32), jnp.concatenate(thirds, axis=0)]
         for h in range(heads):
             pair = slice(h // 2 * BLOCK, h // 2 * BLOCK + BLOCK)
-            grad = ga_ref[at, pair].astype(f32)
+            grad = received[h // 2]
             out = att_ref[at, pair].astype(f32)
             if h % 2 == 1:
                 grad = pltpu.roll(grad, 64, 1)
@@ -709,6 +722,9 @@
         for b in range(1, value.shape[1] // BLOCK):
             total = total + value[:, b * BLOCK : (b + 1) * BLOCK]
         return jnp.sum(total, axis=0, keepdims=True)
+
+    def mix(k):
+        mixed_ref[run(k), :] = (hidden_ref[run(k), :] + feed.finish(k)).astype(bf16)
 
     def head(h, carry):
         dk_ref[...] = jnp.zeros_like(dk_ref)
@@ -743,53 +759,59 @@
             def when(head_index, chunk_index):
                 return pl.when((h == head_index) & (c == chunk_index))
 
-            def mix(k):
-                mixed_ref[run(k), :] = (hidden_ref[run(k), :] + feed.finish(k)).astype(bf16)
-
             @when(0, 0)
             def _():
                 grad_of(2)
 
             @when(0, 1)
             def _():
-                grads.forward(0)
-                feed.middle(0)
+                for k in range(chunks):
+                    grads.start(k)
 
             @when(0, 2)
             def _():
-                grads.forward(1)
-                feed.middle(1)
+                for k in range(chunks):
+                    feed.start(k)
+                if fast:
+                    outer.middle()
+                    inner.start()
 
             @when(1, 0)
             def _():
+                grads.forward(0)
+
+            @when(1, 1)
+            def _():
+                grads.forward(1)
+                if fast:
+                    outer.third()
+
+            @when(1, 2)
+            def _():
                 grads.forward(2)
+                feed.middle(0)
+
+            @when(2, 0)
+            def _():
+                feed.middle(1)
+                if fast:
+                    inner.middle()
+
+            @when(2, 1)
+            def _():
                 feed.middle(2)
                 mix(0)
                 if fast:
-                    outer.middle()
-                    inner.start()
-
-            @when(1, 1)
+                    qkv(0).middle()
+                    o_outer_ref[...] = outer.finish()
+
+            @when(2, 2)
             def _():
                 mix(1)
-
-            @when(1, 2)
-            def _():
-                mix(2)
-
-            if fast:
-
-                @when(2, 0)
-                def _():
-                    inner.middle()
-
-                @when(2, 1)
-                def _():
-                    qkv(0).middle()
-
-                @when(2, 2)
-                def _():
+                if fast:
+                    inner.third()
                     output.middle()
+                    qkv(0).third()
                     qkv(1).middle()
 
             return carry
@@ -848,6 +870,13 @@
 
     lax.fori_loop(0, heads, head, 0)
 
+    mix(2)
+    credits = [(sibling, credit.at[0]), (across, credit.at[1])]
+    for other, sem in credits:
+        pl.semaphore_signal(
+            sem, inc=1, device_id=(lax.axis_index("dp"), other), device_id_type=pl.DeviceIdType.MESH
+        )
+    loads[-1].start()
     for c in range(chunks):
         norm.drain(c)
     gain_total = jnp.zeros((1, model), f32)
@@ -857,23 +886,28 @@
             partial = dot(nf_ref[at, :], wt_ref[...])
             gain_total = gain_total + jnp.sum(partial * x1[at, :].astype(f32), axis=0, keepdims=True)
             last.put(c, m, partial)
+        if c == 0:
+            for _, sem in credits:
+                pl.semaphore_wait(sem, 1)
         last.start(c)
+        if c > 0:
+            last.middle(c - 1)
     sums_ref[3:4, :model] = gain_total / gain_a
     sums_ref[4:5, :model] = gain_sum_ref[0:1, :]
     if fast:
-        small.value[0] = sums_ref[...]
-        small.start()
-        o_outer_ref[...] = outer.finish()
-    for c in range(chunks):
-        last.middle(c)
+        small.start(sums_ref[...])
+        output.third()
+        qkv(1).third()
+    last.middle(chunks - 1)
     if fast:
         qkv(2).middle()
-        small.over_z()
+        small.turn(1)
         o_inner_ref[...] = inner.finish()
+        small.turn(2)
         o_output_ref[...] = output.finish()[:, :width].T
-        small.over_core()
+    loads[-1].wait()
     for c in range(chunks):
-        x = share_ref[run(c), :].astype(f32)
+        x = cot_ref[run(c), :].astype(f32)
         grad_normed = last.finish(c)
         factor = factor_of(x)
         hat = x * factor
@@ -881,7 +915,10 @@
         back = factor * (scaled - hat * jnp.mean(scaled * hat, axis=-1, keepdims=True))
         input_ref[run(c), :] += back
         if fast and c == 0:
-            small.over_y()
+            small.turn(3)
+            qkv(2).third()
+        if fast and c == 1:
+            small.turn(4)
     if fast:
         low_each = lax.broadcasted_iota(jnp.int32, (model // 8, BLOCK), 1) < 64
         parts = [qkv(h).finish() for h in range(heads)]
@@ -897,10 +934,10 @@
                 else:
                     o_qkv_ref[k, :, h * 64 :] = one[:, :64]
         totals = small.finish()
-        o_gain_a_ref[...] = totals[3:4, :model]
-        o_gain_f_ref[...] = totals[4:5, :model]
-        per_head = small.value[2]
-        tables = sum(dot_nt(part.astype(bf16), collapse_ref[...]) for part in split3(per_head))
+        o_gain_a_ref[...] = totals[3:4, :model].reshape(model)
+        o_gain_f_ref[...] = totals[4:5, :model].reshape(model)
+        buckets = collapse()
+        tables = sum(dot_nt(part.astype(bf16), buckets) for part in split3(small.value[3]))
         o_tables_ref[...] = tables[:heads]
         outer.drain()
         inner.drain()
@@ -920,9 +957,10 @@
     buffers = [pltpu.VMEM((*lead, 8 * rows, columns), bf16)] if own_part else []
     return buffers + [
         pltpu.VMEM((*lead, 4 * rows, columns), bf16),
-        pltpu.VMEM((*lead, 3 * rows, columns), bf16),
-        pltpu.SemaphoreType.DMA((*lead, 4)),
-        pltpu.SemaphoreType.DMA((*lead, 4)),
+        pltpu.VMEM((*lead, 2 * rows, columns), bf16),
+        pltpu.VMEM((*lead, rows, columns), bf16),
+        pltpu.SemaphoreType.DMA((*lead, 3)),
+        pltpu.SemaphoreType.DMA((*lead, 3)),
     ]
 
 
@@ -946,36 +984,35 @@
         return pltpu.VMEM(shape, dtype)
 
     scratch = [
-        vmem(rows, model), vmem(share, model), vmem(3, model, width), vmem(model, units), vmem(units, model),
-        vmem(rows, model), dma(7),
-        vmem(heads, BLOCK, BLOCK), vmem(rows, BLOCK), vmem(BLOCK, rows), vmem(heads, rows, BLOCK),
+        vmem(rows, model), vmem(3, width, model), vmem(model, units), vmem(units, model),
+        vmem(rows, model), dma(7 + 4 * chunks),
+        vmem(8, rows, dtype=jnp.int32), vmem(heads, BLOCK, BLOCK), vmem(rows, BLOCK), vmem(BLOCK, rows), vmem(heads, rows, BLOCK),
         vmem(heads, rows, BLOCK), vmem(heads, rows, BLOCK), vmem(heads, BLOCK, rows), vmem(heads, rows, BLOCK),
         vmem(heads, BLOCK, WIDE), vmem(heads, WIDE, BLOCK),
         vmem(heads, chunks, 256, CHUNK),
         vmem(rows, CHUNK, dtype=f32), vmem(heads * CHUNK, BLOCK, dtype=f32), vmem(rows, BLOCK, dtype=f32),
         vmem(256, rows, dtype=f32), vmem(WIDE, BLOCK, dtype=f32), vmem(heads, BLOCK, rows),
         vmem(*sums, dtype=f32), vmem(8, model, dtype=f32),
-        vmem(rows, 256), vmem(rows, 256), dma(chunks, 3), dma(chunks, 3),
-        vmem(chunks * 3 * BLOCK, 256), vmem(rows, 256), dma(chunks, 3), dma(chunks, 3),
+        vmem(rows, 256), vmem(6 * rows, BLOCK), dma(chunks, 3), dma(chunks, 3),
+        vmem(chunks * 9 * BLOCK // 2, BLOCK), vmem(chunks * 6 * BLOCK, BLOCK), dma(chunks, 3), dma(chunks, 3),
         vmem(4 * width, model), dma(1, 3), dma(1, 3),
+        vmem(rows, model),
         vmem(rows, model), dma(chunks, 3), dma(chunks, 3),
-        vmem(rows, model), dma(chunks, 3), dma(chunks, 3),
-        vmem(rows, model), vmem(rows // 2, model), vmem(share, model), dma(chunks, 2), dma(chunks, 2),
-        vmem(rows, model), vmem(rows // 2, model), vmem(share, model), dma(chunks, 2), dma(chunks, 2),
-        dma(chunks, 2), dma(chunks, 2),
+        vmem(rows, model), dma(chunks, 2), dma(chunks, 2), vmem(rows, model), dma(chunks, 2), dma(chunks, 2),
+        dma(chunks, 2), dma(chunks, 2), vmem(rows // 2, model), vmem(share, model),
+        pltpu.SemaphoreType.REGULAR((2,)),
         vmem(rows, units), vmem(rows, units), vmem(share, model, dtype=f32),
     ]
     outs = [((share, model), bf16), ((share, model), f32)]
     if fast:
         outs += [
             ((3, each, width), f32), ((width, each), f32), ((each, units), f32), ((each, units), f32),
-            ((1, model), f32), ((1, model), f32), ((heads, 3 * BUCKETS), f32),
+            ((model,), f32), ((model,), f32), ((heads, 3 * BUCKETS), f32),
         ]
         scratch += [
             *spread_scratch(each, units, own_part=False), *spread_scratch(each, units), *spread_scratch(each, 256),
             *spread_scratch(each, 256, lead=(heads,)),
-            vmem(4, *sums, dtype=f32), vmem(*sums, dtype=f32), vmem(3, *sums, dtype=f32), vmem(2, *sums, dtype=f32),
-            dma(6), dma(6),
+            vmem(5, *sums, dtype=f32), vmem(5, *sums, dtype=f32), dma(5), dma(5),
         ]
     else:
         outs += [
@@ -985,27 +1022,26 @@
     anywhere = pl.BlockSpec(memory_space=pl.ANY)
     results = pl.pallas_call(
         functools.partial(layer_kernel, fast),
-        in_specs=[pl.BlockSpec(memory_space=pltpu.SMEM)] + [full] * 7 + [anywhere] * 6,
+        in_specs=[pl.BlockSpec(memory_space=pltpu.SMEM)] + [full] * 5 + [anywhere] * 6,
         out_specs=[full] * len(outs),
         out_shape=[jax.ShapeDtypeStruct(*out) for out in outs],
         scratch_shapes=scratch,
         compiler_params=pltpu.CompilerParams(vmem_limit_bytes=64 * MIB, collective_id=1, has_side_effects=True),
         name="layer",
     )(
-        lengths, horizontal.reshape(1, rows), vertical.reshape(1, rows), gain_attn.reshape(1, model),
-        gain_ffn.reshape(1, model), bias_tables.T, jnp.asarray(expansion(), bf16), jnp.asarray(collapse().T, bf16),
-        tokens, w_qkv, w_output, w_inner, w_outer, cotangent,
+        lengths, horizontal, vertical, gain_attn, gain_ffn, bias_tables.T,
+        tokens, jnp.swapaxes(w_qkv, 1, 2), w_output, w_inner, w_outer, cotangent,
     )
     if fast:
         mixed, input_grad, qkv, output, inner, outer, gain_a, gain_f, tables = results
-        return mixed, input_grad, qkv, output, inner, outer.T, gain_a[0], gain_f[0], tables.T
+        return mixed, input_grad, qkv, output, inner, outer.T, gain_a, gain_f, tables.T
     mixed, input_grad, qkv, output, inner, outer, sums = results
     qkv = qkv[:, :, : 3 * 64].reshape(heads, model, 3, 64).transpose(2, 1, 0, 3).reshape(3, model, width)
     gains = lax.psum(sums[3:5, :model], ("dp", "mp"))
     tables = lax.dot_general(
-        jnp.asarray(collapse(), f32),
+        collapse().astype(f32),
         lax.psum(sums[:heads], "dp"),
-        (((0,), (1,)), ((), ())),
+        (((1,), (1,)), ((), ())),
         precision=lax.Precision.HIGHEST,
     )
 

time: 169 us -> 140 us (0.83)
  Pallas kernels: 151 us -> 131 us
  local copies, waits for them, and re-layouts: 13.8 us -> 7.68 us
  other arithmetic: 2.66 us -> 0 us
    pallas_call x1, Pallas kernels: 151 us -> 131 us  [local(): pl.pallas_call(functools.partial(layer_kernel, fast), in_specs=[pl.BlockS...]
    reshape x4 -> x0, local copies, waits for them, and re-layouts: 5.11 us -> none  [the longest x1 1.29 us: local(): horizontal.reshape(1, rows)]
    pallas_call x2 -> x0, other arithmetic: 2.66 us -> none  [local(): pl.pallas_call(functools.partial(layer_kernel, fast), in_specs=[pl.BlockS...]
    unnamed x20 -> x25, local copies, waits for them, and re-layouts: 8.71 us -> 7.68 us
where the time goes in v5:
time: 140 us
  Pallas kernels  131 us (94%)
  local copies, waits for them, and re-layouts  7.68 us (5%)
    pallas_call x1, Pallas kernels, local(): pl.pallas_call(functools.partial(layer_kernel, fast), in_specs=[pl.BlockS...  131 us
    unnamed x25, local copies, waits for them, and re-layouts  7.68 us

profile of v5, /device:TPU:0, one launch (start us, length us, event | category | flops | bytes accessed | tf_op | source)
XLA Modules:
  0.0 139.7 jit_solution(17329128784163935682)
XLA Ops:
  1.3 130.7 %layer.1 = (bf16[384,768]{1,0:T(8,128)(2,1)}, f32[384,768]{1,0:T(8,128)}, f32[3,96,192]{2,1,0:T(8,128)}, f32[192,96]{1,0:T(8,128)}, f32[96,768]{1,0:T(8,128)}, /...) custom-call(s32[1]{0:T(128)S(6)} %copy.30.length_ref, s32[1536]{0:T(1024)} %across_ref.1, ...), custom_call_target="tpu_custom_call" | custom-call | tf_op jit(solution)/shard_map/layer/pallas_call | solution.py:1023
  132.0 0.0 copy-start
  132.0 2.0 %copy.31 = bf16[384,768]{1,0:T(8,128)(2,1)} copy(bf16[384,768]{1,0:T(8,128)(2,1)} %get-tuple-element.36) | data formatting | bytes 1179648
  134.0 0.0 copy-done
  134.0 0.0 copy-start.3
  134.0 0.0 copy-start.4
  134.1 0.0 copy-start.2
  134.1 1.0 copy.32
  135.1 0.1 copy-done.3
  135.2 0.0 copy-start.1
  135.2 0.0 copy-start.6
  135.2 0.0 copy-start.5
  135.2 0.0 copy-start.7
  135.2 0.7 copy.33
  135.9 0.0 copy-done.4
  135.9 0.6 copy.34
  136.5 0.0 copy-done.2
  136.5 0.7 copy.35
  137.2 0.0 copy-done.1
  137.2 0.7 copy.36
  138.0 0.0 copy-done.6
  138.0 0.6 copy.37
  138.6 0.0 copy-done.5
  138.6 0.6 copy.38
  139.1 0.0 copy-done.7
  139.2 0.6 copy.39
Async XLA Ops:
  132.0 2.0 %copy-start = (f32[384,768]{1,0:T(8,128)S(1)}, f32[384,768]{1,0:T(8,128)}, u32[]{:S(2)}) copy-start(f32[384,768]{1,0:T(8,128)} %get-tuple-element.37) | copy-start | bytes 3538948
  134.0 1.1 copy-start.3
  134.0 1.8 %copy-start.4 = (f32[192,96]{1,0:T(8,128)S(1)}, f32[192,96]{1,0:T(8,128)}, u32[]{:S(2)}) copy-start(f32[192,96]{1,0:T(8,128)} %get-tuple-element.39) | copy-start | bytes 221188
  134.1 2.5 %copy-start.2 = (f32[96,768]{1,0:T(8,128)S(1)}, f32[96,768]{1,0:T(8,128)}, u32[]{:S(2)}) copy-start(f32[96,768]{1,0:T(8,128)} %get-tuple-element.40) | copy-start | bytes 884740
  135.2 2.1 %copy-start.1 = (f32[96,768]{1,0:T(8,128)S(1)}, f32[96,768]{1,0:T(8,128)}, u32[]{:S(2)}) copy-start(f32[96,768]{1,0:T(8,128)} %get-tuple-element.23) | copy-start | bytes 884740
  135.2 2.8 %copy-start.6 = (f32[768]{0:T(1024)S(1)}, f32[768]{0:T(1024)}, u32[]{:S(2)}) copy-start(f32[768]{0:T(1024)} %get-tuple-element.42) | copy-start | bytes 9220
  135.2 3.4 %copy-start.5 = (f32[768]{0:T(1024)S(1)}, f32[768]{0:T(1024)}, u32[]{:S(2)}) copy-start(f32[768]{0:T(1024)} %get-tuple-element.43) | copy-start | bytes 9220
  135.2 4.0 %copy-start.7 = (f32[3,96]{1,0:T(4,128)S(1)}, f32[3,96]{1,0:T(4,128)}, u32[]{:S(2)}) copy-start(f32[3,96]{1,0:T(4,128)} %get-tuple-element.26) | copy-start | bytes 3460

commit v6 on v5

--- a/solution.py
+++ b/solution.py
@@ -140,8 +140,8 @@
     def block(self, c, core, y):
         return (c * 2 + core) * 2 + y
 
-    def put(self, c, m, value):
-        self.part[run(self.block(c, m % 2, m // 2)), :] = value.astype(bf16)
+    def put(self, c, m, value, columns=slice(None)):
+        self.part[run(self.block(c, m % 2, m // 2)), columns] = value.astype(bf16)
 
     def first(self, c):
         _, _, core, sibling, _ = mp_places()
@@ -394,8 +394,8 @@
 
     def window(m, c):
         block = m * chunks + c
-        start = jnp.clip(block - 1, 0, blocks - 3)
-        return start, start - block + 2
+        start = min(max(block - 1, 0), blocks - 3)
+        return range(start, start + 3), 2 - block
 
 
     expanded = dot(tables_ref[...], expansion())
@@ -534,26 +534,30 @@
             es_ref[run(c * 3 + d - 1, 1, size), :] = of((mp + d) % 4)
         grad_att.start(c)
 
-    def attend(t, carry):
-        c = t // heads
-        h = t % heads
+    def attend(c, h, carry):
         query_far = jnp.concatenate([qa_ref[h, place(m, c), :] for m in range(pieces)], axis=0)
         query_near = jnp.concatenate([qb_ref[h, place(m, c), :] for m in range(pieces)], axis=0)
         query = jnp.concatenate([query_far, query_near], axis=1)
+        tops, mixes = [], []
         for j in range(chunks):
             cols = slice(j * CHUNK, (j + 1) * CHUNK)
-            s_ref[cols, :] = dot(query, jnp.concatenate([hot_t_ref[:, cols], kt2_ref[h, :, cols]], axis=0))
-        for m in range(pieces):
-            start, of = window(m, c)
-            for i in range(3):
-                panel = (start + i) // pieces
-                s_ref[run(panel * 4 + m), run((start + i) % pieces)] += band_ref[h, :, run(of + i)].astype(f32)
-        panels = [s_ref[j * CHUNK : (j + 1) * CHUNK, :] for j in range(chunks)]
-        top = jnp.max(functools.reduce(jnp.maximum, panels), axis=1, keepdims=True)
-        mixed = jnp.zeros((CHUNK, BLOCK), f32)
-        for j in range(chunks):
-            weights = jnp.exp(panels[j] - top).astype(bf16)
-            mixed = mixed + dot(weights, v_ref[h, j * CHUNK : (j + 1) * CHUNK, :])
+            s = dot(query, jnp.concatenate([hot_t_ref[:, cols], kt2_ref[h, :, cols]], axis=0))
+            lines = []
+            for m in range(pieces):
+                near, shift = window(m, c)
+                tiles = []
+                for b in range(pieces):
+                    tile = s[m * BLOCK : (m + 1) * BLOCK, b * BLOCK : (b + 1) * BLOCK]
+                    if j * pieces + b in near:
+                        at = (j * pieces + b + shift) * BLOCK
+                        tile = tile + band_ref[h, :, at : at + BLOCK].astype(f32)
+                    tiles.append(tile)
+                lines.append(jnp.concatenate(tiles, axis=1))
+            s = jnp.concatenate(lines, axis=0)
+            tops.append(jnp.max(s, axis=1, keepdims=True))
+            mixes.append(dot(jnp.exp(s - tops[j]).astype(bf16), v_ref[h, cols, :]))
+        top = functools.reduce(jnp.maximum, tops)
+        mixed = sum(mix * jnp.exp(part - top) for mix, part in zip(mixes, tops))
         res_ref[run(h, 1, CHUNK), :] = jnp.where(low, mixed / pltpu.roll(mixed, 64, 1), 0.0)
         high, middle, rest = split3(-(top + jnp.log(mixed[:, 64:65])))
         second = jnp.where(
@@ -564,29 +568,24 @@
         qt_ref[h, c, :BLOCK, :] = query_far.astype(f32).T.astype(bf16)
         qt_ref[h, c, BLOCK:, :] = second.T.astype(bf16)
 
-        @pl.when(h == heads - 1)
-        def _():
-            pairs = []
-            for g in range(0, heads, 2):
-                pair = res_ref[g * CHUNK : (g + 1) * CHUNK, :]
-                if g + 1 < heads:
-                    pair = jnp.where(low, pair, pltpu.roll(res_ref[(g + 1) * CHUNK : (g + 2) * CHUNK, :], 64, 1))
-                pairs.append(pair.astype(bf16))
-            merged = jnp.concatenate(pairs, axis=1)
-            att_ref[run(c, 1, CHUNK), :] = merged
-            share_attended(c)
-
-        @pl.when(t == 4)
-        def _():
-            att.forward(0)
-
-        @pl.when(t == 7)
-        def _():
-            att.forward(1)
+        if c > 0:
+
+            @pl.when(h == 1)
+            def _():
+                att.forward(c - 1)
 
         return carry
 
-    lax.fori_loop(0, chunks * heads, attend, 0)
+    for c in range(chunks):
+        lax.fori_loop(0, heads, functools.partial(attend, c), 0)
+        pairs = []
+        for g in range(0, heads, 2):
+            pair = res_ref[g * CHUNK : (g + 1) * CHUNK, :]
+            if g + 1 < heads:
+                pair = jnp.where(low, pair, pltpu.roll(res_ref[(g + 1) * CHUNK : (g + 2) * CHUNK, :], 64, 1))
+            pairs.append(pair.astype(bf16))
+        att_ref[run(c, 1, CHUNK), :] = jnp.concatenate(pairs, axis=1)
+        share_attended(c)
     for load in loads[3:-1]:
         load.wait()
     wo.finish(0)
@@ -614,27 +613,17 @@
         grad_low = (slope * grad_act).astype(bf16)
         low_ref[run(c, 1, CHUNK), at] = activated
         grad_low_ref[run(c, 1, CHUNK), at] = grad_low
-        part_ffn = dot(activated, w_outer_ref[at, :])
-        part_norm = dot_nt(grad_low, w_inner_ref[:, at])
-
-        @pl.when(b == 0)
-        def _():
-            for p in range(chunks):
-                s_ref[p * CHUNK : (p + 1) * CHUNK, :256] = part_ffn[:, p * 256 : (p + 1) * 256]
-                s_ref[p * CHUNK : (p + 1) * CHUNK, 256:] = part_norm[:, p * 256 : (p + 1) * 256]
-
-        @pl.when(b > 0)
-        def _():
-            for p in range(chunks):
-                s_ref[p * CHUNK : (p + 1) * CHUNK, :256] += part_ffn[:, p * 256 : (p + 1) * 256]
-                s_ref[p * CHUNK : (p + 1) * CHUNK, 256:] += part_norm[:, p * 256 : (p + 1) * 256]
 
         @pl.when(b == steps - 1)
         def _():
-            for m in range(pieces):
-                parts = [s_ref[p * CHUNK + m * BLOCK : p * CHUNK + (m + 1) * BLOCK, :] for p in range(chunks)]
-                feed.put(c, m, jnp.concatenate([p[:, :256] for p in parts], axis=1))
-                norm.put(c, m, jnp.concatenate([p[:, 256:] for p in parts], axis=1))
+            chunk_rows = run(c, 1, CHUNK)
+            for p in range(model // 256):
+                cols = slice(p * 256, (p + 1) * 256)
+                part_norm = dot_nt(grad_low_ref[chunk_rows, :], w_inner_ref[cols, :])
+                part_ffn = dot(low_ref[chunk_rows, :], w_outer_ref[:, cols])
+                for m in range(pieces):
+                    norm.put(c, m, part_norm[m * BLOCK : (m + 1) * BLOCK], cols)
+                    feed.put(c, m, part_ffn[m * BLOCK : (m + 1) * BLOCK], cols)
             norm.start(c)
 
         @pl.when(t == 1)
@@ -726,49 +715,23 @@
     def mix(k):
         mixed_ref[run(k), :] = (hidden_ref[run(k), :] + feed.finish(k)).astype(bf16)
 
-    def head(h, carry):
-        dk_ref[...] = jnp.zeros_like(dk_ref)
-        dv_ref[...] = jnp.zeros_like(dv_ref)
-        bands_ref[...] = jnp.zeros_like(bands_ref)
-
-        def chunk(c, carry):
+    def events(h, c):
+        if c == 0:
+
             @pl.when(h == 0)
             def _():
-                receive(c)
-
-            at = run(c, 1, CHUNK)
-            s_ref[...] = dot(jnp.concatenate([hot_ref[...], k2_ref[h]], axis=1), qt_ref[h, c])
-            for m in range(pieces):
-                start, of = window(m, c)
-                s_ref[run(start, 3), m * BLOCK : (m + 1) * BLOCK] += band_t_ref[h, run(of, 3), :].astype(f32)
-            probs = jnp.exp(s_ref[...])
-            low_ref[:, :CHUNK] = probs.astype(bf16)
-            grad_low_ref[:, :CHUNK] = (probs * dot(v_ref[h], dat_ref[h, :, at])).astype(bf16)
-            probs_t = low_ref[:, :CHUNK]
-            grad_t = grad_low_ref[:, :CHUNK]
-            dv_ref[...] += dot(probs_t, da_ref[h, at, :])
-            dk_ref[...] += dot(grad_t, jnp.concatenate([qb_ref[h, place(m, c), :] for m in range(pieces)], axis=0))
-            dq_far = dot(hot_t_ref[...], grad_t)
-            dq_near = dot(kt2_ref[h], grad_t)
-            for m in range(pieces):
-                dqt_ref[:BLOCK, place(m, c)] = dq_far[:, m * BLOCK : (m + 1) * BLOCK]
-                dqt_ref[BLOCK:, place(m, c)] = dq_near[:, m * BLOCK : (m + 1) * BLOCK]
-                start, of = window(m, c)
-                bands_ref[run(of, 3), :] += grad_low_ref[run(start, 3), m * BLOCK : (m + 1) * BLOCK].astype(f32)
-
-            def when(head_index, chunk_index):
-                return pl.when((h == head_index) & (c == chunk_index))
-
-            @when(0, 0)
-            def _():
                 grad_of(2)
 
-            @when(0, 1)
+        if c == 1:
+
+            @pl.when(h == 0)
             def _():
                 for k in range(chunks):
                     grads.start(k)
 
-            @when(0, 2)
+        if c == 2:
+
+            @pl.when(h == 0)
             def _():
                 for k in range(chunks):
                     feed.start(k)
@@ -776,28 +739,38 @@
                     outer.middle()
                     inner.start()
 
-            @when(1, 0)
+        if c == 0:
+
+            @pl.when(h == 1)
             def _():
                 grads.forward(0)
 
-            @when(1, 1)
+        if c == 1:
+
+            @pl.when(h == 1)
             def _():
                 grads.forward(1)
                 if fast:
                     outer.third()
 
-            @when(1, 2)
+        if c == 2:
+
+            @pl.when(h == 1)
             def _():
                 grads.forward(2)
                 feed.middle(0)
 
-            @when(2, 0)
+        if c == 0:
+
+            @pl.when(h == 2)
             def _():
                 feed.middle(1)
                 if fast:
                     inner.middle()
 
-            @when(2, 1)
+        if c == 1:
+
+            @pl.when(h == 2)
             def _():
                 feed.middle(2)
                 mix(0)
@@ -805,7 +778,9 @@
                     qkv(0).middle()
                     o_outer_ref[...] = outer.finish()
 
-            @when(2, 2)
+        if c == 2:
+
+            @pl.when(h == 2)
             def _():
                 mix(1)
                 if fast:
@@ -814,9 +789,47 @@
                     qkv(0).third()
                     qkv(1).middle()
 
-            return carry
-
-        lax.fori_loop(0, chunks, chunk, 0)
+    def head(h, carry):
+        dk_ref[...] = jnp.zeros_like(dk_ref)
+        dv_ref[...] = jnp.zeros_like(dv_ref)
+        bands_ref[...] = jnp.zeros_like(bands_ref)
+
+        for c in range(chunks):
+
+            @pl.when(h == 0)
+            def _(c=c):
+                receive(c)
+
+            at = slice(c * CHUNK, (c + 1) * CHUNK)
+            query = jnp.concatenate([qb_ref[h, place(m, c), :] for m in range(pieces)], axis=0)
+            for j in range(chunks):
+                keys = slice(j * CHUNK, (j + 1) * CHUNK)
+                s = dot(jnp.concatenate([hot_ref[keys, :], k2_ref[h, keys, :]], axis=1), qt_ref[h, c])
+                columns = []
+                for m in range(pieces):
+                    near, shift = window(m, c)
+                    tiles = []
+                    for b in range(pieces):
+                        tile = s[b * BLOCK : (b + 1) * BLOCK, m * BLOCK : (m + 1) * BLOCK]
+                        if j * pieces + b in near:
+                            of = (j * pieces + b + shift) * BLOCK
+                            tile = tile + band_t_ref[h, of : of + BLOCK, :].astype(f32)
+                        tiles.append(tile)
+                    columns.append(jnp.concatenate(tiles, axis=0))
+                probs = jnp.exp(jnp.concatenate(columns, axis=1))
+                probs_t = probs.astype(bf16)
+                grad_t = (probs * dot(v_ref[h, keys, :], dat_ref[h, :, at])).astype(bf16)
+                grad_low_ref[keys, :CHUNK] = grad_t
+                dv_ref[keys, :] += dot(probs_t, da_ref[h, at, :])
+                dk_ref[keys, :] += dot(grad_t, query)
+            dq = dot(jnp.concatenate([hot_t_ref[...], kt2_ref[h]], axis=0), grad_low_ref[:, :CHUNK])
+            for m in range(pieces):
+                dqt_ref[:, place(m, c)] = dq[:, m * BLOCK : (m + 1) * BLOCK]
+                near, shift = window(m, c)
+                of = slice((near.start + shift) * BLOCK, (near.stop + shift) * BLOCK)
+                keys = slice(near.start * BLOCK, near.stop * BLOCK)
+                bands_ref[of, :] += grad_low_ref[keys, m * BLOCK : (m + 1) * BLOCK].astype(f32)
+            events(h, c)
 
         dq = dqt_ref[BLOCK:, :].T * 0.125
         grads_of = run(h, 1, 256)

time: 140 us -> 134 us (0.957)
  Pallas kernels: 131 us -> 125 us
    pallas_call x1, Pallas kernels: 131 us -> 125 us  [local(): pl.pallas_call(functools.partial(layer_kernel, fast), in_specs=[pl.BlockS...]
where the time goes in v6:
time: 134 us
  Pallas kernels  125 us (93%)
  local copies, waits for them, and re-layouts  7.68 us (6%)
    pallas_call x1, Pallas kernels, local(): pl.pallas_call(functools.partial(layer_kernel, fast), in_specs=[pl.BlockS...  125 us
    unnamed x25, local copies, waits for them, and re-layouts  7.68 us

profile of v6, /device:TPU:0, one launch (start us, length us, event | category | flops | bytes accessed | tf_op | source)
XLA Modules:
  0.0 134.0 jit_solution(6681040302215597430)
XLA Ops:
  1.3 125.0 %layer.1 = (bf16[384,768]{1,0:T(8,128)(2,1)}, f32[384,768]{1,0:T(8,128)}, f32[3,96,192]{2,1,0:T(8,128)}, f32[192,96]{1,0:T(8,128)}, f32[96,768]{1,0:T(8,128)}, /...) custom-call(s32[1]{0:T(128)S(6)} %copy.30.length_ref, s32[1536]{0:T(1024)} %across_ref.1, ...), custom_call_target="tpu_custom_call" | custom-call | tf_op jit(solution)/shard_map/layer/pallas_call | solution.py:1036
  126.3 0.0 copy-start
  126.3 2.0 %copy.31 = bf16[384,768]{1,0:T(8,128)(2,1)} copy(bf16[384,768]{1,0:T(8,128)(2,1)} %get-tuple-element.36) | data formatting | bytes 1179648
  128.4 0.0 copy-done
  128.4 0.0 copy-start.3
  128.4 0.0 copy-start.4
  128.4 0.0 copy-start.2
  128.4 1.0 copy.32
  129.4 0.1 copy-done.3
  129.5 0.0 copy-start.1
  129.5 0.0 copy-start.6
  129.5 0.0 copy-start.5
  129.5 0.0 copy-start.7
  129.5 0.7 copy.33
  130.2 0.0 copy-done.4
  130.2 0.6 copy.34
  130.8 0.0 copy-done.2
  130.8 0.7 copy.35
  131.6 0.0 copy-done.1
  131.6 0.7 copy.36
  132.3 0.0 copy-done.6
  132.3 0.6 copy.37
  132.9 0.0 copy-done.5
  132.9 0.6 copy.38
  133.5 0.0 copy-done.7
  133.5 0.6 copy.39
Async XLA Ops:
  126.3 2.0 %copy-start = (f32[384,768]{1,0:T(8,128)S(1)}, f32[384,768]{1,0:T(8,128)}, u32[]{:S(2)}) copy-start(f32[384,768]{1,0:T(8,128)} %get-tuple-element.37) | copy-start | bytes 3538948
  128.4 1.1 copy-start.3
  128.4 1.8 %copy-start.4 = (f32[192,96]{1,0:T(8,128)S(1)}, f32[192,96]{1,0:T(8,128)}, u32[]{:S(2)}) copy-start(f32[192,96]{1,0:T(8,128)} %get-tuple-element.39) | copy-start | bytes 221188
  128.4 2.5 %copy-start.2 = (f32[96,768]{1,0:T(8,128)S(1)}, f32[96,768]{1,0:T(8,128)}, u32[]{:S(2)}) copy-start(f32[96,768]{1,0:T(8,128)} %get-tuple-element.40) | copy-start | bytes 884740
  129.5 2.1 %copy-start.1 = (f32[96,768]{1,0:T(8,128)S(1)}, f32[96,768]{1,0:T(8,128)}, u32[]{:S(2)}) copy-start(f32[96,768]{1,0:T(8,128)} %get-tuple-element.23) | copy-start | bytes 884740
  129.5 2.8 %copy-start.6 = (f32[768]{0:T(1024)S(1)}, f32[768]{0:T(1024)}, u32[]{:S(2)}) copy-start(f32[768]{0:T(1024)} %get-tuple-element.42) | copy-start | bytes 9220
  129.5 3.4 %copy-start.5 = (f32[768]{0:T(1024)S(1)}, f32[768]{0:T(1024)}, u32[]{:S(2)}) copy-start(f32[768]{0:T(1024)} %get-tuple-element.43) | copy-start | bytes 9220
  129.5 4.0 %copy-start.7 = (f32[3,96]{1,0:T(4,128)S(1)}, f32[3,96]{1,0:T(4,128)}, u32[]{:S(2)}) copy-start(f32[3,96]{1,0:T(4,128)} %get-tuple-element.26) | copy-start | bytes 3460

commit v7 on v6

--- a/solution.py
+++ b/solution.py
@@ -118,10 +118,9 @@
 
 def meet(fast):
     mp, dp = lax.axis_index("mp"), lax.axis_index("dp")
-    z, x = dp_places()
     others = [(dp, (mp + d) % 4) for d in (1, 2, 3)]
     if fast:
-        others.extend([(z * 2 + 1 - x, mp), (beside(z) * 2 + x, mp), ((z + 2) % 4 * 2 + x, mp)])
+        others.extend(((dp + d) % 8, mp) for d in range(1, 8))
     barrier = pltpu.get_barrier_semaphore()
     for other in others:
         pl.semaphore_signal(barrier, inc=1, device_id=other, device_id_type=pl.DeviceIdType.MESH)
@@ -288,33 +287,75 @@
             self.copy(kind).wait_send()
 
 
+class Direct:
+
+    def __init__(self, part, taken, send, recv):
+        self.part, self.taken, self.send, self.recv = part, taken, send, recv
+        self.each = part.shape[0] // 8
+
+    put = Spread.put
+
+    def at(self, index, count=1):
+        return run(index, count, self.each)
+
+    def block(self, dp):
+        return self.at(dp % 2 * 4 + dp // 2 % 2 * 2 + dp // 4)
+
+    def copy(self, d):
+        to = (lax.axis_index("dp") + d) % 8
+        src = self.part.at[self.block(to)]
+        return remote(src, self.taken.at[run(d - 1, 1, self.each)], self.send.at[d - 1], self.recv.at[d - 1], dp=to)
+
+    def start(self):
+        for d in (4, 3, 5, 2, 6, 1, 7):
+            self.copy(d).start()
+
+    def finish(self):
+        total = self.part[self.block(lax.axis_index("dp")), :].astype(f32)
+        for d in range(1, 8):
+            self.copy(d).wait_recv()
+            total = total + self.taken[run(d - 1, 1, self.each), :].astype(f32)
+        return total
+
+    def drain(self):
+        for d in range(1, 8):
+            self.copy(d).wait_send()
+
+
 class Total:
 
     def __init__(self, value, taken, send, recv):
         self.value, self.taken, self.send, self.recv = value, taken, send, recv
 
     def copy(self, kind):
-        z, x = dp_places()
-        _, _, _, sibling, across = mp_places()
-        mp = {3: sibling, 4: across}.get(kind)
-        dp = {0: z * 2 + 1 - x, 1: beside(z) * 2 + x, 2: (z + 2) % 4 * 2 + x}.get(kind)
-        return remote(self.value.at[kind], self.taken.at[kind], self.send.at[kind], self.recv.at[kind], mp, dp)
-
-    def start(self, value):
-        self.value[0] = value
-        self.copy(0).start()
-
-    def turn(self, kind):
-        self.copy(kind - 1).wait_recv()
-        self.value[kind] = self.value[kind - 1] + self.taken[kind - 1]
-        self.copy(kind).start()
+        mp, dp = lax.axis_index("mp"), lax.axis_index("dp")
+        send, recv = self.send.at[kind], self.recv.at[kind]
+        if kind < 7:
+            return remote(self.value.at[0], self.taken.at[kind], send, recv, dp=(dp + kind + 1) % 8)
+        return remote(self.value.at[1], self.taken.at[kind], send, recv, mp=(mp + kind - 6) % 4)
+
+    def start(self):
+        for kind in range(7):
+            self.copy(kind).start()
+
+    def turn(self):
+        total = self.value[0]
+        for kind in range(7):
+            self.copy(kind).wait_recv()
+            total = total + self.taken[kind]
+        self.value[1] = total
+        for kind in range(7, 10):
+            self.copy(kind).start()
 
     def finish(self):
-        self.copy(4).wait_recv()
-        return self.value[4] + self.taken[4]
+        total = self.value[1]
+        for kind in range(7, 10):
+            self.copy(kind).wait_recv()
+            total = total + self.taken[kind]
+        return total
 
     def drain(self):
-        for kind in range(5):
+        for kind in range(10):
             self.copy(kind).wait_send()
 
 
@@ -332,7 +373,7 @@
     (
         x1, w_qkv_ref, w_inner_ref, w_outer_ref, cot_ref, load_sem,
         codes_ref, plane_ref, hot_ref, hot_t_ref, qa_ref, qb_ref, k2_ref, kt2_ref, v_ref, band_ref, band_t_ref, qt_ref,
-        s_ref, res_ref, dv_ref, dqt_ref, bands_ref, dat_ref, sums_ref, gain_sum_ref,
+        s_ref, res_ref, dv_ref, dqt_ref, bands_ref, dat_ref, sums_ref, gain_sum_ref, collapse_ref,
         att_ref, af_ref, att_send, att_recv,
         es_ref, ga_ref, es_send, es_recv,
         wo_ref, wo_send, wo_recv,
@@ -365,7 +406,8 @@
         outer = Spread(w_outer_ref, *spreads[0:5])
         inner = Spread(*spreads[5:11])
         output = Spread(*spreads[11:17])
-        small = Total(*spreads[23:27])
+        qkv_last = Direct(*spreads[23:27])
+        small = Total(*spreads[27:31])
 
         def qkv(h):
             return Spread(*[ref.at[h] for ref in spreads[17:23]])
@@ -479,6 +521,7 @@
     wo.forward(0)
     gain_sum_ref[...] = jnp.zeros_like(gain_sum_ref)
     sums_ref[...] = jnp.zeros_like(sums_ref)
+    collapse_ref[...] = collapse()
 
     half_low = lax.broadcasted_iota(jnp.int32, (CHUNK // 2, BLOCK), 1) < 64
     quarter_low = lax.broadcasted_iota(jnp.int32, (BLOCK // 2, BLOCK), 1) < 64
@@ -568,16 +611,12 @@
         qt_ref[h, c, :BLOCK, :] = query_far.astype(f32).T.astype(bf16)
         qt_ref[h, c, BLOCK:, :] = second.T.astype(bf16)
 
-        if c > 0:
-
-            @pl.when(h == 1)
-            def _():
-                att.forward(c - 1)
-
         return carry
 
     for c in range(chunks):
         lax.fori_loop(0, heads, functools.partial(attend, c), 0)
+        if c > 0:
+            att.forward(c - 1)
         pairs = []
         for g in range(0, heads, 2):
             pair = res_ref[g * CHUNK : (g + 1) * CHUNK, :]
@@ -626,7 +665,7 @@
                     feed.put(c, m, part_ffn[m * BLOCK : (m + 1) * BLOCK], cols)
             norm.start(c)
 
-        @pl.when(t == 1)
+        @pl.when(t == 2)
         def _():
             att.forward(2)
 
@@ -665,8 +704,10 @@
     if fast:
         outer.start()
     norm.middle(2)
+    weights_of(False)
+    if fast:
+        inner.start()
     grad_of(1)
-    weights_of(False)
     wt_ref[...] = jnp.zeros_like(wt_ref)
     for k in range(3):
         for h in range(heads):
@@ -715,79 +756,67 @@
     def mix(k):
         mixed_ref[run(k), :] = (hidden_ref[run(k), :] + feed.finish(k)).astype(bf16)
 
-    def events(h, c):
-        if c == 0:
-
-            @pl.when(h == 0)
-            def _():
-                grad_of(2)
-
-        if c == 1:
-
-            @pl.when(h == 0)
-            def _():
-                for k in range(chunks):
-                    grads.start(k)
-
-        if c == 2:
-
-            @pl.when(h == 0)
-            def _():
-                for k in range(chunks):
-                    feed.start(k)
-                if fast:
-                    outer.middle()
-                    inner.start()
-
-        if c == 0:
-
-            @pl.when(h == 1)
-            def _():
-                grads.forward(0)
-
-        if c == 1:
-
-            @pl.when(h == 1)
-            def _():
-                grads.forward(1)
-                if fast:
-                    outer.third()
-
-        if c == 2:
-
-            @pl.when(h == 1)
-            def _():
-                grads.forward(2)
-                feed.middle(0)
-
-        if c == 0:
-
-            @pl.when(h == 2)
-            def _():
-                feed.middle(1)
-                if fast:
-                    inner.middle()
-
-        if c == 1:
-
-            @pl.when(h == 2)
-            def _():
-                feed.middle(2)
-                mix(0)
-                if fast:
-                    qkv(0).middle()
-                    o_outer_ref[...] = outer.finish()
-
-        if c == 2:
-
-            @pl.when(h == 2)
-            def _():
-                mix(1)
-                if fast:
-                    inner.third()
-                    output.middle()
-                    qkv(0).third()
-                    qkv(1).middle()
+    def events(h, c, j):
+        due = {
+            (0, 0, 2): [lambda: grad_of(2)],
+            (0, 1, 2): [lambda: grads.start(0)],
+            (0, 2, 2): [lambda: grads.start(1)],
+            (1, 0, 2): [lambda: grads.forward(0), lambda: grads.start(2), lambda: grads.forward(1)],
+            (1, 1, 2): [lambda: feed.start(0), lambda: feed.start(1), lambda: feed.start(2)],
+            (1, 2, 2): [lambda: grads.forward(2), lambda: feed.middle(0), lambda: feed.middle(1)],
+            (2, 0, 2): [lambda: feed.middle(2)],
+            (2, 1, 2): [lambda: mix(0), lambda: mix(1)],
+            (2, 2, 2): [lambda: mix(2)],
+        }
+        if fast:
+            for at, what in {
+                (1, 1, 2): [outer.middle],
+                (1, 2, 2): [inner.middle],
+                (2, 0, 2): [outer.third, lambda: qkv(0).middle()],
+                (2, 1, 2): [inner.third, lambda: qkv(0).third()],
+                (2, 2, 2): [lambda: qkv(1).middle(), output.middle],
+            }.items():
+                due[at] = due.get(at, []) + what
+        for (head_due, chunk_due, panel_due), what in due.items():
+            if (chunk_due, panel_due) == (c, j):
+
+                @pl.when(h == head_due)
+                def _(what=what):
+                    for each in what:
+                        each()
+
+    def leave(h, spread):
+        grads_of = run(h, 1, 256)
+        for b in range(2):
+            cols = slice(b * half_model, (b + 1) * half_model)
+            grad_qkv = dot_tn(x1[:, cols], nf_ref[:, grads_of])
+            if fast:
+                spread.put(b * half_model, grad_qkv)
+            else:
+                o_qkv_ref[h, cols, :] = grad_qkv
+        if fast:
+            spread.start()
+
+    def leave_tables(h):
+        band = roll_rows(bands_ref[...].T, False)
+        spread = dqt_ref[:BLOCK, :]
+        high = spread.astype(bf16)
+        rest = (spread - high.astype(f32)).astype(bf16)
+        plane = (dot(high, hot_ref[...]) + dot(rest, hot_ref[...])).T
+        plane = jnp.where((square_rows < CODES) == (square_lanes < CODES), plane, 0.0)
+        plane = roll_rows(plane, False)
+        far = dqt_ref[BLOCK + FAR : BLOCK + FAR + 16, :]
+        line = jnp.concatenate(
+            [
+                jnp.sum(band, axis=0, keepdims=True),
+                jnp.sum(plane[:CODES], axis=0, keepdims=True),
+                jnp.sum(plane[CODES:], axis=0, keepdims=True),
+                fold(jnp.where(real & (lines16 < start16), far, 0.0)),
+                fold(jnp.where(real & (lines16 > start16 + 2), far, 0.0)),
+            ],
+            axis=1,
+        )
+        sums_ref[...] += jnp.where(lax.broadcasted_iota(jnp.int32, sums_ref.shape, 0) == h, line, 0.0)
 
     def head(h, carry):
         dk_ref[...] = jnp.zeros_like(dk_ref)
@@ -822,6 +851,8 @@
                 grad_low_ref[keys, :CHUNK] = grad_t
                 dv_ref[keys, :] += dot(probs_t, da_ref[h, at, :])
                 dk_ref[keys, :] += dot(grad_t, query)
+                if j < chunks - 1:
+                    events(h, c, j)
             dq = dot(jnp.concatenate([hot_t_ref[...], kt2_ref[h]], axis=0), grad_low_ref[:, :CHUNK])
             for m in range(pieces):
                 dqt_ref[:, place(m, c)] = dq[:, m * BLOCK : (m + 1) * BLOCK]
@@ -829,22 +860,18 @@
                 of = slice((near.start + shift) * BLOCK, (near.stop + shift) * BLOCK)
                 keys = slice(near.start * BLOCK, near.stop * BLOCK)
                 bands_ref[of, :] += grad_low_ref[keys, m * BLOCK : (m + 1) * BLOCK].astype(f32)
-            events(h, c)
+            events(h, c, chunks - 1)
 
         dq = dqt_ref[BLOCK:, :].T * 0.125
         grads_of = run(h, 1, 256)
         nf_ref[:, grads_of] = jnp.concatenate(
             [jnp.where(tall_low, dq, pltpu.roll(dk_ref[...], 64, 1)), jnp.where(tall_low, dv_ref[...], 0.0)], axis=1
         ).astype(bf16)
-        for b in range(2):
-            cols = slice(b * half_model, (b + 1) * half_model)
-            grad_qkv = dot_tn(x1[:, cols], nf_ref[:, grads_of])
-            if fast:
-                qkv(h).put(b * half_model, grad_qkv)
-            else:
-                o_qkv_ref[h, cols, :] = grad_qkv
-        if fast:
-            qkv(h).start()
+
+        @pl.when(h < heads - 1)
+        def _():
+            leave(h, qkv(h) if fast else None)
+            leave_tables(h)
 
         @pl.when(h == 1)
         def _():
@@ -860,35 +887,16 @@
             if fast:
                 output.start()
 
-        band = roll_rows(bands_ref[...].T, False)
-        spread = dqt_ref[:BLOCK, :]
-        high = spread.astype(bf16)
-        rest = (spread - high.astype(f32)).astype(bf16)
-        plane = (dot(high, hot_ref[...]) + dot(rest, hot_ref[...])).T
-        plane = jnp.where((square_rows < CODES) == (square_lanes < CODES), plane, 0.0)
-        plane = roll_rows(plane, False)
-        far = dqt_ref[BLOCK + FAR : BLOCK + FAR + 16, :]
-        line = jnp.concatenate(
-            [
-                jnp.sum(band, axis=0, keepdims=True),
-                jnp.sum(plane[:CODES], axis=0, keepdims=True),
-                jnp.sum(plane[CODES:], axis=0, keepdims=True),
-                fold(jnp.where(real & (lines16 < start16), far, 0.0)),
-                fold(jnp.where(real & (lines16 > start16 + 2), far, 0.0)),
-            ],
-            axis=1,
-        )
-        sums_ref[...] += jnp.where(lax.broadcasted_iota(jnp.int32, sums_ref.shape, 0) == h, line, 0.0)
         return carry
 
     lax.fori_loop(0, heads, head, 0)
 
-    mix(2)
     credits = [(sibling, credit.at[0]), (across, credit.at[1])]
     for other, sem in credits:
         pl.semaphore_signal(
             sem, inc=1, device_id=(lax.axis_index("dp"), other), device_id_type=pl.DeviceIdType.MESH
         )
+    leave(heads - 1, qkv_last if fast else None)
     loads[-1].start()
     for c in range(chunks):
         norm.drain(c)
@@ -905,18 +913,23 @@
         last.start(c)
         if c > 0:
             last.middle(c - 1)
-    sums_ref[3:4, :model] = gain_total / gain_a
-    sums_ref[4:5, :model] = gain_sum_ref[0:1, :]
+    leave_tables(heads - 1)
+    last.middle(chunks - 1)
+    gain_total = gain_total / gain_a
+    tables = sum(dot_nt(part.astype(bf16), collapse_ref[...]) for part in split3(sums_ref[...]))[:heads]
     if fast:
-        small.start(sums_ref[...])
+        lines = model // BLOCK
+        small.value[0] = jnp.zeros_like(small.value[0])
+        for i in range(lines):
+            lane = slice(i * BLOCK, (i + 1) * BLOCK)
+            small.value[0, i : i + 1, :] = gain_total[:, lane]
+            small.value[0, lines + i : lines + i + 1, :] = gain_sum_ref[0:1, lane]
+        small.value[0, 2 * lines : 2 * lines + heads, : 3 * BUCKETS] = tables
+        small.start()
         output.third()
         qkv(1).third()
-    last.middle(chunks - 1)
-    if fast:
-        qkv(2).middle()
-        small.turn(1)
-        o_inner_ref[...] = inner.finish()
-        small.turn(2)
+        o_outer_ref[...] = outer.finish()
+        small.turn()
         o_output_ref[...] = output.finish()[:, :width].T
     loads[-1].wait()
     for c in range(chunks):
@@ -927,14 +940,11 @@
         scaled = grad_normed * gain_a
         back = factor * (scaled - hat * jnp.mean(scaled * hat, axis=-1, keepdims=True))
         input_ref[run(c), :] += back
-        if fast and c == 0:
-            small.turn(3)
-            qkv(2).third()
-        if fast and c == 1:
-            small.turn(4)
+    if fast:
+        o_inner_ref[...] = inner.finish()
     if fast:
         low_each = lax.broadcasted_iota(jnp.int32, (model // 8, BLOCK), 1) < 64
-        parts = [qkv(h).finish() for h in range(heads)]
+        parts = [(qkv(h) if h < heads - 1 else qkv_last).finish() for h in range(heads)]
         for k in range(3):
             for h in range(0, heads, 2):
                 at = slice(0, BLOCK) if k < 2 else slice(BLOCK, 2 * BLOCK)
@@ -947,19 +957,22 @@
                 else:
                     o_qkv_ref[k, :, h * 64 :] = one[:, :64]
         totals = small.finish()
-        o_gain_a_ref[...] = totals[3:4, :model].reshape(model)
-        o_gain_f_ref[...] = totals[4:5, :model].reshape(model)
-        buckets = collapse()
-        tables = sum(dot_nt(part.astype(bf16), buckets) for part in split3(small.value[3]))
-        o_tables_ref[...] = tables[:heads]
+        for i in range(lines):
+            o_gain_a_ref[i * BLOCK : (i + 1) * BLOCK] = totals[i : i + 1].reshape(BLOCK)
+            o_gain_f_ref[i * BLOCK : (i + 1) * BLOCK] = totals[lines + i : lines + i + 1].reshape(BLOCK)
+        o_tables_ref[...] = small.value[1, 2 * lines : 2 * lines + heads, : 3 * BUCKETS]
         outer.drain()
         inner.drain()
         output.drain()
-        for h in range(heads):
+        for h in range(heads - 1):
             qkv(h).drain()
+        qkv_last.drain()
         small.drain()
     else:
-        o_sums_ref[...] = sums_ref[...]
+        o_sums_ref[...] = jnp.zeros_like(o_sums_ref)
+        o_sums_ref[0:1, :] = gain_total
+        o_sums_ref[1:2, :] = gain_sum_ref[0:1, :]
+        o_sums_ref[2 : 2 + heads, : 3 * BUCKETS] = tables
     wo.drain(0)
     for c in range(chunks):
         for each in (att, grad_att, grads, feed, last):
@@ -975,6 +988,23 @@
         pltpu.SemaphoreType.DMA((*lead, 3)),
         pltpu.SemaphoreType.DMA((*lead, 3)),
     ]
+
+
+def hand_over_kernel(*refs):
+    count = len(refs) // 2
+    for i in range(count):
+        refs[count + i][...] = refs[i][...]
+
+
+def hand_over(results):
+    full = pl.BlockSpec(memory_space=pltpu.VMEM)
+    return pl.pallas_call(
+        hand_over_kernel,
+        in_specs=[full] * len(results),
+        out_specs=[full] * len(results),
+        out_shape=[jax.ShapeDtypeStruct(each.shape, each.dtype) for each in results],
+        name="hand_over",
+    )(*results)
 
 
 def local(
@@ -1003,9 +1033,9 @@
         vmem(heads, rows, BLOCK), vmem(heads, rows, BLOCK), vmem(heads, BLOCK, rows), vmem(heads, rows, BLOCK),
         vmem(heads, BLOCK, WIDE), vmem(heads, WIDE, BLOCK),
         vmem(heads, chunks, 256, CHUNK),
-        vmem(rows, CHUNK, dtype=f32), vmem(heads * CHUNK, BLOCK, dtype=f32), vmem(rows, BLOCK, dtype=f32),
+        vmem(CHUNK, 256, dtype=f32), vmem(heads * CHUNK, BLOCK, dtype=f32), vmem(rows, BLOCK, dtype=f32),
         vmem(256, rows, dtype=f32), vmem(WIDE, BLOCK, dtype=f32), vmem(heads, BLOCK, rows),
-        vmem(*sums, dtype=f32), vmem(8, model, dtype=f32),
+        vmem(*sums, dtype=f32), vmem(8, model, dtype=f32), vmem(3 * BUCKETS, sums[1]),
         vmem(rows, 256), vmem(6 * rows, BLOCK), dma(chunks, 3), dma(chunks, 3),
         vmem(chunks * 9 * BLOCK // 2, BLOCK), vmem(chunks * 6 * BLOCK, BLOCK), dma(chunks, 3), dma(chunks, 3),
         vmem(4 * width, model), dma(1, 3), dma(1, 3),
@@ -1024,12 +1054,13 @@
         ]
         scratch += [
             *spread_scratch(each, units, own_part=False), *spread_scratch(each, units), *spread_scratch(each, 256),
-            *spread_scratch(each, 256, lead=(heads,)),
-            vmem(5, *sums, dtype=f32), vmem(5, *sums, dtype=f32), dma(5), dma(5),
+            *spread_scratch(each, 256, lead=(heads - 1,)),
+            vmem(8 * each, 256), vmem(7 * each, 256), dma(7), dma(7),
+            vmem(2, 16, BLOCK, dtype=f32), vmem(10, 16, BLOCK, dtype=f32), dma(10), dma(10),
         ]
     else:
         outs += [
-            ((heads, model, 256), f32), ((model, width), f32), ((model, units), f32), ((model, units), f32), (sums, f32),
+            ((heads, model, 256), f32), ((model, width), f32), ((model, units), f32), ((model, units), f32), ((8, model), f32),
         ]
     full = pl.BlockSpec(memory_space=pltpu.VMEM)
     anywhere = pl.BlockSpec(memory_space=pl.ANY)
@@ -1046,17 +1077,12 @@
         tokens, jnp.swapaxes(w_qkv, 1, 2), w_output, w_inner, w_outer, cotangent,
     )
     if fast:
-        mixed, input_grad, qkv, output, inner, outer, gain_a, gain_f, tables = results
+        mixed, input_grad, qkv, output, inner, outer, gain_a, gain_f, tables = hand_over(results)
         return mixed, input_grad, qkv, output, inner, outer.T, gain_a, gain_f, tables.T
     mixed, input_grad, qkv, output, inner, outer, sums = results
     qkv = qkv[:, :, : 3 * 64].reshape(heads, model, 3, 64).transpose(2, 1, 0, 3).reshape(3, model, width)
-    gains = lax.psum(sums[3:5, :model], ("dp", "mp"))
-    tables = lax.dot_general(
-        collapse().astype(f32),
-        lax.psum(sums[:heads], "dp"),
-        (((1,), (1,)), ((), ())),
-        precision=lax.Precision.HIGHEST,
-    )
+    gains = lax.psum(sums[:2], ("dp", "mp"))
+    tables = lax.psum(sums[2 : 2 + heads, : 3 * BUCKETS], "dp").T
 
     def spread(x, axis):
         return lax.psum_scatter(x, "dp", scatter_dimension=axis, tiled=True)

time: 134 us -> 128 us (0.955)
  local copies, waits for them, and re-layouts: 7.68 us -> 0 us
    unnamed x25 -> x0, local copies, waits for them, and re-layouts: 7.68 us -> none
    pallas_call x0 -> x1, Pallas kernels: none -> 3.35 us  [hand_over(): pl.pallas_call(hand_over_kernel, in_specs=[full] * len(results), out_spec...]
    pallas_call x1, Pallas kernels: 125 us -> 123 us  [local(): pl.pallas_call(functools.partial(layer_kernel, fast), in_specs=[pl.BlockS...]
where the time goes in v7:
time: 128 us
  Pallas kernels  126 us (98%)
  between operations  1.37 us (1%)
    pallas_call x1, Pallas kernels, local(): pl.pallas_call(functools.partial(layer_kernel, fast), in_specs=[pl.BlockS...  123 us
    pallas_call x1, Pallas kernels, hand_over(): pl.pallas_call(hand_over_kernel, in_specs=[full] * len(results), out_spec...  3.35 us

profile of v7, /device:TPU:0, one launch (start us, length us, event | category | flops | bytes accessed | tf_op | source)
XLA Modules:
  0.0 127.7 jit_solution(456720883965660245)
XLA Ops:
  1.3 123.0 %layer.1 = (bf16[384,768]{1,0:T(8,128)(2,1)}, f32[384,768]{1,0:T(8,128)}, f32[3,96,192]{2,1,0:T(8,128)}, f32[192,96]{1,0:T(8,128)}, f32[96,768]{1,0:T(8,128)}, /...) custom-call(s32[1]{0:T(128)S(6)} %copy.21.length_ref, s32[1536]{0:T(1024)} %across_ref.1, ...), custom_call_target="tpu_custom_call" | custom-call | tf_op jit(solution)/shard_map/layer/pallas_call | solution.py:1067
  124.3 3.4 %hand_over.1 = (bf16[384,768]{1,0:T(8,128)(2,1)}, f32[384,768]{1,0:T(8,128)}, f32[3,96,192]{2,1,0:T(8,128)}, f32[192,96]{1,0:T(8,128)}, f32[96,768]{1,0:T(8,128)...) custom-call(bf16[384,768]{1,0:T(8,128)(2,1)} %get-tuple-element.27.refs_0_, ...), custom_call_target="tpu_custom_call" | custom-call | tf_op jit(solution)/shard_map/hand_over/pallas_call | solution.py:1001

commit v8 on v7

--- a/solution.py
+++ b/solution.py
@@ -124,7 +124,7 @@
     barrier = pltpu.get_barrier_semaphore()
     for other in others:
         pl.semaphore_signal(barrier, inc=1, device_id=other, device_id_type=pl.DeviceIdType.MESH)
-    pl.semaphore_wait(barrier, len(others))
+    return lambda: pl.semaphore_wait(barrier, len(others))
 
 
 def run(index, count=1, size=BLOCK):
@@ -376,7 +376,7 @@
         s_ref, res_ref, dv_ref, dqt_ref, bands_ref, dat_ref, sums_ref, gain_sum_ref, collapse_ref,
         att_ref, af_ref, att_send, att_recv,
         es_ref, ga_ref, es_send, es_recv,
-        wo_ref, wo_send, wo_recv,
+        wo_ref, wo_send, wo_recv, wo_t_ref,
         nf_ref,
         ghl_ref, ghl_send, ghl_recv,
         feed_part, feed_send, feed_recv, norm_part, norm_send, norm_recv, last_send, last_recv, near_ref, far_ref,
@@ -432,7 +432,7 @@
     ]
     for load in loads[:-1]:
         load.start()
-    meet(fast)
+    everyone_is_here = meet(fast)
 
     def window(m, c):
         block = m * chunks + c
@@ -456,6 +456,7 @@
             jnp.where((square_rows >= CODES) & (square_lanes >= CODES), upward, 0.0),
         )
         plane_ref[h] = plane.astype(bf16)
+    everyone_is_here()
     loads[2].wait()
     wo.start(0)
     loads[1].wait()
@@ -565,16 +566,21 @@
         grad_low = grad.astype(bf16)
         ghl_ref[grads.at(c, mp), :] = grad_low
 
-        def of(m):
-            value = dot_nt(grad_low, wo_ref[run(m, 1, width), :])
-            third = jnp.concatenate([value[:, BLOCK:], jnp.zeros((BLOCK, 64), f32)], axis=1)
+        size = BLOCK + BLOCK // 2
+        every = dot(grad_low, wo_t_ref[...])
+        for m in range(pieces):
+            third = every[:, m * 256 + BLOCK : (m + 1) * 256]
             third = jnp.where(quarter_low, third[: BLOCK // 2], pltpu.roll(third[BLOCK // 2 :], 64, 1))
-            return jnp.concatenate([value[:, :BLOCK], third], axis=0).astype(bf16)
-
-        size = BLOCK + BLOCK // 2
-        ga_ref[run(c * 4 + mp, 1, size), :] = of(mp)
-        for d in (1, 2, 3):
-            es_ref[run(c * 3 + d - 1, 1, size), :] = of((mp + d) % 4)
+            value = jnp.concatenate([every[:, m * 256 : m * 256 + BLOCK], third], axis=0).astype(bf16)
+
+            @pl.when(mp == m)
+            def _(value=value):
+                ga_ref[run(c * 4 + mp, 1, size), :] = value
+
+            @pl.when(mp != m)
+            def _(value=value, m=m):
+                es_ref[run(c * 3 + (m - mp + 4) % 4 - 1, 1, size), :] = value
+
         grad_att.start(c)
 
     def attend(c, h, carry):
@@ -617,6 +623,12 @@
         lax.fori_loop(0, heads, functools.partial(attend, c), 0)
         if c > 0:
             att.forward(c - 1)
+        if c == 1:
+            wo.finish(0)
+            for m in range(pieces):
+                turned = wo_ref[m * width : (m + 1) * width, :].astype(f32).T
+                wo_t_ref[:, m * 256 : m * 256 + width] = turned.astype(bf16)
+                wo_t_ref[:, m * 256 + width : (m + 1) * 256] = jnp.zeros((model, 256 - width), bf16)
         pairs = []
         for g in range(0, heads, 2):
             pair = res_ref[g * CHUNK : (g + 1) * CHUNK, :]
@@ -627,7 +639,11 @@
         share_attended(c)
     for load in loads[3:-1]:
         load.wait()
-    wo.finish(0)
+    outer_t = w_outer_ref[...].astype(f32).T.astype(bf16)
+    inner_t = w_inner_ref[...].astype(f32).T.astype(bf16)
+    for r in range(units // BLOCK):
+        qa_ref[r // 2, run(r % 2, 1, model), :] = outer_t[:, r * BLOCK : (r + 1) * BLOCK]
+        dat_ref[r // 2, :, r % 2 * model : (r % 2 + 1) * model] = inner_t[r * BLOCK : (r + 1) * BLOCK, :]
 
     steps = units // 256
 
@@ -643,7 +659,7 @@
         x = nf_ref[run(c, 1, CHUNK), :]
         cot = jnp.concatenate([cot_ref[place(m, c), :] for m in range(pieces)], axis=0)
         inner_units = dot(x, w_inner_ref[:, at])
-        grad_act = dot_nt(cot, w_outer_ref[at, :])
+        grad_act = dot(cot, jnp.concatenate([qa_ref[b, :model, :], qa_ref[b, model:, :]], axis=1))
         square = inner_units * inner_units
         tanh = jnp.tanh(ROOT * inner_units * (1.0 + CUBE * square))
         half = 0.5 * (1.0 + tanh)
@@ -658,7 +674,10 @@
             chunk_rows = run(c, 1, CHUNK)
             for p in range(model // 256):
                 cols = slice(p * 256, (p + 1) * 256)
-                part_norm = dot_nt(grad_low_ref[chunk_rows, :], w_inner_ref[cols, :])
+                turned = [
+                    dat_ref[r // 2, :, r % 2 * model + p * 256 : r % 2 * model + (p + 1) * 256] for r in range(units // BLOCK)
+                ]
+                part_norm = dot(grad_low_ref[chunk_rows, :], jnp.concatenate(turned, axis=0))
                 part_ffn = dot(low_ref[chunk_rows, :], w_outer_ref[:, cols])
                 for m in range(pieces):
                     norm.put(c, m, part_norm[m * BLOCK : (m + 1) * BLOCK], cols)
@@ -787,13 +806,11 @@
 
     def leave(h, spread):
         grads_of = run(h, 1, 256)
-        for b in range(2):
-            cols = slice(b * half_model, (b + 1) * half_model)
-            grad_qkv = dot_tn(x1[:, cols], nf_ref[:, grads_of])
-            if fast:
-                spread.put(b * half_model, grad_qkv)
-            else:
-                o_qkv_ref[h, cols, :] = grad_qkv
+        grad_qkv = dot_tn(nf_ref[:, grads_of], x1[...]).T
+        if fast:
+            spread.put(0, grad_qkv)
+        else:
+            o_qkv_ref[h] = grad_qkv
         if fast:
             spread.start()
 
@@ -877,13 +894,11 @@
         def _():
             for c in range(chunks):
                 grads.finish(c)
-            for b in range(2):
-                cols = slice(b * half_model, (b + 1) * half_model)
-                grad_output = dot_tn(ghl_ref[:, cols], att_ref[...])
-                if fast:
-                    output.put(b * half_model, grad_output)
-                else:
-                    o_output_ref[cols, :] = grad_output[:, :width]
+            grad_output = dot_tn(att_ref[...], ghl_ref[...]).T
+            if fast:
+                output.put(0, grad_output)
+            else:
+                o_output_ref[...] = grad_output[:, :width]
             if fast:
                 output.start()
 
@@ -902,11 +917,17 @@
         norm.drain(c)
     gain_total = jnp.zeros((1, model), f32)
     for c in range(chunks):
-        for m in range(pieces):
-            at = place(m, c)
-            partial = dot(nf_ref[at, :], wt_ref[...])
-            gain_total = gain_total + jnp.sum(partial * x1[at, :].astype(f32), axis=0, keepdims=True)
-            last.put(c, m, partial)
+        at = [place(m, c) for m in range(pieces)]
+        grad_rows = jnp.concatenate([nf_ref[rows_of, :] for rows_of in at], axis=0)
+        sums = []
+        for p in range(model // 256):
+            cols = slice(p * 256, (p + 1) * 256)
+            partial = dot(grad_rows, wt_ref[:, cols])
+            normed_rows = jnp.concatenate([x1[rows_of, cols] for rows_of in at], axis=0)
+            sums.append(jnp.sum(partial * normed_rows.astype(f32), axis=0, keepdims=True))
+            for m in range(pieces):
+                last.put(c, m, partial[m * BLOCK : (m + 1) * BLOCK], cols)
+        gain_total = gain_total + jnp.concatenate(sums, axis=1)
         if c == 0:
             for _, sem in credits:
                 pl.semaphore_wait(sem, 1)
@@ -1038,7 +1059,7 @@
         vmem(*sums, dtype=f32), vmem(8, model, dtype=f32), vmem(3 * BUCKETS, sums[1]),
         vmem(rows, 256), vmem(6 * rows, BLOCK), dma(chunks, 3), dma(chunks, 3),
         vmem(chunks * 9 * BLOCK // 2, BLOCK), vmem(chunks * 6 * BLOCK, BLOCK), dma(chunks, 3), dma(chunks, 3),
-        vmem(4 * width, model), dma(1, 3), dma(1, 3),
+        vmem(4 * width, model), dma(1, 3), dma(1, 3), vmem(model, 4 * 256),
         vmem(rows, model),
         vmem(rows, model), dma(chunks, 3), dma(chunks, 3),
         vmem(rows, model), dma(chunks, 2), dma(chunks, 2), vmem(rows, model), dma(chunks, 2), dma(chunks, 2),

time: 128 us -> 126 us (0.984)
    pallas_call x1, Pallas kernels: 123 us -> 121 us  [local(): pl.pallas_call(functools.partial(layer_kernel, fast), in_specs=[pl.BlockS...]
where the time goes in v8:
time: 126 us
  Pallas kernels  125 us (99%)
  between operations  1.37 us (1%)
    pallas_call x1, Pallas kernels, local(): pl.pallas_call(functools.partial(layer_kernel, fast), in_specs=[pl.BlockS...  121 us
    pallas_call x1, Pallas kernels, hand_over(): pl.pallas_call(hand_over_kernel, in_specs=[full] * len(results), out_spec...  3.35 us

profile of v8, /device:TPU:0, one launch (start us, length us, event | category | flops | bytes accessed | tf_op | source)
XLA Modules:
  0.0 126.0 jit_solution(9238940942897229321)
XLA Ops:
  1.3 121.2 %layer.1 = (bf16[384,768]{1,0:T(8,128)(2,1)}, f32[384,768]{1,0:T(8,128)}, f32[3,96,192]{2,1,0:T(8,128)}, f32[192,96]{1,0:T(8,128)}, f32[96,768]{1,0:T(8,128)}, /...) custom-call(s32[1]{0:T(128)S(6)} %copy.21.length_ref, s32[1536]{0:T(1024)} %across_ref.1, ...), custom_call_target="tpu_custom_call" | custom-call | tf_op jit(solution)/shard_map/layer/pallas_call | solution.py:1088
  122.5 3.4 %hand_over.1 = (bf16[384,768]{1,0:T(8,128)(2,1)}, f32[384,768]{1,0:T(8,128)}, f32[3,96,192]{2,1,0:T(8,128)}, f32[192,96]{1,0:T(8,128)}, f32[96,768]{1,0:T(8,128)...) custom-call(bf16[384,768]{1,0:T(8,128)(2,1)} %get-tuple-element.27.refs_0_, ...), custom_call_target="tpu_custom_call" | custom-call | tf_op jit(solution)/shard_map/hand_over/pallas_call | solution.py:1022

commit v9 on v8

--- a/solution.py
+++ b/solution.py
@@ -789,10 +789,11 @@
         }
         if fast:
             for at, what in {
-                (1, 1, 2): [outer.middle],
-                (1, 2, 2): [inner.middle],
-                (2, 0, 2): [outer.third, lambda: qkv(0).middle()],
-                (2, 1, 2): [inner.third, lambda: qkv(0).third()],
+                (0, 2, 2): [outer.middle],
+                (1, 1, 2): [outer.third, inner.middle],
+                (1, 2, 2): [lambda: qkv(0).middle()],
+                (2, 0, 2): [inner.third],
+                (2, 1, 2): [lambda: qkv(0).third()],
                 (2, 2, 2): [lambda: qkv(1).middle(), output.middle],
             }.items():
                 due[at] = due.get(at, []) + what

time: 126 us -> 122 us (0.968)
  Pallas kernels: 125 us -> 120 us
    pallas_call x1, Pallas kernels: 121 us -> 117 us  [local(): pl.pallas_call(functools.partial(layer_kernel, fast), in_specs=[pl.BlockS...]
where the time goes in v9:
time: 122 us
  Pallas kernels  120 us (98%)
  between operations  1.37 us (1%)
    pallas_call x1, Pallas kernels, local(): pl.pallas_call(functools.partial(layer_kernel, fast), in_specs=[pl.BlockS...  117 us
    pallas_call x1, Pallas kernels, hand_over(): pl.pallas_call(hand_over_kernel, in_specs=[full] * len(results), out_spec...  3.35 us

profile of v9, /device:TPU:0, one launch (start us, length us, event | category | flops | bytes accessed | tf_op | source)
XLA Modules:
  0.0 121.6 jit_solution(2289967754849303148)
XLA Ops:
  1.3 116.8 %layer.1 = (bf16[384,768]{1,0:T(8,128)(2,1)}, f32[384,768]{1,0:T(8,128)}, f32[3,96,192]{2,1,0:T(8,128)}, f32[192,96]{1,0:T(8,128)}, f32[96,768]{1,0:T(8,128)}, /...) custom-call(s32[1]{0:T(128)S(6)} %copy.21.length_ref, s32[1536]{0:T(1024)} %across_ref.1, ...), custom_call_target="tpu_custom_call" | custom-call | tf_op jit(solution)/shard_map/layer/pallas_call | solution.py:1089
  118.1 3.4 %hand_over.1 = (bf16[384,768]{1,0:T(8,128)(2,1)}, f32[384,768]{1,0:T(8,128)}, f32[3,96,192]{2,1,0:T(8,128)}, f32[192,96]{1,0:T(8,128)}, f32[96,768]{1,0:T(8,128)...) custom-call(bf16[384,768]{1,0:T(8,128)(2,1)} %get-tuple-element.27.refs_0_, ...), custom_call_target="tpu_custom_call" | custom-call | tf_op jit(solution)/shard_map/hand_over/pallas_call | solution.py:1023

commit v10 on v9

--- a/solution.py
+++ b/solution.py
@@ -792,8 +792,7 @@
                 (0, 2, 2): [outer.middle],
                 (1, 1, 2): [outer.third, inner.middle],
                 (1, 2, 2): [lambda: qkv(0).middle()],
-                (2, 0, 2): [inner.third],
-                (2, 1, 2): [lambda: qkv(0).third()],
+                (2, 0, 2): [inner.third, lambda: qkv(0).third()],
                 (2, 2, 2): [lambda: qkv(1).middle(), output.middle],
             }.items():
                 due[at] = due.get(at, []) + what

time: 122 us -> 123 us (level)
  no operation moved by 1% of the time
where the time goes in v10:
time: 123 us; the launch traced here: 122 us
  Pallas kernels  121 us (98%)
  between operations  1.37 us (1%)
    pallas_call x1, Pallas kernels, local(): pl.pallas_call(functools.partial(layer_kernel, fast), in_specs=[pl.BlockS...  118 us
    pallas_call x1, Pallas kernels, hand_over(): pl.pallas_call(hand_over_kernel, in_specs=[full] * len(results), out_spec...  3.35 us

profile of v10, /device:TPU:0, one launch (start us, length us, event | category | flops | bytes accessed | tf_op | source)
XLA Modules:
  0.0 122.3 jit_solution(10309057764198359390)
XLA Ops:
  1.3 117.6 %layer.1 = (bf16[384,768]{1,0:T(8,128)(2,1)}, f32[384,768]{1,0:T(8,128)}, f32[3,96,192]{2,1,0:T(8,128)}, f32[192,96]{1,0:T(8,128)}, f32[96,768]{1,0:T(8,128)}, /...) custom-call(s32[1]{0:T(128)S(6)} %copy.21.length_ref, s32[1536]{0:T(1024)} %across_ref.1, ...), custom_call_target="tpu_custom_call" | custom-call | tf_op jit(solution)/shard_map/layer/pallas_call | solution.py:1088
  118.9 3.4 %hand_over.1 = (bf16[384,768]{1,0:T(8,128)(2,1)}, f32[384,768]{1,0:T(8,128)}, f32[3,96,192]{2,1,0:T(8,128)}, f32[192,96]{1,0:T(8,128)}, f32[96,768]{1,0:T(8,128)...) custom-call(bf16[384,768]{1,0:T(8,128)(2,1)} %get-tuple-element.27.refs_0_, ...), custom_call_target="tpu_custom_call" | custom-call | tf_op jit(solution)/shard_map/hand_over/pallas_call | solution.py:1022
